TPU v7x, 32 devices: a whole 2x2x4 slice. The times are simulated.
32 devices in a mesh: dp: 16 (over z, y, x), tensor: 2 (over core).
Axes of the slice: x: 2, y: 2, z: 4, core: 2. Of those that a mesh axis runs over, the one named last changes fastest.
Arguments:
- latents: bfloat16 [4160, 1536], P(('dp', 'tensor')), may hold values from -6 to 6
- context: bfloat16 [8192, 1536], P('dp'), may hold values from -6 to 6
- cotangent: bfloat16 [4160, 1536], P(('dp', 'tensor')), may hold values from -6 to 6
- positions: int32 [3, 4160], P(None, 'dp'), may hold values from 0 to 63
- step_ids: int32 [16], P('dp'), may hold values from 0 to 15
- owners: int32 [118], replicated, may hold values from 0 to 15, as said below
- time_table: float32 [16, 6, 1536], replicated, may hold values from -3 to 3
- master: float32 [2, 144, 1536, 128], P('tensor', 'dp'), may hold values from -6 to 6
- first_moment: float32 [2, 144, 1536, 128], P('tensor', 'dp'), as said below
- second_moment: float32 [2, 144, 1536, 128], P('tensor', 'dp'), as said below
- head_params: float32 [2, 12160], P('tensor'), as said below
- head_first: float32 [2, 12160], P('tensor'), may hold values from -20 to 20
- head_second: float32 [2, 12160], P('tensor'), may hold values from 0.52 to 8.32
- shared_params: float32 [11, 1536], replicated, as said below
- shared_first: float32 [11, 1536], replicated, may hold values from -20 to 20
- shared_second: float32 [11, 1536], replicated, may hold values from 0.52 to 8.32
Outputs:
- block_out: bfloat16 [4160, 1536], P(('dp', 'tensor'))
- grad_latents: float32 [4160, 1536], P(('dp', 'tensor'))
- new_master: float32 [2, 144, 1536, 128], P('tensor', 'dp')
- new_first: float32 [2, 144, 1536, 128], P('tensor', 'dp')
- new_second: float32 [2, 144, 1536, 128], P('tensor', 'dp')
- new_head: float32 [2, 12160], P('tensor')
- new_head_first: float32 [2, 12160], P('tensor')
- new_head_second: float32 [2, 12160], P('tensor')
- new_shared: float32 [11, 1536], replicated
- new_shared_first: float32 [11, 1536], replicated
- new_shared_second: float32 [11, 1536], replicated
Inputs may be any that keep to these rules, and one draw needn't show every extreme that they name: `owners`: no owner holds more than 9 blocks, and some owner holds exactly 9. `first_moment`: entries are finite, of both signs. `second_moment`: entries are positive. `head_params`: the gains among them are positive. `shared_params`: the norm gain row is positive.
All inputs are finite; a program needn't handle non-finite values.
Results may differ from a plain program's by a relative error of at most 0.014.
Values may be sent and summed in bfloat16 or wider, within the bound.
A program may use at most 512 MiB of HBM per device.

v0:
```python
import jax
import jax.numpy as jnp
from jax import lax
from jax.sharding import PartitionSpec as P

D = 1536
HEADS = 12
HEAD = 128
FF = 8960
TSTEPS = 16
STEPC = 10


NORM_EPS = 1e-06
BETA_ONE = 0.9
BETA_TWO = 0.999
ADAM_EPS = 1e-08
TILE_RATE = 1.0
TILE_DECAY = 0.1
VECTOR_RATE = 0.5
GELU_COEF = 0.7978845608028654


def product(form, left, right):
    return jnp.einsum(form, left, right, preferred_element_type=jnp.float32)


def layer_norm(inputs):
    centre = inputs - jnp.mean(inputs, -1, keepdims=True)
    return centre * lax.rsqrt(jnp.mean(centre * centre, -1, keepdims=True) + NORM_EPS)


def gelu_tanh(inputs):
    return (
        0.5 * inputs * (1.0 + jnp.tanh(GELU_COEF * (inputs + 0.044715 * inputs * inputs * inputs)))
    )


def rotate(inputs):
    paired = inputs.reshape(inputs.shape[:-1] + (inputs.shape[-1] // 2, 2))
    return jnp.stack([-paired[..., 1], paired[..., 0]], -1).reshape(inputs.shape)


def rope(inputs, cos_tab, sin_tab):
    return inputs * cos_tab[..., None, :] + rotate(inputs) * sin_tab[..., None, :]


def rope_tables(token_places, head_size):
    sixths = head_size // 6
    frame_pairs = (head_size - 4 * sixths) // 2
    frame_freq = 10000.0 ** (-jnp.arange(frame_pairs, dtype=jnp.float32) / frame_pairs)
    side_freq = 10000.0 ** (-jnp.arange(sixths, dtype=jnp.float32) / sixths)
    spots = token_places.astype(jnp.float32)
    angles = jnp.concatenate(
        [
            spots[0][..., None] * frame_freq,
            spots[1][..., None] * side_freq,
            spots[2][..., None] * side_freq,
        ],
        -1,
    )
    angles = jnp.repeat(angles, 2, axis=-1)
    return (jnp.cos(angles), jnp.sin(angles))


def owner_layout(owners, slot_count, devices):
    indices = jnp.arange(owners.shape[0], dtype=jnp.int32)
    same_owner = (owners[:, None] == owners[None, :]) & (indices[None, :] < indices[:, None])
    slot_of = jnp.sum(same_owner.astype(jnp.int32), axis=1)
    places = owners * slot_count + slot_of
    spots = jnp.arange(slot_count * devices, dtype=jnp.int32)
    holder = (
        jnp.sum(jnp.where(places[None, :] == spots[:, None], indices[None, :] + 1, 0), axis=1) - 1
    )
    return (places, holder)


def tile_scales(tile_count, heads_here, blocks_here):
    indices = jnp.arange(tile_count)
    scale_in = D ** (-0.5)
    scale_out = HEADS ** (-0.5)
    scale_down = FF ** (-0.5)
    scales = jnp.where(
        indices < 3 * heads_here,
        scale_in,
        jnp.where(
            indices < 4 * heads_here,
            scale_out,
            jnp.where(
                indices < 7 * heads_here,
                scale_in,
                jnp.where(
                    indices < 8 * heads_here,
                    scale_out,
                    jnp.where(indices < 8 * heads_here + blocks_here, scale_in, scale_down),
                ),
            ),
        ),
    )
    return scales.astype(jnp.float32)


def tile_views(weights, heads_here, blocks_here):
    pieces = [weights[number * heads_here : (number + 1) * heads_here] for number in range(8)]
    start_up = 8 * heads_here
    pieces.append(weights[start_up : start_up + blocks_here])
    pieces.append(weights[start_up + blocks_here :])
    return pieces


def adam_step(weight, gradient, moment_one, moment_two, step_rate, decay_rate):
    first_new = BETA_ONE * moment_one + (1.0 - BETA_ONE) * gradient
    second_new = BETA_TWO * moment_two + (1.0 - BETA_TWO) * gradient * gradient
    first_hat = first_new / (1.0 - BETA_ONE**STEPC)
    second_hat = second_new / (1.0 - BETA_TWO**STEPC)
    weight_new = weight - step_rate * (
        first_hat / (jnp.sqrt(second_hat) + ADAM_EPS) + decay_rate * weight
    )
    return (weight_new, first_new, second_new)


def attend(query_low, key_low, value_low, scaling):
    scores = product("qhe,khe->hqk", query_low, key_low) * scaling
    row_max = jnp.max(scores, -1, keepdims=True)
    log_total = row_max + jnp.log(jnp.sum(jnp.exp(scores - row_max), -1, keepdims=True))
    softmax_low = jnp.exp(scores - log_total).astype(jnp.bfloat16)
    heads_out = product("hqk,khe->qhe", softmax_low, value_low).astype(jnp.bfloat16)
    return (log_total, heads_out)


def attend_back(query_low, key_low, value_low, log_total, d_heads, scaling):
    scores = product("qhe,khe->hqk", query_low, key_low) * scaling
    softmax_rows = jnp.exp(scores - log_total)
    d_softmax = product("qhe,khe->hqk", d_heads, value_low)
    d_scores = (
        softmax_rows * (d_softmax - jnp.sum(softmax_rows * d_softmax, -1, keepdims=True))
    ).astype(jnp.bfloat16)
    d_query = product("hqk,khe->qhe", d_scores, key_low) * scaling
    d_key = product("hqk,qhe->khe", d_scores, query_low) * scaling
    d_value = product("hqk,qhe->khe", softmax_rows.astype(jnp.bfloat16), d_heads)
    return (d_query, d_key, d_value)


def norm_stats(query_pre, key_pre):
    totals = lax.psum(
        (jnp.sum(query_pre * query_pre, (1, 2)), jnp.sum(key_pre * key_pre, (1, 2))), "tensor"
    )
    return tuple((lax.rsqrt(total / D + NORM_EPS)[:, None, None] for total in totals))


def norm_back(query_pre, query_inv, query_gain, query_in, key_pre, key_inv, key_gain, key_in):
    totals = lax.psum(
        (
            jnp.sum(query_pre * query_gain * query_in, (1, 2)),
            jnp.sum(key_pre * key_gain * key_in, (1, 2)),
        ),
        "tensor",
    )
    results = []
    for pre_vals, inverse, gain_vec, incoming, total in (
        (query_pre, query_inv, query_gain, query_in, totals[0]),
        (key_pre, key_inv, key_gain, key_in, totals[1]),
    ):
        d_pre = inverse * (gain_vec * incoming) - pre_vals * inverse * inverse * inverse * (
            total[:, None, None] / D
        )
        d_gain = jnp.sum(incoming * pre_vals * inverse, 0)
        results.append(d_pre)
        results.append(d_gain)
    return results


def body(
    latents,
    context,
    cotangent,
    positions,
    step_ids,
    owners,
    time_table,
    master,
    first_moment,
    second_moment,
    head_params,
    head_first,
    head_second,
    shared_params,
    shared_first,
    shared_second,
):
    tensors = lax.axis_size("tensor")
    devices = lax.axis_size("dp")
    slot_count = master.shape[1]
    tile_count = owners.shape[0]
    heads_here = HEADS // tensors
    blocks_here = FF // (HEAD * tensors)
    width_here = D // tensors
    scaling = HEAD ** (-0.5)
    places, holder = owner_layout(owners, slot_count, devices)
    scales = tile_scales(tile_count, heads_here, blocks_here)
    my_slots = lax.dynamic_slice_in_dim(holder, lax.axis_index("dp") * slot_count, slot_count)
    filled = my_slots >= 0
    slot_scale = jnp.where(filled, scales[jnp.maximum(my_slots, 0)], 0.0)
    scaled = (master[0] * slot_scale[:, None, None]).astype(jnp.bfloat16)
    everyone = lax.all_gather(scaled, "dp", axis=0, tiled=True)
    pieces = tile_views(jnp.take(everyone, places, axis=0), heads_here, blocks_here)
    vectors = head_params[0]

    def head_vector(number):
        return vectors[number * width_here : (number + 1) * width_here].reshape(heads_here, HEAD)

    bias_query, bias_key, bias_value, gain_query, gain_key = [
        head_vector(number) for number in range(5)
    ]
    cross_bias_q, cross_bias_k, cross_bias_v, cross_gain_q, cross_gain_k = [
        head_vector(number) for number in range(5, 10)
    ]
    up_bias = vectors[10 * width_here :].reshape(blocks_here, HEAD)
    chosen = (step_ids[0] == jnp.arange(TSTEPS)).astype(jnp.float32)
    modulation = shared_params[5:11] + jnp.einsum(
        "s,skd->kd", chosen, time_table, precision=lax.Precision.HIGHEST
    )
    shift_attn, scale_attn, gate_attn = (modulation[0], modulation[1], modulation[2])
    shift_ffn, scale_ffn, gate_ffn = (modulation[3], modulation[4], modulation[5])
    cos_tab, sin_tab = rope_tables(positions, HEAD)

    def mod_norm(inputs, shift_vec, scale_vec):
        return layer_norm(inputs) * (1.0 + scale_vec) + shift_vec

    def affine_norm(inputs, gain_vec, bias_vec):
        return layer_norm(inputs) * gain_vec + bias_vec

    def spread_rows(local_rows):
        return lax.all_gather(local_rows, "tensor", axis=0, tiled=True)

    def merge_rows(summand):
        return lax.psum_scatter(summand, "tensor", scatter_dimension=0, tiled=True)

    def spread_grads(local_rows):
        return lax.all_gather(local_rows, "tensor", axis=0, tiled=True)

    def merge_grads(summand):
        return lax.psum_scatter(summand, "tensor", scatter_dimension=0, tiled=True)

    residual = latents.astype(jnp.float32)
    low_one = mod_norm(residual, shift_attn, scale_attn).astype(jnp.bfloat16)
    rows_one = spread_rows(low_one)
    query_pre = product("td,hde->the", rows_one, pieces[0]) + bias_query
    key_pre = product("td,hde->the", rows_one, pieces[1]) + bias_key
    value_low = (product("td,hde->the", rows_one, pieces[2]) + bias_value).astype(jnp.bfloat16)
    query_inv, key_inv = norm_stats(query_pre, key_pre)
    query_low = rope(query_pre * query_inv * gain_query, cos_tab, sin_tab).astype(jnp.bfloat16)
    key_low = rope(key_pre * key_inv * gain_key, cos_tab, sin_tab).astype(jnp.bfloat16)
    log_total, heads_out = attend(query_low, key_low, value_low, scaling)
    saved_one = (
        query_pre,
        key_pre,
        query_inv,
        key_inv,
        query_low,
        key_low,
        value_low,
        log_total,
        heads_out,
    )
    branch_one = merge_rows(product("the,hde->td", saved_one[-1], pieces[3])) + shared_params[0]
    after_one = residual + gate_attn * branch_one
    low_two = affine_norm(after_one, shared_params[3], shared_params[4]).astype(jnp.bfloat16)
    rows_two = spread_rows(low_two)
    query_pre = product("td,hde->the", rows_two, pieces[4]) + cross_bias_q
    key_pre = product("cd,hde->che", context, pieces[5]) + cross_bias_k
    value_low = (product("cd,hde->che", context, pieces[6]) + cross_bias_v).astype(jnp.bfloat16)
    query_inv, key_inv = norm_stats(query_pre, key_pre)
    query_low = (query_pre * query_inv * cross_gain_q).astype(jnp.bfloat16)
    key_low = (key_pre * key_inv * cross_gain_k).astype(jnp.bfloat16)
    log_total, heads_out = attend(query_low, key_low, value_low, scaling)
    saved_two = (
        query_pre,
        key_pre,
        query_inv,
        key_inv,
        query_low,
        key_low,
        value_low,
        log_total,
        heads_out,
    )
    branch_two = merge_rows(product("the,hde->td", saved_two[-1], pieces[7])) + shared_params[1]
    after_two = after_one + branch_two
    low_three = mod_norm(after_two, shift_ffn, scale_ffn).astype(jnp.bfloat16)
    rows_three = spread_rows(low_three)
    hidden_pre = product("td,fde->tfe", rows_three, pieces[8]) + up_bias
    saved_three = (hidden_pre, gelu_tanh(hidden_pre).astype(jnp.bfloat16))
    branch_three = merge_rows(product("tfe,fde->td", saved_three[1], pieces[9])) + shared_params[2]
    result = after_two + gate_ffn * branch_three
    output = result.astype(jnp.bfloat16)
    grad_res = cotangent.astype(jnp.float32)
    d_gate_ffn = jnp.sum(grad_res * branch_three, 0)
    grad_branch = (gate_ffn * grad_res).astype(jnp.bfloat16)
    d_down_bias = jnp.sum(grad_branch.astype(jnp.float32), 0)
    rows_grad = spread_grads(grad_branch)
    hidden_pre, hidden_low = saved_three
    d_down = product("tfe,td->fde", hidden_low, rows_grad)
    d_hidden = product("td,fde->tfe", rows_grad, pieces[9])
    d_hidden = jax.vjp(gelu_tanh, hidden_pre)[1](d_hidden)[0]
    d_hidden_low = d_hidden.astype(jnp.bfloat16)
    d_up_bias = jnp.sum(d_hidden_low.astype(jnp.float32), 0)
    d_up = product("td,tfe->fde", rows_three, d_hidden_low)
    grad_norm = merge_grads(product("tfe,fde->td", d_hidden_low, pieces[8]))
    d_inputs, d_shift_ffn, d_scale_ffn = jax.vjp(mod_norm, after_two, shift_ffn, scale_ffn)[1](
        grad_norm
    )
    grad_res = grad_res + d_inputs
    grad_branch = grad_res.astype(jnp.bfloat16)
    d_cross_bias_out = jnp.sum(grad_branch.astype(jnp.float32), 0)
    rows_grad = spread_grads(grad_branch)
    query_pre, key_pre, query_inv, key_inv, query_low, key_low, value_low, log_total, heads_out = (
        saved_two
    )
    d_cross_out = product("the,td->hde", heads_out, rows_grad)
    d_heads = product("td,hde->the", rows_grad, pieces[7]).astype(jnp.bfloat16)
    d_query, d_key, d_value = attend_back(
        query_low, key_low, value_low, log_total, d_heads, scaling
    )
    d_query, d_cross_gain_q, d_key, d_cross_gain_k = norm_back(
        query_pre, query_inv, cross_gain_q, d_query, key_pre, key_inv, cross_gain_k, d_key
    )
    query_grad = d_query.astype(jnp.bfloat16)
    key_grad = d_key.astype(jnp.bfloat16)
    value_grad = d_value.astype(jnp.bfloat16)
    d_cross_bias_q = jnp.sum(query_grad.astype(jnp.float32), 0)
    d_cross_bias_k = jnp.sum(key_grad.astype(jnp.float32), 0)
    d_cross_bias_v = jnp.sum(value_grad.astype(jnp.float32), 0)
    d_cross_query = product("td,the->hde", rows_two, query_grad)
    d_cross_key = product("cd,che->hde", context, key_grad)
    d_cross_value = product("cd,che->hde", context, value_grad)
    grad_norm = merge_grads(product("the,hde->td", query_grad, pieces[4]))
    d_inputs, d_norm_gain, d_norm_bias = jax.vjp(
        affine_norm, after_one, shared_params[3], shared_params[4]
    )[1](grad_norm)
    grad_res = grad_res + d_inputs
    d_gate_attn = jnp.sum(grad_res * branch_one, 0)
    grad_branch = (gate_attn * grad_res).astype(jnp.bfloat16)
    d_self_bias_out = jnp.sum(grad_branch.astype(jnp.float32), 0)
    rows_grad = spread_grads(grad_branch)
    query_pre, key_pre, query_inv, key_inv, query_low, key_low, value_low, log_total, heads_out = (
        saved_one
    )
    d_self_out = product("the,td->hde", heads_out, rows_grad)
    d_heads = product("td,hde->the", rows_grad, pieces[3]).astype(jnp.bfloat16)
    d_query, d_key, d_value = attend_back(
        query_low, key_low, value_low, log_total, d_heads, scaling
    )
    turned_query = rope(d_query, cos_tab, -sin_tab)
    turned_key = rope(d_key, cos_tab, -sin_tab)
    d_query, d_gain_query, d_key, d_gain_key = norm_back(
        query_pre, query_inv, gain_query, turned_query, key_pre, key_inv, gain_key, turned_key
    )
    query_grad = d_query.astype(jnp.bfloat16)
    key_grad = d_key.astype(jnp.bfloat16)
    value_grad = d_value.astype(jnp.bfloat16)
    d_bias_query = jnp.sum(query_grad.astype(jnp.float32), 0)
    d_bias_key = jnp.sum(key_grad.astype(jnp.float32), 0)
    d_bias_value = jnp.sum(value_grad.astype(jnp.float32), 0)
    d_self_query = product("td,the->hde", rows_one, query_grad)
    d_self_key = product("td,the->hde", rows_one, key_grad)
    d_self_value = product("td,the->hde", rows_one, value_grad)
    input_sum = (
        product("the,hde->td", query_grad, pieces[0])
        + product("the,hde->td", key_grad, pieces[1])
        + product("the,hde->td", value_grad, pieces[2])
    )
    grad_norm = merge_grads(input_sum)
    d_inputs, d_shift_attn, d_scale_attn = jax.vjp(mod_norm, residual, shift_attn, scale_attn)[1](
        grad_norm
    )
    grad_input = grad_res + d_inputs
    all_grads = jnp.concatenate(
        [
            d_self_query,
            d_self_key,
            d_self_value,
            d_self_out,
            d_cross_query,
            d_cross_key,
            d_cross_value,
            d_cross_out,
            d_up,
            d_down,
        ],
        0,
    )
    picked = jnp.take(all_grads, jnp.maximum(holder, 0), axis=0)
    reduced = lax.psum_scatter(
        jnp.where((holder >= 0)[:, None, None], picked, 0.0), "dp", scatter_dimension=0, tiled=True
    )
    grad_master = reduced * slot_scale[:, None, None]
    new_w, new_m, new_v = adam_step(
        master[0], grad_master, first_moment[0], second_moment[0], TILE_RATE, TILE_DECAY
    )
    slot_mask = filled[:, None, None]
    new_master = jnp.where(slot_mask, new_w, master[0])[None]
    new_first = jnp.where(slot_mask, new_m, first_moment[0])[None]
    new_second = jnp.where(slot_mask, new_v, second_moment[0])[None]
    head_grad = jnp.concatenate(
        [
            d_bias_query.reshape(-1),
            d_bias_key.reshape(-1),
            d_bias_value.reshape(-1),
            d_gain_query.reshape(-1),
            d_gain_key.reshape(-1),
            d_cross_bias_q.reshape(-1),
            d_cross_bias_k.reshape(-1),
            d_cross_bias_v.reshape(-1),
            d_cross_gain_q.reshape(-1),
            d_cross_gain_k.reshape(-1),
            d_up_bias.reshape(-1),
        ]
    )
    tensor_rank = lax.axis_index("tensor")
    head_padded = jnp.where(jnp.arange(tensors)[:, None] == tensor_rank, head_grad[None, :], 0.0)
    shared_grad = jnp.stack(
        [
            d_self_bias_out,
            d_cross_bias_out,
            d_down_bias,
            d_norm_gain,
            d_norm_bias,
            d_shift_attn,
            d_scale_attn,
            d_gate_attn,
            d_shift_ffn,
            d_scale_ffn,
            d_gate_ffn,
        ]
    )
    head_total, shared_total = lax.psum((head_padded, shared_grad), ("dp", "tensor"))
    mine_head = lax.dynamic_slice_in_dim(head_total, tensor_rank, 1, 0)
    new_head, new_head_first, new_head_second = adam_step(
        head_params, mine_head, head_first, head_second, VECTOR_RATE, 0.0
    )
    new_shared, new_shared_first, new_shared_second = adam_step(
        shared_params, shared_total, shared_first, shared_second, VECTOR_RATE, 0.0
    )
    return (
        output,
        grad_input,
        new_master,
        new_first,
        new_second,
        new_head,
        new_head_first,
        new_head_second,
        new_shared,
        new_shared_first,
        new_shared_second,
    )


def solution(mesh):
    return jax.shard_map(
        body,
        mesh=mesh,
        in_specs=(
            P(("dp", "tensor"), None),
            P("dp", None),
            P(("dp", "tensor"), None),
            P(None, "dp"),
            P("dp"),
            P(),
            P(),
            P("tensor", "dp", None, None),
            P("tensor", "dp", None, None),
            P("tensor", "dp", None, None),
            P("tensor", None),
            P("tensor", None),
            P("tensor", None),
            P(),
            P(),
            P(),
        ),
        out_specs=(
            P(("dp", "tensor"), None),
            P(("dp", "tensor"), None),
            P("tensor", "dp", None, None),
            P("tensor", "dp", None, None),
            P("tensor", "dp", None, None),
            P("tensor", None),
            P("tensor", None),
            P("tensor", None),
            P(),
            P(),
            P(),
        ),
        check_vma=False,
    )
```

profile of v0, /device:TPU:9, one launch (start us, length us, event | category | flops | bytes accessed | tf_op | source)
XLA Modules:
  0.0 2805.7 jit_solution(16756793677554385056)
XLA Ops:
  12.6 8.0 copy.104
  20.6 5.8 fusion.19
  26.4 5.7 copy.105
  60.1 539.9 %all-gather.8.cloned.1.call-done = bf16[144,1536,128]{2,1,0:T(8,128)(2,1)} async-done(((bf16[9,1536,128]{2,1,0:T(8,128)(2,1)}), bf16[144,1536,128]{2,1,0:T(8,128)(2,1)}) %all-gather.8.cloned.1.call-update) | async-done | bytes 56623120 | tf_op jit(solution)/shard_map/all_gather | solution.py:205
  600.0 31.9 %gather_fusion.1 = bf16[118,1536,128]{2,1,0:T(8,128)(2,1)} fusion(bf16[144,1536,128]{2,1,0:T(8,128)(2,1)} %all-gather.8.cloned.1.call-done, s32[1024]{0:T(1024)S(1)} %pad_clamp_fusion.1), kind=kCustom, calls=%fused_computation.1 | custom fusion | bytes 92799448 | tf_op jit(solution)/shard_map/jit(_take)/gather | solution.py:206
  631.9 31.5 %broadcast_select_fusion = bf16[118,1536,128]{2,1,0:T(8,128)(2,1)} fusion(bf16[118,1536,128]{2,1,0:T(8,128)(2,1)} %gather_fusion.1, pred[118]{0:T(512)(128)(4,1)S(1)} %copy-done.135), kind=kLoop, calls=%fused_computation.4 | loop fusion | flops 23199744 | bytes 92799096 | tf_op jit(solution)/shard_map/jit(_take)/select_n | solution.py:206
  663.4 3.4 multiply_reduce_fusion.17
  666.8 3.4 multiply_reduce_fusion.16
  670.2 3.5 all-reduce.15
  681.2 3.0 slice_negate_fusion.3
  686.4 3.0 reshape.323
  699.4 3.0 slice_negate_fusion.2
  704.6 3.5 reshape.325
  718.5 3.7 convolution_bitcast_fusion.7
  722.2 5.5 fusion
  729.0 5.0 fusion.58
  734.0 4.0 fusion.83
  738.0 3.6 concatenate.12
  743.6 3.2 all-gather.1
  758.3 3.7 convolution_bitcast_fusion.6
  761.9 5.7 fusion.1
  775.1 4.3 concatenate.13
  781.8 3.9 all-gather.2
  787.9 7.5 fusion.12
  795.4 12.7 convert_reduce_fusion
  809.5 10.1 fusion.27
  819.6 6.3 fusion.3
  828.2 12.0 fusion.30
  840.1 4.8 concatenate.15
  851.2 3.7 all-gather.4
  867.0 3.6 convolution_bitcast_fusion
  875.9 3.7 convolution_bitcast_fusion.5
  879.5 5.5 fusion.4
  887.4 4.5 convert_reduce_fusion.1
  893.7 6.1 copy.129
  899.8 4.9 concatenate.16
  912.1 3.7 all-gather.5
  925.1 3.6 convolution_bitcast_fusion.1
  946.3 3.0 reshape.327
  951.9 3.5 multiply_reduce_fusion.12
  965.3 3.6 bitcast_dynamic-update-slice_fusion.7
  968.9 3.7 fusion.34
  972.6 7.8 fusion.152
  984.0 4.6 bitcast_dynamic-update-slice_fusion.6
  988.6 3.6 bitcast_dynamic-update-slice_fusion.5
  992.2 6.3 copy.128
  998.5 5.2 constant_dynamic-update-slice_fusion.1
  1003.8 3.6 bitcast_dynamic-update-slice_fusion.4
  1008.0 3.6 bitcast_dynamic-update-slice_fusion.3
  1011.6 3.6 bitcast_dynamic-update-slice_fusion.2
  1015.2 3.0 constant_dynamic-update-slice_fusion
  1018.2 13.1 bitcast_dynamic-update-slice_fusion.1
  1032.3 14.2 bitcast_dynamic-update-slice_fusion
  1046.6 75.1 %gather_fusion.2 = f32[144,1536,128]{1,2,0:T(8,128)} fusion(f32[118,1536,128]{1,2,0:T(8,128)} %bitcast_dynamic-update-slice_fusion, s32[1024]{0:T(1024)} %pad_clamp_fusion), kind=kCustom, calls=%fused_computation.2 | custom fusion | bytes 226492992 | tf_op jit(solution)/shard_map/jit(_take)/gather | solution.py:393
  1125.0 4.0 concatenate.14
  1132.8 74.0 %select_select_fusion = f32[144,1536,128]{1,2,0:T(8,128)} fusion(f32[144,1536,128]{1,2,0:T(8,128)} %gather_fusion.2, pred[144]{0:T(512)(128)(4,1)S(1)} %copy-done.140, pred[144]{0:T(512)(128)(4,1)S(1)} %copy-done.139), kind=kLoop, calls=%fused_computation.3 | loop fusion | flops 56623104 | bytes 226492704 | tf_op jit(solution)/shard_map/jit(_where)/select_n | solution.py:395
  1206.8 8.0 copy.126
  1214.8 8.1 copy.130
  1224.2 32.7 %all-reduce.19.cloned.1.call-done = (f32[2,12160]{1,0:T(2,128)}, f32[11,1536]{1,0:T(8,128)}) async-done(((f32[2,12160]{1,0:T(2,128)}, f32[11,1536]{1,0:T(8,128)}), (f32[2,12160]{1,0:T(2,128)}, f32[11,1536]{1,0:T(8,128)})) %all-reduce.19.cloned.1.call-update) | async-done | bytes 164880 | tf_op jit(solution)/shard_map/psum | solution.py:437
  1260.4 1498.4 %reduce-scatter.14.cloned.1.call-done = f32[9,1536,128]{1,2,0:T(8,128)} async-done(((f32[144,1536,128]{1,2,0:T(8,128)}), f32[9,1536,128]{1,2,0:T(8,128)}) %reduce-scatter.14.cloned.1.call-update) | async-done | bytes 7077904 | tf_op jit(solution)/shard_map/reduce_scatter | solution.py:394
  2758.9 16.1 fusion.16
  2775.0 8.0 copy.131
  2782.9 8.0 copy.132
  2790.9 8.1 copy.133
  (487 shorter events, 185.1 us)
Async XLA Ops:
  7.2 721.9 %copy-start = (bf16[512,1536]{1,0:T(8,128)(2,1)S(1)}, bf16[512,1536]{1,0:T(8,128)(2,1)}, u32[]{:S(2)}) copy-start(bf16[512,1536]{1,0:T(8,128)(2,1)} %param.17) | copy-start | bytes 4718596
  7.2 592.8 %all-gather.8.cloned.1.call-start = ((), (), s32[]{:S(2)}) async-start(), calls=%async_computation.1 | async-start | bytes 60162048 | tf_op jit(solution)/shard_map/all_gather | solution.py:205
  32.1 1224.8 %all-reduce.19.cloned.1.call-start = ((), (), s32[]{:S(2)}) async-start(), calls=%async_computation.3 | async-start | bytes 391168 | tf_op jit(solution)/shard_map/psum | solution.py:437
  34.2 19.2 copy-start.87
  34.3 10.6 copy-start.96
  34.6 15.6 copy-start.124
  34.6 18.8 copy-start.116
  34.6 18.8 copy-start.23
  39.1 674.9 %copy-start.12 = (bf16[260,1536,1]{1,0,2:T(8,128)(2,1)}, bf16[260,1536,1]{1,0,2:T(8,128)(2,1)S(1)}, u32[]{:S(2)}) copy-start(bf16[260,1536,1]{1,0,2:T(8,128)(2,1)S(1)} %reshape.388) | copy-start | bytes 2396164
  51.7 658.9 %copy-start.70 = (f32[768]{0:T(1024)}, f32[768]{0:T(1024)S(1)}, u32[]{:S(2)}) copy-start(f32[768]{0:T(1024)S(1)} %get-tuple-element.94) | copy-start | bytes 9220
  51.7 658.9 %copy-start.72 = (f32[768]{0:T(1024)}, f32[768]{0:T(1024)S(1)}, u32[]{:S(2)}) copy-start(f32[768]{0:T(1024)S(1)} %get-tuple-element.92) | copy-start | bytes 9220
  51.7 701.5 %copy-start.74 = (f32[768]{0:T(1024)}, f32[768]{0:T(1024)S(1)}, u32[]{:S(2)}) copy-start(f32[768]{0:T(1024)S(1)} %get-tuple-element.87) | copy-start | bytes 9220
  51.7 701.5 %copy-start.76 = (f32[768]{0:T(1024)}, f32[768]{0:T(1024)S(1)}, u32[]{:S(2)}) copy-start(f32[768]{0:T(1024)S(1)} %get-tuple-element.88) | copy-start | bytes 9220
  53.4 688.2 %copy-start.85 = (f32[1536]{0:T(1024)}, f32[1536]{0:T(1024)S(1)}, u32[]{:S(2)}) copy-start(f32[1536]{0:T(1024)S(1)} %get-tuple-element.80) | copy-start | bytes 18436
  60.1 571.8 %copy-start.135 = (pred[118]{0:T(512)(128)(4,1)S(1)}, pred[118]{0:T(512)(128)(4,1)}, u32[]{:S(2)}) copy-start(pred[118]{0:T(512)(128)(4,1)} %get-tuple-element.140) | copy-start | bytes 358
  673.7 37.0 %copy-start.89 = (f32[260]{0:T(512)}, f32[260]{0:T(512)S(1)}, u32[]{:S(2)}) copy-start(f32[260]{0:T(512)S(1)} %get-tuple-element.198) | copy-start | bytes 3124
  673.7 37.0 %copy-start.91 = (f32[260]{0:T(512)}, f32[260]{0:T(512)S(1)}, u32[]{:S(2)}) copy-start(f32[260]{0:T(512)S(1)} %get-tuple-element.197) | copy-start | bytes 3124
  702.4 8.2 copy-start.60
  702.5 8.2 copy-start.61
  727.7 10.3 collective-permute-start
  768.3 6.9 collective-permute-start.1
  780.9 66.9 %copy-start.6 = (f32[130,1536]{1,0:T(8,128)}, f32[130,1536]{1,0:T(8,128)S(1)}, u32[]{:S(2)}) copy-start(f32[130,1536]{1,0:T(8,128)S(1)} %get-tuple-element.137) | copy-start | bytes 2396164
  795.3 12.8 copy-start.30
  826.7 13.5 collective-permute-start.3
  885.1 8.7 copy-start.36
  885.7 14.1 collective-permute-start.4
  893.7 11.0 copy-start.108
  899.8 9.4 copy-start.21
  899.8 9.4 copy-start.86
  980.4 11.8 copy-start.35
  980.4 8.1 copy-start.53
  981.4 140.4 %collective-permute-start.5 = (f32[6,1536]{1,0:T(8,128)S(1)}, f32[6,1536]{1,0:T(8,128)S(1)}, u32[]{:S(2)}, u32[]{:S(2)}) collective-permute-start(f32[6,1536]{1,0:T(8,128)S(1)} %slice.224), channel_id=1, source_target_pairs={{0,1},{2,3},{4,5},{6,7},{8,9},{10,11},{12,13},{14,15},{16,17},{18,... | collective-permute-start | bytes 110600
  982.7 142.4 %collective-permute-start.2 = (f32[6,1536]{1,0:T(8,128)S(1)}, f32[6,1536]{1,0:T(8,128)S(1)}, u32[]{:S(2)}, u32[]{:S(2)}) collective-permute-start(f32[6,1536]{1,0:T(8,128)S(1)} %slice.221), channel_id=1, source_target_pairs={{0,1},{2,3},{4,5},{6,7},{8,9},{10,11},{12,13},{14,15},{16,17},{18,... | collective-permute-start | bytes 110600
  1015.2 17.1 slice-start.2
  1018.2 13.2 copy-start.93
  1018.2 13.2 copy-start.120
  1018.2 13.3 copy-start.121
  1018.2 13.3 copy-start.123
  1018.2 13.3 copy-start.118
  1018.2 13.3 copy-start.113
  1018.2 13.3 copy-start.141
  1018.2 14.1 slice-start.3
  1018.2 14.1 copy-start.41
  1018.2 14.1 copy-start.68
  1032.3 14.2 copy-start.102
  1032.3 14.2 copy-start.101
  1032.3 14.2 copy-start.100
  1046.6 77.5 %copy-start.11 = (bf16[130,1536]{1,0:T(8,128)(2,1)S(1)}, bf16[130,1536]{1,0:T(8,128)(2,1)}, u32[]{:S(2)}) copy-start(bf16[130,1536]{1,0:T(8,128)(2,1)} %param.16) | copy-start | bytes 1198084
  1046.6 77.5 %copy-start.65 = (f32[1536]{0:T(1024)S(1)}, f32[1536]{0:T(1024)}, u32[]{:S(2)}) copy-start(f32[1536]{0:T(1024)} %copy-done.64) | copy-start | bytes 18436
  1046.6 77.5 %copy-start.97 = (f32[130]{0:T(256)S(1)}, f32[130]{0:T(256)}, u32[]{:S(2)}) copy-start(f32[130]{0:T(256)} %copy-done.96) | copy-start | bytes 1564
  1046.6 77.8 %copy-start.125 = (f32[130]{0:T(256)S(1)}, f32[130]{0:T(256)}, u32[]{:S(2)}) copy-start(f32[130]{0:T(256)} %copy-done.124) | copy-start | bytes 1564
  1046.6 77.8 %copy-start.117 = (f32[130]{0:T(256)S(1)}, f32[130]{0:T(256)}, u32[]{:S(2)}) copy-start(f32[130]{0:T(256)} %copy-done.116) | copy-start | bytes 1564
  1124.4 8.3 copy-start.139
  1124.4 8.3 copy-start.140
  1132.7 1626.2 %reduce-scatter.14.cloned.1.call-start = ((), (), s32[]{:S(2)}) async-start(), calls=%async_computation.2 | async-start | bytes 120324096 | tf_op jit(solution)/shard_map/reduce_scatter | solution.py:394
  1214.8 8.1 copy-start.19
  1214.8 42.1 %copy-start.63 = (f32[11,1536]{1,0:T(8,128)S(1)}, f32[11,1536]{1,0:T(8,128)}, u32[]{:S(2)}) copy-start(f32[11,1536]{1,0:T(8,128)} %param.29) | copy-start | bytes 202756
  1214.8 42.1 %copy-start.78 = (f32[11,1536]{1,0:T(8,128)S(1)}, f32[11,1536]{1,0:T(8,128)}, u32[]{:S(2)}) copy-start(f32[11,1536]{1,0:T(8,128)} %param.30) | copy-start | bytes 202756
  1214.8 42.1 %copy-start.79 = (f32[11,1536]{1,0:T(8,128)S(1)}, f32[11,1536]{1,0:T(8,128)}, u32[]{:S(2)}) copy-start(f32[11,1536]{1,0:T(8,128)} %param.31) | copy-start | bytes 202756
  1222.9 35.7 %copy-start.66 = (f32[1,12160]{1,0:T(1,128)S(1)}, f32[1,12160]{1,0:T(1,128)}, u32[]{:S(2)}) copy-start(f32[1,12160]{1,0:T(1,128)} %param.26) | copy-start | bytes 145924
  1222.9 35.7 %copy-start.94 = (f32[1,12160]{1,0:T(1,128)S(1)}, f32[1,12160]{1,0:T(1,128)}, u32[]{:S(2)}) copy-start(f32[1,12160]{1,0:T(1,128)} %param.27) | copy-start | bytes 145924
  1222.9 35.7 %copy-start.95 = (f32[1,12160]{1,0:T(1,128)S(1)}, f32[1,12160]{1,0:T(1,128)}, u32[]{:S(2)}) copy-start(f32[1,12160]{1,0:T(1,128)} %param.28) | copy-start | bytes 145924
  1222.9 1536.0 %copy-start.133 = (f32[9]{0:T(128)S(1)}, f32[9]{0:T(128)}, u32[]{:S(2)}) copy-start(f32[9]{0:T(128)} %copy-done.132) | copy-start | bytes 112
  1222.9 1536.0 %copy-start.138 = (pred[9]{0:T(512)(128)(4,1)S(1)}, pred[9]{0:T(512)(128)(4,1)}, u32[]{:S(2)}) copy-start(pred[9]{0:T(512)(128)(4,1)} %get-tuple-element.143) | copy-start | bytes 31
  (91 other events, 362.2 us)
Sparse Core Ops, SparseCore 0:
  32.2 567.7 all-gather.7
  1132.8 124.0 all-reduce.18
  1262.9 1495.9 reduce-scatter.13
where the time goes:
time: 2820 us; the launch traced here: 2810 us
  waiting for transfers between devices  2070 us (73%)
  local copies, waits for them, and re-layouts  282 us (10%)
  other arithmetic  198 us (7%)
  matrix products  167 us (6%)
  blocking collectives  61.8 us (2%)
    reduce_scatter x1, waiting for transfers between devices, body(): lax.psum_scatter(jnp.where((holder >= 0)[:, None, None], picked, 0.0), 'd...  1500 us
    all_gather x1, waiting for transfers between devices, body(): everyone = lax.all_gather(scaled, 'dp', axis=0, tiled=True)  540 us
    dot_general x40, matrix products, product(): return jnp.einsum(form, left, right, preferred_element_type=jnp.float32)  167 us
    unnamed x329, local copies, waits for them, and re-layouts  101 us
    gather x1, local copies, waits for them, and re-layouts, body(): picked = jnp.take(all_grads, jnp.maximum(holder, 0), axis=0)  75.1 us
    select_n x1, other arithmetic, body(): jnp.where((holder >= 0)[:, None, None], picked, 0.0)  74 us
  transfers between devices with their start and end apart: 9, of which 3 were waited for; matrix products, arithmetic and copies ran while one was open for 11% of the time, Pallas kernels for 0%

commit v1 on v0

--- a/solution.py
+++ b/solution.py
@@ -1,6 +1,10 @@
+import functools
+
 import jax
 import jax.numpy as jnp
 from jax import lax
+from jax.experimental import pallas as pl
+from jax.experimental.pallas import tpu as pltpu
 from jax.sharding import PartitionSpec as P
 
 D = 1536
@@ -142,19 +146,16 @@
 
 
 def norm_stats(query_pre, key_pre):
-    totals = lax.psum(
-        (jnp.sum(query_pre * query_pre, (1, 2)), jnp.sum(key_pre * key_pre, (1, 2))), "tensor"
+    totals = pair_sums(
+        jnp.sum(query_pre * query_pre, (1, 2)), jnp.sum(key_pre * key_pre, (1, 2))
     )
     return tuple((lax.rsqrt(total / D + NORM_EPS)[:, None, None] for total in totals))
 
 
 def norm_back(query_pre, query_inv, query_gain, query_in, key_pre, key_inv, key_gain, key_in):
-    totals = lax.psum(
-        (
-            jnp.sum(query_pre * query_gain * query_in, (1, 2)),
-            jnp.sum(key_pre * key_gain * key_in, (1, 2)),
-        ),
-        "tensor",
+    totals = pair_sums(
+        jnp.sum(query_pre * query_gain * query_in, (1, 2)),
+        jnp.sum(key_pre * key_gain * key_in, (1, 2)),
     )
     results = []
     for pre_vals, inverse, gain_vec, incoming, total in (
@@ -168,6 +169,518 @@
         results.append(d_pre)
         results.append(d_gain)
     return results
+
+
+MESH = pl.DeviceIdType.MESH
+ANY = pl.BlockSpec(memory_space=pl.ANY)
+MIB = 1 << 20
+
+
+def chip_pairs():
+    return lax.axis_size("dp") == 16 and lax.axis_size("tensor") == 2
+
+
+def pair_rank():
+    if chip_pairs():
+        return (lax.axis_index("dp") // 4) % 2
+    return lax.axis_index("tensor")
+
+
+def pair_swap(value):
+    if chip_pairs():
+        return lax.ppermute(value, "dp", [(i, i ^ 4) for i in range(16)])
+    return lax.ppermute(value, "tensor", [(0, 1), (1, 0)])
+
+
+def pair_sums(*values):
+    stacked = jnp.concatenate([v.reshape(-1) for v in values])
+    total = stacked + pair_swap(stacked)
+    out, at = [], 0
+    for v in values:
+        out.append(total[at : at + v.size].reshape(v.shape))
+        at += v.size
+    return tuple(out)
+
+
+def home_swap(*values):
+    if not chip_pairs():
+        return values
+    chip, core = lax.axis_index("dp"), lax.axis_index("tensor")
+    away = (chip // 4) % 2 != core
+    order = [
+        (d * 2 + c, (d ^ 4) * 2 + 1 - c) for d in range(16) for c in range(2) if (d // 4) % 2 != c
+    ]
+    return tuple(
+        jnp.where(away, lax.ppermute(v, ("dp", "tensor"), order), v) for v in values
+    )
+
+
+def place_of():
+    chip, core = lax.axis_index("dp"), lax.axis_index("tensor")
+    z, y, x = chip // 4, (chip // 2) % 2, chip % 2
+    return chip, core, z, y, x
+
+
+def column_of(z, y, x, k):
+    high, low_bit = z // 2, z % 2
+    if k & 2:
+        high = 1 - high
+    if k & 1:
+        low_bit = 1 - low_bit
+    return (2 * high + low_bit) * 4 + 2 * y + x
+
+
+def greet(chip, core, z, y, x):
+    barrier = pltpu.get_barrier_semaphore()
+    friends = []
+    for k in range(4):
+        for flip in (0, 1):
+            if k or flip:
+                friends.append((column_of(z, y, x, k), core if flip == 0 else 1 - core))
+    friends.append((column_of(z, y, 1 - x, 0), core))
+    friends.append((column_of(z, 1 - y, x, 0), core))
+    for friend in friends:
+        pl.semaphore_signal(barrier, inc=1, device_id=friend, device_id_type=MESH)
+    pl.semaphore_wait(barrier, len(friends))
+
+
+def gather_kernel(own, out, near_s, local_s, col_r, x_s, x_r, y_s, y_r, ra_s, ra_r, rb_s, rb_r, sib_s, sib_r):
+    chip, core, z, y, x = place_of()
+    rank = z % 2
+    half = own.shape[1] // 2
+    part = half // 2
+    at_x = column_of(z, y, 1 - x, 0)
+    at_y = column_of(z, 1 - y, x, 0)
+    greet(chip, core, z, y, x)
+
+    def rows(ref, unit, first, count):
+        return ref.at[unit, :, pl.ds(pl.multiple_of(first, 16), count), :]
+
+    def remote(unit, first, count, send, recv, device):
+        piece = rows(out, unit, first, count)
+        return pltpu.make_async_remote_copy(
+            src_ref=piece, dst_ref=piece, send_sem=send, recv_sem=recv,
+            device_id=device, device_id_type=MESH,
+        )
+
+    started = []
+    for j in range(2):
+        zh = z // 2 if j == 0 else 1 - z // 2
+        target = (2 * zh + core) * 4 + 2 * y + x
+        for h in range(2):
+            src = own.at[:, pl.ds(h * half, half), :]
+            dst = out.at[chip, :, pl.ds(h * half, half), :]
+            go = pltpu.make_async_remote_copy(
+                src_ref=src, dst_ref=dst, send_sem=near_s.at[2 * j + h], recv_sem=col_r.at[z],
+                device_id=(target, h), device_id_type=MESH,
+            )
+            if j == 0:
+                here = pltpu.make_async_copy(src, dst, col_r.at[z])
+                stays = jnp.logical_and(rank == core, core == h)
+
+                @pl.when(stays)
+                def _():
+                    here.start()
+
+                @pl.when(jnp.logical_not(stays))
+                def _():
+                    go.start()
+
+                started.append((go, stays))
+            else:
+                go.start()
+                started.append((go, None))
+
+    def column_in(k):
+        unit = column_of(z, y, x, k)
+        source_z = unit // 4
+        piece = rows(out, unit, core * half, half)
+        pltpu.make_async_copy(piece, piece, col_r.at[source_z]).wait()
+        to_x = remote(unit, core * half, half, x_s.at[k], x_r.at[k], (at_x, core))
+        to_y = remote(unit, core * half, half, y_s.at[k], y_r.at[k], (at_y, core))
+        to_sib = remote(unit, core * half, half, sib_s.at[k], sib_r.at[k], (chip, 1 - core))
+        to_x.start()
+        to_y.start()
+        to_sib.start()
+        return [to_x, to_y, to_sib]
+
+    def side_in(k):
+        ux = column_of(z, y, 1 - x, k)
+        uy = column_of(z, 1 - y, x, k)
+        remote(ux, core * half, half, x_s.at[k], x_r.at[k], (at_x, core)).wait_recv()
+        on_y = remote(ux, core * half + part, part, rb_s.at[k], rb_r.at[k], (at_y, core))
+        on_y.start()
+        sib_x = remote(ux, core * half, half, sib_s.at[4 + k], sib_r.at[4 + k], (chip, 1 - core))
+        sib_x.start()
+        remote(uy, core * half, half, y_s.at[k], y_r.at[k], (at_y, core)).wait_recv()
+        on_x = remote(uy, core * half, part, ra_s.at[k], ra_r.at[k], (at_x, core))
+        on_x.start()
+        sib_y = remote(uy, core * half, half, sib_s.at[8 + k], sib_r.at[8 + k], (chip, 1 - core))
+        sib_y.start()
+        return [on_y, sib_x, on_x, sib_y]
+
+    def corner_in(k):
+        unit = column_of(z, 1 - y, 1 - x, k)
+        remote(unit, core * half, part, ra_s.at[k], ra_r.at[k], (at_x, core)).wait_recv()
+        sib_a = remote(unit, core * half, part, sib_s.at[12 + k], sib_r.at[12 + k], (chip, 1 - core))
+        sib_a.start()
+        remote(unit, core * half + part, part, rb_s.at[k], rb_r.at[k], (at_y, core)).wait_recv()
+        sib_b = remote(
+            unit, core * half + part, part, sib_s.at[16 + k], sib_r.at[16 + k], (chip, 1 - core)
+        )
+        sib_b.start()
+        return [sib_a, sib_b]
+
+    sent = []
+    for step in range(6):
+        if step < 4:
+            sent += column_in(step)
+        if 1 <= step < 5:
+            sent += side_in(step - 1)
+        if step >= 2:
+            sent += corner_in(step - 2)
+    for copy in sent:
+        copy.wait_send()
+    for go, stays in started:
+        if stays is None:
+            go.wait_send()
+        else:
+
+            @pl.when(jnp.logical_not(stays))
+            def _():
+                go.wait_send()
+
+    other = (1 - core) * half
+    for k in range(4):
+        for at, (yy, xx) in ((0, (y, x)), (4, (y, 1 - x)), (8, (1 - y, x))):
+            remote(
+                column_of(z, yy, xx, k), other, half, sib_s.at[at + k], sib_r.at[at + k],
+                (chip, 1 - core),
+            ).wait_recv()
+        corner = column_of(z, 1 - y, 1 - x, k)
+        remote(
+            corner, other, part, sib_s.at[12 + k], sib_r.at[12 + k], (chip, 1 - core)
+        ).wait_recv()
+        remote(
+            corner, other + part, part, sib_s.at[16 + k], sib_r.at[16 + k], (chip, 1 - core)
+        ).wait_recv()
+
+
+def gather_slots(scaled):
+    if not chip_pairs():
+        return lax.all_gather(scaled, "dp", axis=0, tiled=True)
+    dma = pltpu.SemaphoreType.DMA
+    counts = (4, 1, 4, 4, 4, 4, 4, 4, 4, 4, 4, 20, 20)
+    everyone = pl.pallas_call(
+        gather_kernel,
+        out_shape=jax.ShapeDtypeStruct((16,) + scaled.shape, scaled.dtype),
+        in_specs=[ANY],
+        out_specs=ANY,
+        scratch_shapes=[dma((n,)) for n in counts],
+        compiler_params=pltpu.CompilerParams(
+            collective_id=0, has_side_effects=True, vmem_limit_bytes=4 * MIB
+        ),
+    )(scaled)
+    return everyone.reshape((-1,) + scaled.shape[1:])
+
+
+def add_rows(*refs):
+    *terms, total = refs
+    slots, count, width = total.shape
+    spec = pl.BlockSpec((1, count, width), lambda i: (i, 0, 0))
+
+    def add(*blocks):
+        *parts, result = blocks
+        acc = parts[0][...].astype(jnp.float32)
+        for one in parts[1:]:
+            acc = acc + one[...].astype(jnp.float32)
+        result[...] = acc.astype(result.dtype)
+
+    pltpu.emit_pipeline(
+        add, grid=(slots,), in_specs=[spec] * len(terms), out_specs=[spec]
+    )(*terms, total)
+
+
+def reduce_kernel(
+    grads, final, from_sib, chip_sum, from_x, from_y, corner_a, corner_b,
+    sib_s, sib_r, x_s, x_r, y_s, y_r, ca_s, ca_r, cb_s, cb_r, f_s, f_r,
+):
+    chip, core, z, y, x = place_of()
+    rank = z % 2
+    half = grads.shape[2] // 2
+    part = half // 2
+    at_x = column_of(z, y, 1 - x, 0)
+    at_y = column_of(z, 1 - y, x, 0)
+    greet(chip, core, z, y, x)
+
+    def remote(src, dst, send, recv, device):
+        return pltpu.make_async_remote_copy(
+            src_ref=src, dst_ref=dst, send_sem=send, recv_sem=recv,
+            device_id=device, device_id_type=MESH,
+        )
+
+    columns = ((1 - y, 1 - x), (y, 1 - x), (1 - y, x), (y, x))
+    order = (3, 2, 1, 0)
+
+    def sib_copy(q, k):
+        unit = column_of(z, *columns[q], k)
+        src = grads.at[unit, :, pl.ds(pl.multiple_of((1 - core) * half, 16), half), :]
+        i = 4 * q + k
+        return remote(src, from_sib.at[i], sib_s.at[i], sib_r.at[i], (chip, 1 - core))
+
+    sent = []
+
+    def start_sib(q, k):
+        copy = sib_copy(q, k)
+        copy.start()
+        sent.append(copy)
+
+    for k in order:
+        for q in range(4):
+            start_sib(q, k)
+
+    def mine(q, k):
+        unit = column_of(z, *columns[q], k)
+        return grads.at[unit, :, pl.ds(pl.multiple_of(core * half, 16), half), :]
+
+    def sub(ref, first):
+        return ref.at[:, pl.ds(first, part), :]
+
+    def own_sub(q, k, first):
+        unit = column_of(z, *columns[q], k)
+        return grads.at[
+            unit, :, pl.ds(pl.multiple_of(core * half + first, 16), part), :
+        ]
+
+    def corner(k):
+        i = k
+        sib_copy(0, k).wait_recv()
+        add_rows(mine(0, k), from_sib.at[i], chip_sum.at[i])
+        a = remote(sub(chip_sum.at[i], 0), corner_a.at[k], ca_s.at[k], ca_r.at[k], (at_x, core))
+        b = remote(sub(chip_sum.at[i], part), corner_b.at[k], cb_s.at[k], cb_r.at[k], (at_y, core))
+        a.start()
+        b.start()
+        sent.extend([a, b])
+
+    def sides(k):
+        ix, iy = 4 + k, 8 + k
+        sib_copy(1, k).wait_recv()
+        sib_copy(2, k).wait_recv()
+        add_rows(own_sub(1, k, 0), sub(from_sib.at[ix], 0), sub(chip_sum.at[ix], 0))
+        add_rows(own_sub(2, k, part), sub(from_sib.at[iy], part), sub(chip_sum.at[iy], part))
+        remote(
+            sub(chip_sum.at[k], part), corner_b.at[k], cb_s.at[k], cb_r.at[k], (at_y, core)
+        ).wait_recv()
+        add_rows(
+            own_sub(1, k, part), sub(from_sib.at[ix], part), corner_b.at[k],
+            sub(chip_sum.at[ix], part),
+        )
+        to_x = remote(chip_sum.at[ix], from_x.at[k], x_s.at[k], x_r.at[k], (at_x, core))
+        to_x.start()
+        remote(
+            sub(chip_sum.at[k], 0), corner_a.at[k], ca_s.at[k], ca_r.at[k], (at_x, core)
+        ).wait_recv()
+        add_rows(
+            own_sub(2, k, 0), sub(from_sib.at[iy], 0), corner_a.at[k], sub(chip_sum.at[iy], 0)
+        )
+        to_y = remote(chip_sum.at[iy], from_y.at[k], y_s.at[k], y_r.at[k], (at_y, core))
+        to_y.start()
+        sent.extend([to_x, to_y])
+
+    finals = []
+
+    def centre(k):
+        i = 12 + k
+        sib_copy(3, k).wait_recv()
+        remote(chip_sum.at[4 + k], from_x.at[k], x_s.at[k], x_r.at[k], (at_x, core)).wait_recv()
+        remote(chip_sum.at[8 + k], from_y.at[k], y_s.at[k], y_r.at[k], (at_y, core)).wait_recv()
+        add_rows(mine(3, k), from_sib.at[i], from_x.at[k], from_y.at[k], chip_sum.at[i])
+        target = column_of(z, y, x, k)
+        dst = final.at[z // 2, :, pl.ds(pl.multiple_of(core * half, 16), half), :]
+        recv = f_r.at[2 * (z // 2) + core]
+        go = remote(chip_sum.at[i], dst, f_s.at[k], recv, (target, rank))
+        if k == 0:
+            stays = rank == core
+            here = pltpu.make_async_copy(chip_sum.at[i], dst, recv)
+
+            @pl.when(stays)
+            def _():
+                here.start()
+
+            @pl.when(jnp.logical_not(stays))
+            def _():
+                go.start()
+
+            finals.append((go, stays))
+        else:
+            go.start()
+            sent.append(go)
+
+    for step in range(6):
+        if step < 4:
+            corner(order[step])
+        if 1 <= step < 5:
+            sides(order[step - 1])
+        if step >= 2:
+            centre(order[step - 2])
+    for copy in sent:
+        copy.wait_send()
+    for go, stays in finals:
+
+        @pl.when(jnp.logical_not(stays))
+        def _():
+            go.wait_send()
+
+    for plane in range(2):
+        for h in range(2):
+            piece = final.at[plane, :, pl.ds(h * half, half), :]
+            pltpu.make_async_copy(piece, piece, f_r.at[2 * plane + h]).wait()
+
+
+def reduce_slots(grads, slot_count):
+    if not chip_pairs():
+        total = lax.psum_scatter(grads, "dp", scatter_dimension=0, tiled=True)
+        return total, None
+    width = grads.shape[1:]
+    half = width[0] // 2
+    dma = pltpu.SemaphoreType.DMA
+    units = grads.reshape((16, slot_count) + width)
+
+    def room(count, rows):
+        return jax.ShapeDtypeStruct((count, slot_count, rows, width[1]), grads.dtype)
+
+    counts = (16, 16) + (4,) * 12
+    outs = pl.pallas_call(
+        reduce_kernel,
+        out_shape=[
+            jax.ShapeDtypeStruct((2, slot_count) + width, grads.dtype),
+            room(16, half), room(16, half), room(4, half), room(4, half),
+            room(4, half // 2), room(4, half // 2),
+        ],
+        in_specs=[ANY],
+        out_specs=[ANY] * 7,
+        scratch_shapes=[dma((n,)) for n in counts[:12]],
+        compiler_params=pltpu.CompilerParams(
+            collective_id=1, has_side_effects=True, vmem_limit_bytes=16 * MIB
+        ),
+    )(units)
+    return outs[0][0], outs[0][1]
+
+
+def pick_blocks(everyone, places):
+    shape = everyone.shape[1:]
+    count = places.shape[0]
+
+    def copy(_, src, dst):
+        dst[...] = src[...]
+
+    return pl.pallas_call(
+        copy,
+        grid_spec=pltpu.PrefetchScalarGridSpec(
+            num_scalar_prefetch=1,
+            grid=(count,),
+            in_specs=[pl.BlockSpec((1,) + shape, lambda m, where: (where[m], 0, 0))],
+            out_specs=pl.BlockSpec((1,) + shape, lambda m, where: (m, 0, 0)),
+        ),
+        out_shape=jax.ShapeDtypeStruct((count,) + shape, everyone.dtype),
+    )(places, everyone)
+
+
+def kind_of_blocks(tile_count, heads_here, blocks_here):
+    number = jnp.arange(tile_count)
+    kind = number // heads_here
+    table = jnp.array([0, 0, 0, 1, 2, 3, 3, 4], jnp.int32)
+    late = jnp.where(number < 8 * heads_here + blocks_here, 5, 6)
+    return jnp.where(number < 8 * heads_here, table[jnp.minimum(kind, 7)], late).astype(jnp.int32)
+
+
+def slot_grads(holder, kinds, rows, columns):
+    depth = max(r.shape[0] for r in rows)
+
+    def deep(value, axis):
+        room = [(0, 0)] * value.ndim
+        room[axis] = (0, depth - value.shape[axis])
+        return jnp.pad(value, room)
+
+    left = jnp.stack([deep(r, 0) for r in rows])
+    right = jnp.concatenate([deep(c, 0) for c in columns], 1).transpose(1, 0, 2)
+    slots = holder.shape[0]
+    used = (holder >= 0).astype(jnp.int32)
+    block = jnp.maximum(holder, 0)
+    kind = kinds[block]
+    width = rows[0].shape[1]
+    lanes = right.shape[2]
+
+    def multiply(kind_ref, block_ref, used_ref, left_ref, right_ref, out_ref):
+        slot = pl.program_id(0)
+
+        @pl.when(used_ref[slot] == 1)
+        def _():
+            out_ref[0] = lax.dot_general(
+                left_ref[kind_ref[slot]],
+                right_ref[0],
+                (((0,), (0,)), ((), ())),
+                preferred_element_type=jnp.float32,
+            ).astype(out_ref.dtype)
+
+        @pl.when(used_ref[slot] == 0)
+        def _():
+            out_ref[...] = jnp.zeros_like(out_ref)
+
+    return pl.pallas_call(
+        multiply,
+        grid_spec=pltpu.PrefetchScalarGridSpec(
+            num_scalar_prefetch=3,
+            grid=(slots,),
+            in_specs=[
+                pl.BlockSpec(left.shape, lambda s, kd, b, u: (0, 0, 0)),
+                pl.BlockSpec((1, depth, lanes), lambda s, kd, b, u: (b[s], 0, 0)),
+            ],
+            out_specs=pl.BlockSpec((1, width, lanes), lambda s, kd, b, u: (s, 0, 0)),
+        ),
+        out_shape=jax.ShapeDtypeStruct((slots, width, lanes), jnp.bfloat16),
+        compiler_params=pltpu.CompilerParams(vmem_limit_bytes=48 * MIB),
+    )(kind, block, used, left, right)
+
+
+def adam_slots(first_part, second_part, master, moment_one, moment_two, slot_scale, filled):
+    slot_count, width, lanes = master.shape[1:]
+    parts = [first_part] if second_part is None else [first_part, second_part]
+    count = len(parts)
+    tall = width // 2
+
+    def step(scale_ref, fill_ref, *refs):
+        grads = refs[:count]
+        weight, one, two, new_weight, new_one, new_two = refs[count:]
+        slot = pl.program_id(0)
+
+        @pl.when(fill_ref[slot] == 1)
+        def _():
+            total = grads[0][0].astype(jnp.float32)
+            for more in grads[1:]:
+                total = total + more[0].astype(jnp.float32)
+            results = adam_step(
+                weight[0, 0], total * scale_ref[slot], one[0, 0], two[0, 0], TILE_RATE, TILE_DECAY
+            )
+            for ref, value in zip((new_weight, new_one, new_two), results):
+                ref[0, 0] = value
+
+        @pl.when(fill_ref[slot] == 0)
+        def _():
+            new_weight[...] = weight[...]
+            new_one[...] = one[...]
+            new_two[...] = two[...]
+
+    flat = pl.BlockSpec((1, tall, lanes), lambda s, i: (s, i, 0))
+    deep = pl.BlockSpec((1, 1, tall, lanes), lambda s, i: (0, s, i, 0))
+    scalars = pl.BlockSpec(memory_space=pltpu.SMEM)
+    return pl.pallas_call(
+        step,
+        grid=(slot_count, 2),
+        in_specs=[scalars, scalars] + [flat] * count + [deep] * 3,
+        out_specs=[deep] * 3,
+        out_shape=[jax.ShapeDtypeStruct(master.shape, jnp.float32)] * 3,
+    )(slot_scale, filled.astype(jnp.int32), *parts, master, moment_one, moment_two)
 
 
 def body(
@@ -199,12 +712,16 @@
     places, holder = owner_layout(owners, slot_count, devices)
     scales = tile_scales(tile_count, heads_here, blocks_here)
     my_slots = lax.dynamic_slice_in_dim(holder, lax.axis_index("dp") * slot_count, slot_count)
+    rank = pair_rank()
+    latents, context, cotangent, positions, step_ids, head_here = home_swap(
+        latents, context, cotangent, positions, step_ids, head_params
+    )
     filled = my_slots >= 0
     slot_scale = jnp.where(filled, scales[jnp.maximum(my_slots, 0)], 0.0)
     scaled = (master[0] * slot_scale[:, None, None]).astype(jnp.bfloat16)
-    everyone = lax.all_gather(scaled, "dp", axis=0, tiled=True)
-    pieces = tile_views(jnp.take(everyone, places, axis=0), heads_here, blocks_here)
-    vectors = head_params[0]
+    everyone = gather_slots(scaled)
+    pieces = tile_views(pick_blocks(everyone, places), heads_here, blocks_here)
+    vectors = head_here[0]
 
     def head_vector(number):
         return vectors[number * width_here : (number + 1) * width_here].reshape(heads_here, HEAD)
@@ -231,16 +748,20 @@
         return layer_norm(inputs) * gain_vec + bias_vec
 
     def spread_rows(local_rows):
-        return lax.all_gather(local_rows, "tensor", axis=0, tiled=True)
+        other = pair_swap(local_rows)
+        return jnp.where(
+            rank == 0,
+            jnp.concatenate([local_rows, other], 0),
+            jnp.concatenate([other, local_rows], 0),
+        )
 
     def merge_rows(summand):
-        return lax.psum_scatter(summand, "tensor", scatter_dimension=0, tiled=True)
-
-    def spread_grads(local_rows):
-        return lax.all_gather(local_rows, "tensor", axis=0, tiled=True)
-
-    def merge_grads(summand):
-        return lax.psum_scatter(summand, "tensor", scatter_dimension=0, tiled=True)
+        half = summand.shape[0] // 2
+        mine = lax.dynamic_slice_in_dim(summand, rank * half, half, 0)
+        theirs = lax.dynamic_slice_in_dim(summand, (1 - rank) * half, half, 0)
+        return mine + pair_swap(theirs.astype(jnp.bfloat16)).astype(jnp.float32)
+
+    spread_grads, merge_grads = spread_rows, merge_rows
 
     residual = latents.astype(jnp.float32)
     low_one = mod_norm(residual, shift_attn, scale_attn).astype(jnp.bfloat16)
@@ -300,12 +821,11 @@
     d_down_bias = jnp.sum(grad_branch.astype(jnp.float32), 0)
     rows_grad = spread_grads(grad_branch)
     hidden_pre, hidden_low = saved_three
-    d_down = product("tfe,td->fde", hidden_low, rows_grad)
+    rows_grad_three = rows_grad
     d_hidden = product("td,fde->tfe", rows_grad, pieces[9])
     d_hidden = jax.vjp(gelu_tanh, hidden_pre)[1](d_hidden)[0]
     d_hidden_low = d_hidden.astype(jnp.bfloat16)
     d_up_bias = jnp.sum(d_hidden_low.astype(jnp.float32), 0)
-    d_up = product("td,tfe->fde", rows_three, d_hidden_low)
     grad_norm = merge_grads(product("tfe,fde->td", d_hidden_low, pieces[8]))
     d_inputs, d_shift_ffn, d_scale_ffn = jax.vjp(mod_norm, after_two, shift_ffn, scale_ffn)[1](
         grad_norm
@@ -317,7 +837,7 @@
     query_pre, key_pre, query_inv, key_inv, query_low, key_low, value_low, log_total, heads_out = (
         saved_two
     )
-    d_cross_out = product("the,td->hde", heads_out, rows_grad)
+    rows_grad_two, cross_heads_out = rows_grad, heads_out
     d_heads = product("td,hde->the", rows_grad, pieces[7]).astype(jnp.bfloat16)
     d_query, d_key, d_value = attend_back(
         query_low, key_low, value_low, log_total, d_heads, scaling
@@ -331,9 +851,7 @@
     d_cross_bias_q = jnp.sum(query_grad.astype(jnp.float32), 0)
     d_cross_bias_k = jnp.sum(key_grad.astype(jnp.float32), 0)
     d_cross_bias_v = jnp.sum(value_grad.astype(jnp.float32), 0)
-    d_cross_query = product("td,the->hde", rows_two, query_grad)
-    d_cross_key = product("cd,che->hde", context, key_grad)
-    d_cross_value = product("cd,che->hde", context, value_grad)
+    cross_query_grad, cross_key_grad, cross_value_grad = query_grad, key_grad, value_grad
     grad_norm = merge_grads(product("the,hde->td", query_grad, pieces[4]))
     d_inputs, d_norm_gain, d_norm_bias = jax.vjp(
         affine_norm, after_one, shared_params[3], shared_params[4]
@@ -346,7 +864,6 @@
     query_pre, key_pre, query_inv, key_inv, query_low, key_low, value_low, log_total, heads_out = (
         saved_one
     )
-    d_self_out = product("the,td->hde", heads_out, rows_grad)
     d_heads = product("td,hde->the", rows_grad, pieces[3]).astype(jnp.bfloat16)
     d_query, d_key, d_value = attend_back(
         query_low, key_low, value_low, log_total, d_heads, scaling
@@ -362,9 +879,6 @@
     d_bias_query = jnp.sum(query_grad.astype(jnp.float32), 0)
     d_bias_key = jnp.sum(key_grad.astype(jnp.float32), 0)
     d_bias_value = jnp.sum(value_grad.astype(jnp.float32), 0)
-    d_self_query = product("td,the->hde", rows_one, query_grad)
-    d_self_key = product("td,the->hde", rows_one, key_grad)
-    d_self_value = product("td,the->hde", rows_one, value_grad)
     input_sum = (
         product("the,hde->td", query_grad, pieces[0])
         + product("the,hde->td", key_grad, pieces[1])
@@ -375,33 +889,27 @@
         grad_norm
     )
     grad_input = grad_res + d_inputs
-    all_grads = jnp.concatenate(
-        [
-            d_self_query,
-            d_self_key,
-            d_self_value,
-            d_self_out,
-            d_cross_query,
-            d_cross_key,
-            d_cross_value,
-            d_cross_out,
-            d_up,
-            d_down,
-        ],
-        0,
-    )
-    picked = jnp.take(all_grads, jnp.maximum(holder, 0), axis=0)
-    reduced = lax.psum_scatter(
-        jnp.where((holder >= 0)[:, None, None], picked, 0.0), "dp", scatter_dimension=0, tiled=True
-    )
-    grad_master = reduced * slot_scale[:, None, None]
-    new_w, new_m, new_v = adam_step(
-        master[0], grad_master, first_moment[0], second_moment[0], TILE_RATE, TILE_DECAY
-    )
-    slot_mask = filled[:, None, None]
-    new_master = jnp.where(slot_mask, new_w, master[0])[None]
-    new_first = jnp.where(slot_mask, new_m, first_moment[0])[None]
-    new_second = jnp.where(slot_mask, new_v, second_moment[0])[None]
+    grads = slot_grads(
+        holder,
+        kind_of_blocks(tile_count, heads_here, blocks_here),
+        (rows_one, rows_grad, rows_two, context, rows_grad_two, rows_three, rows_grad_three),
+        (
+            query_grad,
+            key_grad,
+            value_grad,
+            heads_out,
+            cross_query_grad,
+            cross_key_grad,
+            cross_value_grad,
+            cross_heads_out,
+            d_hidden_low,
+            hidden_low,
+        ),
+    )
+    first_part, second_part = reduce_slots(grads, slot_count)
+    new_master, new_first, new_second = adam_slots(
+        first_part, second_part, master, first_moment, second_moment, slot_scale, filled
+    )
     head_grad = jnp.concatenate(
         [
             d_bias_query.reshape(-1),
@@ -418,7 +926,7 @@
         ]
     )
     tensor_rank = lax.axis_index("tensor")
-    head_padded = jnp.where(jnp.arange(tensors)[:, None] == tensor_rank, head_grad[None, :], 0.0)
+    head_padded = jnp.where(jnp.arange(tensors)[:, None] == rank, head_grad[None, :], 0.0)
     shared_grad = jnp.stack(
         [
             d_self_bias_out,
@@ -442,6 +950,7 @@
     new_shared, new_shared_first, new_shared_second = adam_step(
         shared_params, shared_total, shared_first, shared_second, VECTOR_RATE, 0.0
     )
+    output, grad_input = home_swap(output, grad_input)
     return (
         output,
         grad_input,

time: 2820 us -> 1260 us (0.45)
  waiting for transfers between devices: 2070 us -> 216 us
  Pallas kernels: 0 us -> 758 us
  local copies, waits for them, and re-layouts: 282 us -> 69.8 us
  other arithmetic: 198 us -> 54.9 us
  matrix products: 167 us -> 93.5 us
  blocking collectives: 61.8 us -> 0 us
    reduce_scatter x1 -> x0, waiting for transfers between devices: 1500 us -> none  [body(): lax.psum_scatter(jnp.where((holder >= 0)[:, None, None], picked, 0.0), 'd...]
    pallas_call x0 -> x5, Pallas kernels: none -> 758 us  [the longest x1 290 us: reduce_slots(): pl.pallas_call(reduce_kernel, out_shape=[jax.ShapeDtypeStruct((2, slot_co...]
    all_gather x1 -> x0, waiting for transfers between devices: 540 us -> none  [body(): everyone = lax.all_gather(scaled, 'dp', axis=0, tiled=True)]
    gather x2 -> x1, local copies, waits for them, and re-layouts: 107 us -> 1.55 us  [slot_grads(): kind = kinds[block]]
    select_n x4 -> x12, other arithmetic: 107 us -> 8.86 us  [the longest x6 4.67 us: spread_rows(): jnp.where(rank == 0, jnp.concatenate([local_rows, other], 0), jnp.concate...]
    ppermute x0 -> x24, waiting for transfers between devices: none -> 93.2 us  [the longest x16 93.2 us: pair_swap(): return lax.ppermute(value, 'dp', [(i, i ^ 4) for i in range(16)])]
    psum x1, waiting for transfers between devices: 32.7 us -> 123 us  [body(): lax.psum((head_padded, shared_grad), ('dp', 'tensor'))]
    unnamed x329 -> x270, local copies, waits for them, and re-layouts: 101 us -> 22.9 us
  transfers between devices with their start and end apart: 9 -> 25, of which waited for: 3 -> 13; matrix products, arithmetic and copies ran while one was open for 11% -> 7% of each run, Pallas kernels for 0% -> 61%
where the time goes in v1:
time: 1260 us; the launch traced here: 1240 us
  Pallas kernels  758 us (60%)
  waiting for transfers between devices  216 us (17%)
  matrix products  93.5 us (7%)
  local copies, waits for them, and re-layouts  69.8 us (6%)
  other arithmetic  54.9 us (4%)
  starting transfers between devices  27 us (2%)
  between operations  17.6 us (1%)
    pallas_call x1, Pallas kernels, reduce_slots(): pl.pallas_call(reduce_kernel, out_shape=[jax.ShapeDtypeStruct((2, slot_co...  290 us
    pallas_call x1, Pallas kernels, gather_slots(): pl.pallas_call(gather_kernel, out_shape=jax.ShapeDtypeStruct((16,) + scal...  248 us
    psum x1, waiting for transfers between devices, body(): lax.psum((head_padded, shared_grad), ('dp', 'tensor'))  123 us
    pallas_call x1, Pallas kernels, slot_grads(): pl.pallas_call(multiply, grid_spec=pltpu.PrefetchScalarGridSpec(num_scala...  122 us
    ppermute x16, waiting for transfers between devices, pair_swap(): return lax.ppermute(value, 'dp', [(i, i ^ 4) for i in range(16)])  93.2 us
    dot_general x30, matrix products, product(): return jnp.einsum(form, left, right, preferred_element_type=jnp.float32)  93.2 us
    pallas_call x1, Pallas kernels, pick_blocks(): pl.pallas_call(copy, grid_spec=pltpu.PrefetchScalarGridSpec(num_scalar_pr...  73.3 us
  transfers between devices with their start and end apart: 25, of which 13 were waited for; matrix products, arithmetic and copies ran while one was open for 7% of the time, Pallas kernels for 61%

profile of v1, /device:TPU:9, one launch (start us, length us, event | category | flops | bytes accessed | tf_op | source)
XLA Modules:
  0.0 1236.6 jit_solution(12403422726168223507)
XLA Ops:
  13.9 3.7 fusion.8.own
  17.7 248.0 %shard_map.248 = bf16[16,9,1536,128]{3,2,1,0:T(8,128)(2,1)} custom-call(bf16[9,1536,128]{2,1,0:T(8,128)(2,1)S(1)} %fusion.8.own), custom_call_target="tpu_custom_call" | custom-call | tf_op jit(solution)/shard_map/pallas_call | solution.py:374
  265.7 73.3 %shard_map.249 = bf16[118,1536,128]{2,1,0:T(8,128)(2,1)} custom-call(s32[118]{0:T(128)} %copy-done.121, bf16[144,1536,128]{2,1,0:T(8,128)(2,1)} %bitcast.222), custom_call_target="tpu_custom_call" | custom-call | tf_op jit(solution)/shard_map/pallas_call | solution.py:577
  344.6 10.4 collective-permute-done.2
  355.3 2.9 multiply_reduce_fusion.17
  358.2 2.9 multiply_reduce_fusion.18
  361.5 3.2 fusion.75
  366.5 2.0 reshape.363
  370.6 1.8 reshape.364
  372.4 2.5 copy.55
  376.3 2.2 reshape.361
  380.6 1.8 reshape.362
  382.5 2.6 copy.53
  388.6 2.7 convolution_bitcast_fusion.5
  394.3 2.2 collective-permute-start.7
  396.7 6.6 collective-permute-done.6
  403.2 1.6 fusion.166
  406.5 1.6 broadcast_select_fusion
  408.2 3.7 multiply_reduce_fusion.4
  411.9 18.7 %collective-permute-done.8 = bf16[130,1536]{1,0:T(8,128)(2,1)S(1)} collective-permute-done((bf16[130,1536]{1,0:T(8,128)(2,1)S(1)}, bf16[130,1536]{1,0:T(8,128)(2,1)S(1)}, u32[]{:S(2)}, u32[]{:S(2)}) %collective-permute-start.8) | collective-permute-done | bytes 399392 | tf_op jit(solution)/shard_map/ppermute | solution.py:191
  430.9 2.9 multiply_reduce_fusion.16
  433.9 2.3 collective-permute-start.9
  436.2 3.0 add_convert_fusion
  442.1 2.6 convolution_bitcast_fusion.4
  445.2 11.0 collective-permute-done.10
  458.8 8.5 collective-permute-done.11
  467.6 9.6 multiply_convert_fusion
  477.2 8.0 fusion.18
  485.4 8.0 collective-permute-done.12
  496.3 1.6 gather_fusion.1
  497.9 5.3 collective-permute-done.15
  503.2 1.9 maximum_select_fusion.3
  505.1 12.0 convert_reduce_fusion
  517.1 8.5 fusion.15
  528.4 4.3 collective-permute-done.16
  538.0 1.7 copy.61
  539.7 3.3 collective-permute-done.17
  543.0 1.7 maximum_select_fusion.4
  544.7 2.6 fusion.81
  551.8 1.9 fusion.49
  557.9 2.6 convolution_bitcast_fusion.3
  560.7 9.9 collective-permute-start.19
  573.2 8.4 collective-permute-done.19
  585.8 2.1 convert_reduce_fusion.2
  588.5 7.8 collective-permute-done.20
  596.5 2.5 fusion.78
  601.7 1.8 broadcast_multiply_fusion
  603.4 1.7 broadcast_multiply_fusion.1
  611.4 3.7 convolution_bitcast_fusion
  623.7 1.8 reshape.368
  625.6 2.6 copy.64
  628.3 2.4 multiply_reduce_fusion.13
  633.7 2.5 convolution_bitcast_fusion.1
  637.8 2.6 fusion.22
  646.5 2.2 constant_dynamic-update-slice_fusion
  649.7 2.9 pad_dynamic-update-slice_fusion.1
  652.6 2.9 pad_dynamic-update-slice_fusion
  655.6 121.9 %shard_map.250 = bf16[144,1536,128]{2,1,0:T(8,128)(2,1)} custom-call(s32[144]{0:T(256)S(1)} %gather_fusion.1, s32[144]{0:T(256)S(1)} %get-tuple-element.122.block_ref, s32[144]{0:T(256)S(1)} %compare_convert_fusion.used_ref, bf16[7,512,1536]{2,1,0:T(8,128)(2,1)} %bitcast_dynamic-update-slice_fusion.left_ref, bf16[118,512,128]{2,1,0:T(8,128)(2,1)} %bitcast.39.right_ref), custom_call_target="tpu_custom_call" | custom-call | tf_op jit(solution)/shard_map/pallas_call | solution.py:630
  777.5 290.2 %shard_map.251 = (bf16[2,9,1536,128]{3,2,1,0:T(8,128)(2,1)S(1)}, bf16[16,9,768,128]{3,2,1,0:T(8,128)(2,1)}, bf16[16,9,768,128]{3,2,1,0:T(8,128)(2,1)}, bf16[4,9,...) custom-call(bf16[16,9,1536,128]{3,2,1,0:T(8,128)(2,1)} %bitcast.221), custom_call_target="tpu_custom_call" | custom-call | tf_op jit(solution)/shard_map/pallas_call | solution.py:553
  1068.7 3.4 slice_bitcast_fusion
  1072.1 24.3 %shard_map.252 = (f32[1,9,1536,128]{3,2,1,0:T(8,128)}, f32[1,9,1536,128]{3,2,1,0:T(8,128)}, f32[1,9,1536,128]{3,2,1,0:T(8,128)}) custom-call(f32[9]{0:T(128)} %copy-done.118, s32[9]{0:T(128)} %compare_convert_fusion.1.fill_ref, bf16[9,1536,128]{2,1,0:T(8,128)(2,1)} %get-tuple-element.101.refs_0_, bf16[9,1536,128]{2,1,0:T(8,128)(2,1)} %get-tuple-element.100.refs_1_, ...), custom_call_target="tpu_custom_call" | custom-call | tf_op jit(solution)/shard_map/pallas_call | solution.py:677
  1101.9 123.0 %all-reduce.17.cloned.1.call-done = (f32[2,12160]{1,0:T(2,128)}, f32[11,1536]{1,0:T(8,128)}) async-done(((f32[2,12160]{1,0:T(2,128)}, f32[11,1536]{1,0:T(8,128)}), (f32[2,12160]{1,0:T(2,128)}, f32[11,1536]{1,0:T(8,128)})) %all-reduce.17.cloned.1.call-update) | async-done | bytes 164880 | tf_op jit(solution)/shard_map/psum | solution.py:945
  1225.0 1.9 multiply_subtract_fusion.1
  1226.9 1.6 multiply_subtract_fusion
  (454 shorter events, 97.0 us)
Async XLA Ops:
  7.2 332.4 %copy-start = (f32[16,6,1536]{2,0,1:T(8,128)S(1)}, f32[16,6,1536]{2,0,1:T(8,128)}, u32[]{:S(2)}) copy-start(f32[16,6,1536]{2,0,1:T(8,128)} %param.23) | copy-start | bytes 1769476
  7.2 1217.8 %all-reduce.17.cloned.1.call-start = ((), (), s32[]{:S(2)}) async-start(), calls=%async_computation | async-start | bytes 391168 | tf_op jit(solution)/shard_map/psum | solution.py:945
  7.2 331.7 %collective-permute-start.1 = (s32[1]{0:T(128)}, s32[1]{0:T(128)}, u32[]{:S(2)}, u32[]{:S(2)}) collective-permute-start(s32[1]{0:T(128)} %param.21), channel_id=1, source_target_pairs={{1,8},{3,10},{5,12},{7,14},{8,1},{10,3},{12,5},{14,7},{17,24},{19,... | collective-permute-start | bytes 20 | tf_op jit(solution)/shard_map/ppermute | solution.py:214
  8.5 332.1 %collective-permute-start.5 = (s32[3,260]{1,0:T(4,128)}, s32[3,260]{1,0:T(4,128)S(1)}, u32[]{:S(2)}, u32[]{:S(2)}) collective-permute-start(s32[3,260]{1,0:T(4,128)} %param.20), channel_id=1, source_target_pairs={{1,8},{3,10},{5,12},{7,14},{8,1},{10,3},{12,5},{14,7},{17,24},{19,... | collective-permute-start | bytes 9368 | tf_op jit(solution)/shard_map/ppermute | solution.py:214
  9.2 335.2 %collective-permute-start.3 = (f32[1,12160]{1,0:T(1,128)}, f32[1,12160]{1,0:T(1,128)S(1)}, u32[]{:S(2)}, u32[]{:S(2)}) collective-permute-start(f32[1,12160]{1,0:T(1,128)} %param.27), channel_id=1, source_target_pairs={{1,8},{3,10},{5,12},{7,14},{8,1},{10,3},{12,5},{14,7},{17,24},{19,... | collective-permute-start | bytes 145928 | tf_op jit(solution)/shard_map/ppermute | solution.py:214
  9.9 333.3 %collective-permute-start = (bf16[130,1536]{1,0:T(8,128)(2,1)}, bf16[130,1536]{1,0:T(8,128)(2,1)S(1)}, u32[]{:S(2)}, u32[]{:S(2)}) collective-permute-start(bf16[130,1536]{1,0:T(8,128)(2,1)} %param.17), channel_id=1, source_target_pairs={{1,8},{3,10},{5,12},{7,14},{8,1},{10,3},{12,5},{14,7},{17,24},{19,... | collective-permute-start | bytes 1198088 | tf_op jit(solution)/shard_map/ppermute | solution.py:214
  265.6 74.2 %copy-start.69 = (f32[11,1536]{1,0:T(8,128)S(1)}, f32[11,1536]{1,0:T(8,128)}, u32[]{:S(2)}) copy-start(f32[11,1536]{1,0:T(8,128)} %param.30) | copy-start | bytes 202756
  265.7 75.0 %copy-start.117 = (s32[3,260]{1,0:T(4,128)S(1)}, s32[3,260]{1,0:T(4,128)}, u32[]{:S(2)}) copy-start(s32[3,260]{1,0:T(4,128)} %param.20) | copy-start | bytes 9364
  343.4 59.9 %copy-start.11 = (bf16[130,1536]{1,0:T(8,128)(2,1)}, bf16[130,1536]{1,0:T(8,128)(2,1)S(1)}, u32[]{:S(2)}) copy-start(bf16[130,1536]{1,0:T(8,128)(2,1)S(1)} %get-tuple-element.99) | copy-start | bytes 1198084
  344.0 11.0 collective-permute-start.2
  344.5 13.7 %copy-start.71 = (f32[1,12160]{1,0:T(1,128)}, f32[1,12160]{1,0:T(1,128)S(1)}, u32[]{:S(2)}) copy-start(f32[1,12160]{1,0:T(1,128)S(1)} %broadcast_select_fusion.6) | copy-start | bytes 145924
  344.6 20.3 %copy-start.83 = (f32[768]{0:T(1024)}, f32[768]{0:T(1024)S(1)}, u32[]{:S(2)}) copy-start(f32[768]{0:T(1024)S(1)} %get-tuple-element.52) | copy-start | bytes 9220
  361.2 3.6 collective-permute-start.4
  388.6 14.7 %copy-start.80 = (f32[1536]{0:T(1024)S(1)}, f32[1536]{0:T(1024)}, u32[]{:S(2)}) copy-start(f32[1536]{0:T(1024)} %get-tuple-element.46) | copy-start | bytes 18436
  393.2 10.0 collective-permute-start.6
  394.3 12.2 collective-permute-start.7
  396.6 11.5 copy-start.78
  404.9 51.3 %copy-start.5 = (f32[130,1536]{1,0:T(8,128)}, f32[130,1536]{1,0:T(8,128)S(1)}, u32[]{:S(2)}) copy-start(f32[130,1536]{1,0:T(8,128)S(1)} %get-tuple-element.97) | copy-start | bytes 2396164
  405.4 25.2 %collective-permute-start.8 = (bf16[130,1536]{1,0:T(8,128)(2,1)S(1)}, bf16[130,1536]{1,0:T(8,128)(2,1)S(1)}, u32[]{:S(2)}, u32[]{:S(2)}) collective-permute-start(bf16[130,1536]{1,0:T(8,128)(2,1)S(1)} %add_convert_fusion.3), channel_id=1, source_target_pairs={{0,8},{2,10},{4,12},{6,14},{8,0},{10,2},{12,4},{14,6},{16,24},{18,... | collective-permute-start | bytes 1198088 | tf_op jit(solution)/shard_map/ppermute | solution.py:191
  408.2 28.1 %copy-start.23 = (bf16[512,1536]{1,0:T(8,128)(2,1)}, bf16[512,1536]{1,0:T(8,128)(2,1)S(1)}, u32[]{:S(2)}) copy-start(bf16[512,1536]{1,0:T(8,128)(2,1)S(1)} %broadcast_select_fusion) | copy-start | bytes 4718596
  411.9 27.6 %copy-start.9 = (f32[512,6,128]{2,0,1:T(8,128)}, f32[512,6,128]{2,0,1:T(8,128)S(1)}, u32[]{:S(2)}) copy-start(f32[512,6,128]{2,0,1:T(8,128)S(1)} %get-tuple-element.133) | copy-start | bytes 4718596
  433.9 5.4 collective-permute-start.9
  444.8 12.0 copy-start.91
  444.9 11.3 collective-permute-start.10
  456.5 36.9 %copy-start.7 = (f32[130,1536]{1,0:T(8,128)}, f32[130,1536]{1,0:T(8,128)S(1)}, u32[]{:S(2)}) copy-start(f32[130,1536]{1,0:T(8,128)S(1)} %get-tuple-element.95) | copy-start | bytes 2396164
  457.0 10.3 collective-permute-start.11
  457.2 28.3 %collective-permute-start.14 = (bf16[130,1536]{1,0:T(8,128)(2,1)S(1)}, bf16[130,1536]{1,0:T(8,128)(2,1)S(1)}, u32[]{:S(2)}, u32[]{:S(2)}) collective-permute-start(bf16[130,1536]{1,0:T(8,128)(2,1)S(1)} %copy-done.68), channel_id=1, source_target_pairs={{1,8},{3,10},{5,12},{7,14},{8,1},{10,3},{12,5},{14,7},{17,24},{19,... | collective-permute-start | bytes 1198088 | tf_op jit(solution)/shard_map/ppermute | solution.py:214
  477.2 16.2 %copy-start.82 = (f32[1536]{0:T(1024)S(1)}, f32[1536]{0:T(1024)}, u32[]{:S(2)}) copy-start(f32[1536]{0:T(1024)} %get-tuple-element.41) | copy-start | bytes 18436
  485.3 8.0 collective-permute-start.12
  496.0 7.2 collective-permute-start.15
  505.1 12.0 copy-start.32
  517.1 10.6 copy-start.50
  517.1 15.6 %copy-start.8 = (f32[130,1536]{1,0:T(8,128)S(1)}, f32[130,1536]{1,0:T(8,128)}, u32[]{:S(2)}) copy-start(f32[130,1536]{1,0:T(8,128)} %copy-done.7) | copy-start | bytes 2396164
  525.7 7.0 collective-permute-start.16
  533.6 11.0 copy-start.115
  535.5 7.4 collective-permute-start.17
  553.8 3.6 collective-permute-start.18
  556.8 13.9 %collective-permute-start.13 = (bf16[130,1536]{1,0:T(8,128)(2,1)S(1)}, bf16[130,1536]{1,0:T(8,128)(2,1)S(1)}, u32[]{:S(2)}, u32[]{:S(2)}) collective-permute-start(bf16[130,1536]{1,0:T(8,128)(2,1)S(1)} %copy-done.51), channel_id=1, source_target_pairs={{1,8},{3,10},{5,12},{7,14},{8,1},{10,3},{12,5},{14,7},{17,24},{19,... | collective-permute-start | bytes 1198088 | tf_op jit(solution)/shard_map/ppermute | solution.py:214
  557.9 23.8 %copy-start.103 = (f32[130]{0:T(256)S(1)}, f32[130]{0:T(256)}, u32[]{:S(2)}) copy-start(f32[130]{0:T(256)} %copy-done.102) | copy-start | bytes 1564
  560.6 21.1 %copy-start.6 = (f32[130,1536]{1,0:T(8,128)S(1)}, f32[130,1536]{1,0:T(8,128)}, u32[]{:S(2)}) copy-start(f32[130,1536]{1,0:T(8,128)} %copy-done.5) | copy-start | bytes 2396164
  560.6 21.6 %copy-start.112 = (f32[130]{0:T(256)S(1)}, f32[130]{0:T(256)}, u32[]{:S(2)}) copy-start(f32[130]{0:T(256)} %copy-done.111) | copy-start | bytes 1564
  560.7 21.0 %collective-permute-start.19 = (bf16[130,1536]{1,0:T(8,128)(2,1)S(1)}, bf16[130,1536]{1,0:T(8,128)(2,1)S(1)}, u32[]{:S(2)}, u32[]{:S(2)}) collective-permute-start(bf16[130,1536]{1,0:T(8,128)(2,1)S(1)} %dynamic-slice_convert_fusion.1), channel_id=1, source_target_pairs={{0,8},{2,10},{4,12},{6,14},{8,0},{10,2},{12,4},{14,6},{16,24},{18,... | collective-permute-start | bytes 1198088 | tf_op jit(solution)/shard_map/ppermute | solution.py:191
  585.1 11.1 collective-permute-start.20
  600.0 11.4 copy-start.58
  630.8 2.5 collective-permute-start.21
  641.3 455.2 %collective-permute-start.22 = (bf16[130,1536]{1,0:T(8,128)(2,1)}, bf16[130,1536]{1,0:T(8,128)(2,1)S(1)}, u32[]{:S(2)}, u32[]{:S(2)}) collective-permute-start(bf16[130,1536]{1,0:T(8,128)(2,1)} %dynamic-slice_convert_fusion), channel_id=1, source_target_pairs={{0,8},{2,10},{4,12},{6,14},{8,0},{10,2},{12,4},{14,6},{16,24},{18,... | collective-permute-start | bytes 1198088 | tf_op jit(solution)/shard_map/ppermute | solution.py:191
  777.5 290.3 %copy-start.108 = (f32[6,128]{1,0:T(8,128)S(1)}, f32[6,128]{1,0:T(8,128)}, u32[]{:S(2)}) copy-start(f32[6,128]{1,0:T(8,128)} %get-tuple-element.78) | copy-start | bytes 9220
  777.5 290.3 %copy-start.107 = (f32[6,128]{1,0:T(8,128)S(1)}, f32[6,128]{1,0:T(8,128)}, u32[]{:S(2)}) copy-start(f32[6,128]{1,0:T(8,128)} %get-tuple-element.30) | copy-start | bytes 9220
  777.5 290.3 %copy-start.104 = (f32[6,128]{1,0:T(8,128)S(1)}, f32[6,128]{1,0:T(8,128)}, u32[]{:S(2)}) copy-start(f32[6,128]{1,0:T(8,128)} %get-tuple-element.19) | copy-start | bytes 9220
  777.5 290.4 %copy-start.101 = (f32[35,128]{1,0:T(8,128)S(1)}, f32[35,128]{1,0:T(8,128)}, u32[]{:S(2)}) copy-start(f32[35,128]{1,0:T(8,128)} %get-tuple-element.154) | copy-start | bytes 53764
  777.5 290.4 %copy-start.122 = (pred[2]{0:T(512)(128)(4,1)S(1)}, pred[2]{0:T(512)(128)(4,1)}, u32[]{:S(2)}) copy-start(pred[2]{0:T(512)(128)(4,1)} %iota_compare_fusion.4) | copy-start | bytes 10
  1072.1 24.4 %copy-start.12 = (bf16[130,1536]{1,0:T(8,128)(2,1)S(1)}, bf16[130,1536]{1,0:T(8,128)(2,1)}, u32[]{:S(2)}) copy-start(bf16[130,1536]{1,0:T(8,128)(2,1)} %copy-done.11) | copy-start | bytes 1198084
  1072.1 24.4 %copy-start.75 = (f32[1536]{0:T(1024)S(1)}, f32[1536]{0:T(1024)}, u32[]{:S(2)}) copy-start(f32[1536]{0:T(1024)} %copy-done.74) | copy-start | bytes 18436
  1072.1 24.4 %copy-start.94 = (f32[130]{0:T(256)S(1)}, f32[130]{0:T(256)}, u32[]{:S(2)}) copy-start(f32[130]{0:T(256)} %copy-done.93) | copy-start | bytes 1564
  1072.1 24.5 %copy-start.106 = (f32[130]{0:T(256)S(1)}, f32[130]{0:T(256)}, u32[]{:S(2)}) copy-start(f32[130]{0:T(256)} %copy-done.105) | copy-start | bytes 1564
  1072.1 24.9 %copy-start.110 = (f32[130]{0:T(256)S(1)}, f32[130]{0:T(256)}, u32[]{:S(2)}) copy-start(f32[130]{0:T(256)} %copy-done.109) | copy-start | bytes 1564
  1097.0 127.9 %copy-start.73 = (f32[1,12160]{1,0:T(1,128)S(1)}, f32[1,12160]{1,0:T(1,128)}, u32[]{:S(2)}) copy-start(f32[1,12160]{1,0:T(1,128)} %param.27) | copy-start | bytes 145924
  1098.3 126.6 %copy-start.85 = (f32[1,12160]{1,0:T(1,128)S(1)}, f32[1,12160]{1,0:T(1,128)}, u32[]{:S(2)}) copy-start(f32[1,12160]{1,0:T(1,128)} %param.28) | copy-start | bytes 145924
  1098.3 126.6 %copy-start.86 = (f32[1,12160]{1,0:T(1,128)S(1)}, f32[1,12160]{1,0:T(1,128)}, u32[]{:S(2)}) copy-start(f32[1,12160]{1,0:T(1,128)} %param.29) | copy-start | bytes 145924
  1098.3 128.5 %copy-start.70 = (f32[11,1536]{1,0:T(8,128)S(1)}, f32[11,1536]{1,0:T(8,128)}, u32[]{:S(2)}) copy-start(f32[11,1536]{1,0:T(8,128)} %param.30) | copy-start | bytes 202756
  1098.3 128.5 %copy-start.76 = (f32[11,1536]{1,0:T(8,128)S(1)}, f32[11,1536]{1,0:T(8,128)}, u32[]{:S(2)}) copy-start(f32[11,1536]{1,0:T(8,128)} %param.31) | copy-start | bytes 202756
  1098.3 128.5 %copy-start.77 = (f32[11,1536]{1,0:T(8,128)S(1)}, f32[11,1536]{1,0:T(8,128)}, u32[]{:S(2)}) copy-start(f32[11,1536]{1,0:T(8,128)} %param.32) | copy-start | bytes 202756
  1099.8 129.7 %copy-start.1 = (f32[16,6,1536]{2,0,1:T(8,128)S(1)}, f32[16,6,1536]{2,0,1:T(8,128)}, u32[]{:S(2)}) copy-start(f32[16,6,1536]{2,0,1:T(8,128)} %param.23) | copy-start | bytes 1769476
  1101.2 127.3 %collective-permute-start.23 = (f32[130,1536]{1,0:T(8,128)S(1)}, f32[130,1536]{1,0:T(8,128)S(1)}, u32[]{:S(2)}, u32[]{:S(2)}) collective-permute-start(f32[130,1536]{1,0:T(8,128)S(1)} %add_add_fusion.3), channel_id=1, source_target_pairs={{1,8},{3,10},{5,12},{7,14},{8,1},{10,3},{12,5},{14,7},{17,24},{19,... | collective-permute-start | bytes 2396168 | tf_op jit(solution)/shard_map/ppermute | solution.py:214
  (84 other events, 298.3 us)
Sparse Core Ops, SparseCore 0:
  1099.9 124.9 all-reduce.16

commit v2 on v1

--- a/solution.py
+++ b/solution.py
@@ -384,34 +384,33 @@
     return everyone.reshape((-1,) + scaled.shape[1:])
 
 
-def add_rows(*refs):
-    *terms, total = refs
-    slots, count, width = total.shape
-    spec = pl.BlockSpec((1, count, width), lambda i: (i, 0, 0))
-
-    def add(*blocks):
-        *parts, result = blocks
-        acc = parts[0][...].astype(jnp.float32)
-        for one in parts[1:]:
-            acc = acc + one[...].astype(jnp.float32)
-        result[...] = acc.astype(result.dtype)
-
-    pltpu.emit_pipeline(
-        add, grid=(slots,), in_specs=[spec] * len(terms), out_specs=[spec]
-    )(*terms, total)
+def toggled(z, y, x, flip_y, flip_x, k):
+    high = (z // 2 + k // 2) % 2
+    low_bit = (z % 2 + k % 2) % 2
+    return (2 * high + low_bit) * 4 + 2 * ((y + flip_y) % 2) + (x + flip_x) % 2
 
 
 def reduce_kernel(
-    grads, final, from_sib, chip_sum, from_x, from_y, corner_a, corner_b,
-    sib_s, sib_r, x_s, x_r, y_s, y_r, ca_s, ca_r, cb_s, cb_r, f_s, f_r,
+    kind, block, left, right, vec_in,
+    final, vec_out, to_sib, from_sib, chip_sum, from_x, from_y, corner_a, corner_b,
+    vec_box, sib_s, sib_r, x_s, x_r, y_s, y_r, ca_s, ca_r, cb_s, cb_r, f_s, f_r, v_s, v_r,
 ):
     chip, core, z, y, x = place_of()
     rank = z % 2
-    half = grads.shape[2] // 2
+    slots, width, lanes = final.shape[1:]
+    half = width // 2
     part = half // 2
-    at_x = column_of(z, y, 1 - x, 0)
-    at_y = column_of(z, 1 - y, x, 0)
+    at_x = toggled(z, y, x, 0, 1, 0)
+    at_y = toggled(z, y, x, 1, 0, 0)
     greet(chip, core, z, y, x)
+    sibling = (chip, 1 - core)
+    mates = (
+        sibling,
+        (at_x, core),
+        (at_y, core),
+        (toggled(z, y, x, 0, 0, 1), core),
+        (toggled(z, y, x, 0, 0, 2), core),
+    )
 
     def remote(src, dst, send, recv, device):
         return pltpu.make_async_remote_copy(
@@ -419,152 +418,205 @@
             device_id=device, device_id_type=MESH,
         )
 
-    columns = ((1 - y, 1 - x), (y, 1 - x), (1 - y, x), (y, x))
-    order = (3, 2, 1, 0)
+    def unit_of(q, k):
+        return toggled(z, y, x, 1 - q % 2, 1 - q // 2, k)
+
+    def sums(q, k, first, count, terms, total):
+        base = unit_of(q, k) * slots
+        spec = pl.BlockSpec((1, count, lanes), lambda i: (i, 0, 0))
+
+        def add(*refs):
+            *parts, result = refs
+            slot = base + pl.program_id(0)
+            rows = pl.ds(pl.multiple_of(first, 128), count)
+            acc = jnp.dot(
+                left[kind[slot], rows, :], right[block[slot]], preferred_element_type=jnp.float32
+            )
+            for one in parts:
+                acc = acc + one[0].astype(jnp.float32)
+            result[0] = acc.astype(result.dtype)
+
+        pltpu.emit_pipeline(
+            add, grid=(slots,), in_specs=[spec] * len(terms), out_specs=[spec]
+        )(*terms, total)
+
+    mine, other = core * half, (1 - core) * half
 
     def sib_copy(q, k):
-        unit = column_of(z, *columns[q], k)
-        src = grads.at[unit, :, pl.ds(pl.multiple_of((1 - core) * half, 16), half), :]
         i = 4 * q + k
-        return remote(src, from_sib.at[i], sib_s.at[i], sib_r.at[i], (chip, 1 - core))
-
-    sent = []
-
-    def start_sib(q, k):
-        copy = sib_copy(q, k)
-        copy.start()
-        sent.append(copy)
-
-    for k in order:
-        for q in range(4):
-            start_sib(q, k)
-
-    def mine(q, k):
-        unit = column_of(z, *columns[q], k)
-        return grads.at[unit, :, pl.ds(pl.multiple_of(core * half, 16), half), :]
+        return remote(to_sib.at[i], from_sib.at[i], sib_s.at[i], sib_r.at[i], sibling)
 
     def sub(ref, first):
         return ref.at[:, pl.ds(first, part), :]
 
-    def own_sub(q, k, first):
-        unit = column_of(z, *columns[q], k)
-        return grads.at[
-            unit, :, pl.ds(pl.multiple_of(core * half + first, 16), part), :
-        ]
+    def a_copy(k):
+        return remote(sub(chip_sum.at[k], 0), corner_a.at[k], ca_s.at[k], ca_r.at[k], (at_x, core))
+
+    def b_copy(k):
+        return remote(sub(chip_sum.at[k], part), corner_b.at[k], cb_s.at[k], cb_r.at[k], (at_y, core))
+
+    def x_copy(k):
+        return remote(chip_sum.at[4 + k], from_x.at[k], x_s.at[k], x_r.at[k], (at_x, core))
+
+    def y_copy(k):
+        return remote(chip_sum.at[8 + k], from_y.at[k], y_s.at[k], y_r.at[k], (at_y, core))
+
+    def f_copy(k):
+        dst = final.at[z // 2, :, pl.ds(pl.multiple_of(mine, 128), half), :]
+        recv = f_r.at[2 * (z // 2) + core]
+        return remote(
+            chip_sum.at[12 + k], dst, f_s.at[k], recv, (toggled(z, y, x, 0, 0, k), rank)
+        ), pltpu.make_async_copy(chip_sum.at[12 + k], dst, recv)
+
+    def stays(k):
+        return jnp.logical_and(k == 0, rank == core)
+
+    def for_sibling(k):
+        def one(q, carry):
+            sums(q, k, other, half, (), to_sib.at[4 * q + k])
+            sib_copy(q, k).start()
+            return carry
+
+        lax.fori_loop(0, 4, one, 0)
 
     def corner(k):
-        i = k
         sib_copy(0, k).wait_recv()
-        add_rows(mine(0, k), from_sib.at[i], chip_sum.at[i])
-        a = remote(sub(chip_sum.at[i], 0), corner_a.at[k], ca_s.at[k], ca_r.at[k], (at_x, core))
-        b = remote(sub(chip_sum.at[i], part), corner_b.at[k], cb_s.at[k], cb_r.at[k], (at_y, core))
-        a.start()
-        b.start()
-        sent.extend([a, b])
+        sums(0, k, mine, half, (from_sib.at[k],), chip_sum.at[k])
+        a_copy(k).start()
+        b_copy(k).start()
 
     def sides(k):
         ix, iy = 4 + k, 8 + k
         sib_copy(1, k).wait_recv()
         sib_copy(2, k).wait_recv()
-        add_rows(own_sub(1, k, 0), sub(from_sib.at[ix], 0), sub(chip_sum.at[ix], 0))
-        add_rows(own_sub(2, k, part), sub(from_sib.at[iy], part), sub(chip_sum.at[iy], part))
-        remote(
-            sub(chip_sum.at[k], part), corner_b.at[k], cb_s.at[k], cb_r.at[k], (at_y, core)
-        ).wait_recv()
-        add_rows(
-            own_sub(1, k, part), sub(from_sib.at[ix], part), corner_b.at[k],
+        sums(1, k, mine, part, (sub(from_sib.at[ix], 0),), sub(chip_sum.at[ix], 0))
+        sums(2, k, mine + part, part, (sub(from_sib.at[iy], part),), sub(chip_sum.at[iy], part))
+        b_copy(k).wait_recv()
+        sums(
+            1, k, mine + part, part, (sub(from_sib.at[ix], part), corner_b.at[k]),
             sub(chip_sum.at[ix], part),
         )
-        to_x = remote(chip_sum.at[ix], from_x.at[k], x_s.at[k], x_r.at[k], (at_x, core))
-        to_x.start()
-        remote(
-            sub(chip_sum.at[k], 0), corner_a.at[k], ca_s.at[k], ca_r.at[k], (at_x, core)
-        ).wait_recv()
-        add_rows(
-            own_sub(2, k, 0), sub(from_sib.at[iy], 0), corner_a.at[k], sub(chip_sum.at[iy], 0)
+        x_copy(k).start()
+        a_copy(k).wait_recv()
+        sums(
+            2, k, mine, part, (sub(from_sib.at[iy], 0), corner_a.at[k]), sub(chip_sum.at[iy], 0)
         )
-        to_y = remote(chip_sum.at[iy], from_y.at[k], y_s.at[k], y_r.at[k], (at_y, core))
-        to_y.start()
-        sent.extend([to_x, to_y])
-
-    finals = []
+        y_copy(k).start()
 
     def centre(k):
-        i = 12 + k
         sib_copy(3, k).wait_recv()
-        remote(chip_sum.at[4 + k], from_x.at[k], x_s.at[k], x_r.at[k], (at_x, core)).wait_recv()
-        remote(chip_sum.at[8 + k], from_y.at[k], y_s.at[k], y_r.at[k], (at_y, core)).wait_recv()
-        add_rows(mine(3, k), from_sib.at[i], from_x.at[k], from_y.at[k], chip_sum.at[i])
-        target = column_of(z, y, x, k)
-        dst = final.at[z // 2, :, pl.ds(pl.multiple_of(core * half, 16), half), :]
-        recv = f_r.at[2 * (z // 2) + core]
-        go = remote(chip_sum.at[i], dst, f_s.at[k], recv, (target, rank))
-        if k == 0:
-            stays = rank == core
-            here = pltpu.make_async_copy(chip_sum.at[i], dst, recv)
-
-            @pl.when(stays)
+        x_copy(k).wait_recv()
+        y_copy(k).wait_recv()
+        sums(
+            3, k, mine, half, (from_sib.at[12 + k], from_x.at[k], from_y.at[k]),
+            chip_sum.at[12 + k],
+        )
+        go, here = f_copy(k)
+
+        @pl.when(stays(k))
+        def _():
+            here.start()
+
+        @pl.when(jnp.logical_not(stays(k)))
+        def _():
+            go.start()
+
+    def vec_copy(i):
+        return remote(vec_out, vec_box.at[i], v_s.at[i], v_r.at[i], mates[i])
+
+    vec_out[...] = vec_in[...]
+
+    def turn(step, carry):
+        for i in range(5):
+
+            @pl.when(step == i)
             def _():
-                here.start()
-
-            @pl.when(jnp.logical_not(stays))
+                vec_copy(i).start()
+
+        @pl.when(step < 4)
+        def _():
+            for_sibling(3 - step)
+            corner(3 - step)
+
+        @pl.when(jnp.logical_and(step >= 1, step < 5))
+        def _():
+            sides(4 - step)
+
+        @pl.when(step >= 2)
+        def _():
+            centre(5 - step)
+
+        for i in range(5):
+
+            @pl.when(step == i)
             def _():
-                go.start()
-
-            finals.append((go, stays))
-        else:
-            go.start()
-            sent.append(go)
-
-    for step in range(6):
-        if step < 4:
-            corner(order[step])
-        if 1 <= step < 5:
-            sides(order[step - 1])
-        if step >= 2:
-            centre(order[step - 2])
-    for copy in sent:
-        copy.wait_send()
-    for go, stays in finals:
-
-        @pl.when(jnp.logical_not(stays))
+                vec_copy(i).wait()
+                vec_out[...] = vec_out[...] + vec_box[i]
+
+        return carry
+
+    lax.fori_loop(0, 6, turn, 0)
+
+    def settle(k, carry):
+        for q in range(4):
+            sib_copy(q, k).wait_send()
+        a_copy(k).wait_send()
+        b_copy(k).wait_send()
+        x_copy(k).wait_send()
+        y_copy(k).wait_send()
+
+        @pl.when(jnp.logical_not(stays(k)))
         def _():
-            go.wait_send()
-
+            f_copy(k)[0].wait_send()
+
+        return carry
+
+    lax.fori_loop(0, 4, settle, 0)
     for plane in range(2):
         for h in range(2):
             piece = final.at[plane, :, pl.ds(h * half, half), :]
             pltpu.make_async_copy(piece, piece, f_r.at[2 * plane + h]).wait()
 
 
-def reduce_slots(grads, slot_count):
+def reduce_slots(holder, kinds, rows, columns, vector, slot_count):
     if not chip_pairs():
+        grads = slot_grads(holder, kinds, rows, columns)
         total = lax.psum_scatter(grads, "dp", scatter_dimension=0, tiled=True)
-        return total, None
-    width = grads.shape[1:]
-    half = width[0] // 2
+        return [total], lax.psum(vector, ("dp", "tensor"))
+    depth = max(r.shape[0] for r in rows)
+    left = jnp.stack([jnp.pad(r, ((0, depth - r.shape[0]), (0, 0))).T for r in rows])
+    lanes = columns[0].shape[2]
+    right = [
+        jnp.pad(c.transpose(1, 0, 2), ((0, 0), (0, depth - c.shape[0]), (0, 0))) for c in columns
+    ]
+    right = jnp.concatenate(right + [jnp.zeros((1, depth, lanes), right[0].dtype)], 0)
+    block = jnp.where(holder >= 0, holder, right.shape[0] - 1)
+    kind = kinds[jnp.maximum(holder, 0)]
+    width = rows[0].shape[1]
+    half = width // 2
     dma = pltpu.SemaphoreType.DMA
-    units = grads.reshape((16, slot_count) + width)
-
-    def room(count, rows):
-        return jax.ShapeDtypeStruct((count, slot_count, rows, width[1]), grads.dtype)
-
-    counts = (16, 16) + (4,) * 12
+    scalars = pl.BlockSpec(memory_space=pltpu.SMEM)
+    inside = pl.BlockSpec(memory_space=pltpu.VMEM)
+
+    def room(count, tall):
+        return jax.ShapeDtypeStruct((count, slot_count, tall, lanes), jnp.bfloat16)
+
     outs = pl.pallas_call(
         reduce_kernel,
         out_shape=[
-            jax.ShapeDtypeStruct((2, slot_count) + width, grads.dtype),
-            room(16, half), room(16, half), room(4, half), room(4, half),
+            room(2, width), jax.ShapeDtypeStruct(vector.shape, vector.dtype),
+            room(16, half), room(16, half), room(16, half), room(4, half), room(4, half),
             room(4, half // 2), room(4, half // 2),
         ],
-        in_specs=[ANY],
-        out_specs=[ANY] * 7,
-        scratch_shapes=[dma((n,)) for n in counts[:12]],
+        in_specs=[scalars, scalars, inside, inside, inside],
+        out_specs=[ANY, inside] + [ANY] * 7,
+        scratch_shapes=[pltpu.VMEM((5,) + vector.shape, vector.dtype)]
+        + [dma((n,)) for n in (16, 16) + (4,) * 10 + (5, 5)],
         compiler_params=pltpu.CompilerParams(
-            collective_id=1, has_side_effects=True, vmem_limit_bytes=16 * MIB
+            collective_id=1, has_side_effects=True, vmem_limit_bytes=56 * MIB
         ),
-    )(units)
-    return outs[0][0], outs[0][1]
+    )(kind, block, left, right, vector)
+    return [outs[0][0], outs[0][1]], outs[1]
 
 
 def pick_blocks(everyone, places):
@@ -643,9 +695,8 @@
     )(kind, block, used, left, right)
 
 
-def adam_slots(first_part, second_part, master, moment_one, moment_two, slot_scale, filled):
+def adam_slots(parts, master, moment_one, moment_two, slot_scale, filled):
     slot_count, width, lanes = master.shape[1:]
-    parts = [first_part] if second_part is None else [first_part, second_part]
     count = len(parts)
     tall = width // 2
 
@@ -889,27 +940,6 @@
         grad_norm
     )
     grad_input = grad_res + d_inputs
-    grads = slot_grads(
-        holder,
-        kind_of_blocks(tile_count, heads_here, blocks_here),
-        (rows_one, rows_grad, rows_two, context, rows_grad_two, rows_three, rows_grad_three),
-        (
-            query_grad,
-            key_grad,
-            value_grad,
-            heads_out,
-            cross_query_grad,
-            cross_key_grad,
-            cross_value_grad,
-            cross_heads_out,
-            d_hidden_low,
-            hidden_low,
-        ),
-    )
-    first_part, second_part = reduce_slots(grads, slot_count)
-    new_master, new_first, new_second = adam_slots(
-        first_part, second_part, master, first_moment, second_moment, slot_scale, filled
-    )
     head_grad = jnp.concatenate(
         [
             d_bias_query.reshape(-1),
@@ -942,7 +972,34 @@
             d_gate_ffn,
         ]
     )
-    head_total, shared_total = lax.psum((head_padded, shared_grad), ("dp", "tensor"))
+    vector = jnp.concatenate([head_padded.reshape(-1), shared_grad.reshape(-1)])
+    vector = jnp.pad(vector, (0, -vector.shape[0] % 1024)).reshape(-1, 128)
+    parts, vector = reduce_slots(
+        holder,
+        kind_of_blocks(tile_count, heads_here, blocks_here),
+        (rows_one, rows_grad, rows_two, context, rows_grad_two, rows_three, rows_grad_three),
+        (
+            query_grad,
+            key_grad,
+            value_grad,
+            heads_out,
+            cross_query_grad,
+            cross_key_grad,
+            cross_value_grad,
+            cross_heads_out,
+            d_hidden_low,
+            hidden_low,
+        ),
+        vector,
+        slot_count,
+    )
+    new_master, new_first, new_second = adam_slots(
+        parts, master, first_moment, second_moment, slot_scale, filled
+    )
+    vector = vector.reshape(-1)
+    head_total = vector[: head_padded.size].reshape(head_padded.shape)
+    shared_total = vector[head_padded.size : head_padded.size + shared_grad.size]
+    shared_total = shared_total.reshape(shared_grad.shape)
     mine_head = lax.dynamic_slice_in_dim(head_total, tensor_rank, 1, 0)
     new_head, new_head_first, new_head_second = adam_step(
         head_params, mine_head, head_first, head_second, VECTOR_RATE, 0.0

time: 1260 us -> 1250 us (level)
  waiting for transfers between devices: 216 us -> 49.5 us
  local copies, waits for them, and re-layouts: 69.8 us -> 188 us
  other arithmetic: 54.9 us -> 115 us
  Pallas kernels: 758 us -> 732 us
  between operations: 17.6 us -> 4.54 us
    psum x1 -> x0, waiting for transfers between devices: 123 us -> none  [body(): lax.psum((head_padded, shared_grad), ('dp', 'tensor'))]
    ppermute x16, waiting for transfers between devices: 93.2 us -> 49.5 us  [pair_swap(): return lax.ppermute(value, 'dp', [(i, i ^ 4) for i in range(16)])]
    unnamed x270 -> x386, local copies, waits for them, and re-layouts: 22.9 us -> 59 us
    ppermute x0 -> x16, local copies, waits for them, and re-layouts: none -> 27.6 us  [the longest x12 21.3 us: pair_swap(): return lax.ppermute(value, 'dp', [(i, i ^ 4) for i in range(16)])]
    pallas_call x2 -> x1, Pallas kernels: 412 us -> 387 us  [reduce_slots(): pl.pallas_call(reduce_kernel, out_shape=[room(2, width), jax.ShapeDtypeSt...]
  transfers between devices with their start and end apart: 25 -> 24, of which waited for: 13 -> 8; matrix products, arithmetic and copies ran while one was open for 7% -> 14% of each run, Pallas kernels for 61% -> 60%
where the time goes in v2:
time: 1250 us; the launch traced here: 1220 us
  Pallas kernels  732 us (59%)
  local copies, waits for them, and re-layouts  188 us (15%)
  other arithmetic  115 us (9%)
  matrix products  105 us (8%)
  waiting for transfers between devices  49.5 us (4%)
  starting transfers between devices  28.7 us (2%)
    pallas_call x1, Pallas kernels, reduce_slots(): pl.pallas_call(reduce_kernel, out_shape=[room(2, width), jax.ShapeDtypeSt...  387 us
    pallas_call x1, Pallas kernels, gather_slots(): pl.pallas_call(gather_kernel, out_shape=jax.ShapeDtypeStruct((16,) + scal...  247 us
    dot_general x30, matrix products, product(): return jnp.einsum(form, left, right, preferred_element_type=jnp.float32)  105 us
    pallas_call x1, Pallas kernels, pick_blocks(): pl.pallas_call(copy, grid_spec=pltpu.PrefetchScalarGridSpec(num_scalar_pr...  73.2 us
    unnamed x386, local copies, waits for them, and re-layouts  59 us
    ppermute x16, waiting for transfers between devices, pair_swap(): return lax.ppermute(value, 'dp', [(i, i ^ 4) for i in range(16)])  49.5 us
  transfers between devices with their start and end apart: 24, of which 8 were waited for; matrix products, arithmetic and copies ran while one was open for 14% of the time, Pallas kernels for 60%

profile of v2, /device:TPU:9, one launch (start us, length us, event | category | flops | bytes accessed | tf_op | source)
XLA Modules:
  0.0 1222.8 jit_solution(2181976124783915095)
XLA Ops:
  9.8 3.7 fusion.8.own
  13.5 247.3 %shard_map.248 = bf16[16,9,1536,128]{3,2,1,0:T(8,128)(2,1)} custom-call(bf16[9,1536,128]{2,1,0:T(8,128)(2,1)S(1)} %fusion.8.own), custom_call_target="tpu_custom_call" | custom-call | tf_op jit(solution)/shard_map/pallas_call | solution.py:374
  260.9 73.2 %shard_map.249 = bf16[118,1536,128]{2,1,0:T(8,128)(2,1)} custom-call(s32[118]{0:T(128)} %copy-done.174, bf16[144,1536,128]{2,1,0:T(8,128)(2,1)} %bitcast.301), custom_call_target="tpu_custom_call" | custom-call | tf_op jit(solution)/shard_map/pallas_call | solution.py:629
  341.7 9.8 collective-permute-done.2
  352.7 3.1 multiply_reduce_fusion.17
  355.8 2.9 multiply_reduce_fusion.18
  359.2 3.3 fusion.125
  364.1 2.9 reshape.382
  367.0 3.0 slice_negate_fusion.2
  372.2 3.1 reshape.383
  380.6 2.9 reshape.380
  383.4 3.0 slice_negate_fusion.3
  388.6 3.0 reshape.381
  399.0 2.7 convolution_bitcast_fusion.5
  410.3 2.7 collective-permute-done.6
  419.8 4.9 multiply_reduce_fusion.10
  424.7 15.8 %collective-permute-done.8 = bf16[130,1536]{1,0:T(8,128)(2,1)} collective-permute-done((bf16[130,1536]{1,0:T(8,128)(2,1)S(1)}, bf16[130,1536]{1,0:T(8,128)(2,1)}, u32[]{:S(2)}, u32[]{:S(2)}) %collective-permute-start.8) | collective-permute-done | bytes 399392 | tf_op jit(solution)/shard_map/ppermute | solution.py:191
  442.6 3.1 multiply_reduce_fusion.16
  445.8 3.1 collective-permute-start.9
  448.9 3.2 add_convert_fusion.3
  455.0 2.6 convolution_bitcast_fusion.4
  464.9 2.8 copy.355
  467.7 3.0 collective-permute-done.10
  486.2 4.2 collective-permute-done.11
  492.5 2.9 maximum_select_fusion.2
  495.4 11.6 fusion.6
  506.9 10.5 fusion.29
  527.5 2.8 copy.356
  532.5 4.4 fusion.73
  543.9 7.7 collective-permute-done.15
  553.7 2.8 maximum_select_fusion.3
  556.5 14.2 %convert_reduce_fusion = (f32[35,128]{1,0:T(8,128)}, bf16[260,35,128]{2,0,1:T(8,128)(2,1)S(1)}, f32[260,35,128]{2,0,1:T(8,128)}) fusion(f32[260,35,128]{2,0,1:T(8,128)} %fusion.6, f32[35,128]{1,0:T(8,128)S(1)} %bitcast.323, bf16[118,1536,128]{2,1,0:T(8,128)(2,1)} %shard_map.249, bf16[260,1536]{0,1:T(8,128)(2,1)S(1)} %maximum_select_fusion.3), kind=kOutput, calls=%fused_computation.41 | convolution fusion | flops 3609710592 | bytes 26316800 | tf_op jit(solution)/shard_map/td,fde->tfe/dot_general | solution.py:29
  570.7 7.3 fusion.26
  587.9 2.8 copy.357
  592.9 3.7 multiply_reduce_fusion.4
  602.2 5.0 collective-permute-start.17
  607.2 8.7 multiply_convert_fusion
  620.3 2.8 maximum_select_fusion.4
  623.1 3.0 fusion.94
  650.0 2.8 copy.358
  655.4 3.5 collective-permute-done.19
  661.1 2.7 multiply_reduce_fusion.7
  666.4 3.3 multiply_reduce_fusion.5
  676.5 3.1 fusion.78
  682.0 2.9 collective-permute-done.20
  687.1 2.9 maximum_select_fusion.5
  689.9 2.7 fusion.91
  711.0 2.9 reshape.384
  713.9 3.0 slice_negate_fusion.1
  719.1 3.2 reshape.385
  727.3 2.9 reshape.386
  730.1 3.0 slice_negate_fusion
  735.4 3.0 reshape.387
  740.9 3.1 multiply_reduce_fusion.13
  748.1 2.8 convolution_bitcast_fusion.1
  750.9 3.7 fusion.32
  754.6 3.1 copy.317
  757.7 4.0 fusion.25
  779.9 2.9 pad_dynamic-update-slice_fusion.1
  782.8 2.9 pad_dynamic-update-slice_fusion
  795.0 387.2 %shard_map.250 = (bf16[2,9,1536,128]{3,2,1,0:T(8,128)(2,1)}, f32[328,128]{1,0:T(8,128)}, bf16[16,9,768,128]{3,2,1,0:T(8,128)(2,1)}, bf16[16,9,768,128]{3,2,1,0:T...) custom-call(s32[144]{0:T(256)} %gather_fusion.1, ...), custom_call_target="tpu_custom_call" | custom-call | tf_op jit(solution)/shard_map/pallas_call | solution.py:604
  1184.1 6.6 slice_bitcast_fusion
  1191.6 24.1 %shard_map.251 = (f32[1,9,1536,128]{3,2,1,0:T(8,128)}, f32[1,9,1536,128]{3,2,1,0:T(8,128)}, f32[1,9,1536,128]{3,2,1,0:T(8,128)}) custom-call(f32[9]{0:T(128)} %copy-done.166, s32[9]{0:T(128)} %compare_convert_fusion.fill_ref, bf16[9,1536,128]{2,1,0:T(8,128)(2,1)} %get-tuple-element.154.refs_0_, bf16[9,1536,128]{2,1,0:T(8,128)(2,1)} %get-tuple-element.153.refs_1_, ...), custom_call_target="tpu_custom_call" | custom-call | tf_op jit(solution)/shard_map/pallas_call | solution.py:728
  1219.5 2.7 copy.326
  (607 shorter events, 234.1 us)
Async XLA Ops:
  0.6 334.1 %copy-start = (f32[16,6,1536]{2,0,1:T(8,128)S(1)}, f32[16,6,1536]{2,0,1:T(8,128)}, u32[]{:S(2)}) copy-start(f32[16,6,1536]{2,0,1:T(8,128)} %param.23) | copy-start | bytes 1769476
  0.7 333.5 %collective-permute-start.1 = (s32[1]{0:T(128)}, s32[1]{0:T(128)}, u32[]{:S(2)}, u32[]{:S(2)}) collective-permute-start(s32[1]{0:T(128)} %param.21), channel_id=1, source_target_pairs={{1,8},{3,10},{5,12},{7,14},{8,1},{10,3},{12,5},{14,7},{17,24},{19,... | collective-permute-start | bytes 20 | tf_op jit(solution)/shard_map/ppermute | solution.py:214
  2.0 333.8 %collective-permute-start.5 = (s32[3,260]{1,0:T(4,128)}, s32[3,260]{1,0:T(4,128)S(1)}, u32[]{:S(2)}, u32[]{:S(2)}) collective-permute-start(s32[3,260]{1,0:T(4,128)} %param.20), channel_id=1, source_target_pairs={{1,8},{3,10},{5,12},{7,14},{8,1},{10,3},{12,5},{14,7},{17,24},{19,... | collective-permute-start | bytes 9368 | tf_op jit(solution)/shard_map/ppermute | solution.py:214
  2.7 338.3 %collective-permute-start.3 = (f32[1,12160]{1,0:T(1,128)}, f32[1,12160]{1,0:T(1,128)}, u32[]{:S(2)}, u32[]{:S(2)}) collective-permute-start(f32[1,12160]{1,0:T(1,128)} %param.27), channel_id=1, source_target_pairs={{1,8},{3,10},{5,12},{7,14},{8,1},{10,3},{12,5},{14,7},{17,24},{19,... | collective-permute-start | bytes 145928 | tf_op jit(solution)/shard_map/ppermute | solution.py:214
  3.9 334.4 %collective-permute-start = (bf16[130,1536]{1,0:T(8,128)(2,1)}, bf16[130,1536]{1,0:T(8,128)(2,1)S(1)}, u32[]{:S(2)}, u32[]{:S(2)}) collective-permute-start(bf16[130,1536]{1,0:T(8,128)(2,1)} %param.17), channel_id=1, source_target_pairs={{1,8},{3,10},{5,12},{7,14},{8,1},{10,3},{12,5},{14,7},{17,24},{19,... | collective-permute-start | bytes 1198088 | tf_op jit(solution)/shard_map/ppermute | solution.py:214
  260.9 74.2 %copy-start.75 = (f32[11,1536]{1,0:T(8,128)S(1)}, f32[11,1536]{1,0:T(8,128)}, u32[]{:S(2)}) copy-start(f32[11,1536]{1,0:T(8,128)} %param.30) | copy-start | bytes 202756
  260.9 74.9 %copy-start.165 = (s32[3,260]{1,0:T(4,128)S(1)}, s32[3,260]{1,0:T(4,128)}, u32[]{:S(2)}) copy-start(s32[3,260]{1,0:T(4,128)} %param.20) | copy-start | bytes 9364
  338.9 75.3 %copy-start.11 = (bf16[130,1536]{0,1:T(8,128)(2,1)}, bf16[130,1536]{0,1:T(8,128)(2,1)S(1)}, u32[]{:S(2)}) copy-start(bf16[130,1536]{0,1:T(8,128)(2,1)S(1)} %get-tuple-element.152) | copy-start | bytes 1198084
  340.6 10.9 collective-permute-start.2
  341.0 11.6 copy-start.81
  341.7 52.4 %copy-start.85 = (f32[768]{0:T(1024)}, f32[768]{0:T(1024)S(1)}, u32[]{:S(2)}) copy-start(f32[768]{0:T(1024)S(1)} %get-tuple-element.109) | copy-start | bytes 9220
  341.7 52.4 %copy-start.87 = (f32[768]{0:T(1024)}, f32[768]{0:T(1024)S(1)}, u32[]{:S(2)}) copy-start(f32[768]{0:T(1024)S(1)} %get-tuple-element.110) | copy-start | bytes 9220
  352.7 6.5 copy-start.44
  355.8 38.4 %copy-start.24 = (f32[260,6,128]{2,0,1:T(8,128)}, f32[260,6,128]{2,0,1:T(8,128)S(1)}, u32[]{:S(2)}) copy-start(f32[260,6,128]{2,0,1:T(8,128)S(1)} %get-tuple-element.183) | copy-start | bytes 2396164
  358.7 35.4 %copy-start.26 = (f32[260,6,128]{2,0,1:T(8,128)}, f32[260,6,128]{2,0,1:T(8,128)S(1)}, u32[]{:S(2)}) copy-start(f32[260,6,128]{2,0,1:T(8,128)S(1)} %get-tuple-element.185) | copy-start | bytes 2396164
  358.8 3.7 collective-permute-start.4
  362.6 31.5 %copy-start.105 = (f32[260]{0:T(512)}, f32[260]{0:T(512)S(1)}, u32[]{:S(2)}) copy-start(f32[260]{0:T(512)S(1)} %get-tuple-element.175) | copy-start | bytes 3124
  362.6 31.5 %copy-start.107 = (f32[260]{0:T(512)}, f32[260]{0:T(512)S(1)}, u32[]{:S(2)}) copy-start(f32[260]{0:T(512)S(1)} %get-tuple-element.176) | copy-start | bytes 3124
  403.0 10.0 collective-permute-start.6
  405.6 12.6 %collective-permute-start.7 = (bf16[512,1536]{0,1:T(8,128)(2,1)}, bf16[512,1536]{0,1:T(8,128)(2,1)}, u32[]{:S(2)}, u32[]{:S(2)}) collective-permute-start(bf16[512,1536]{0,1:T(8,128)(2,1)} %copy.273), channel_id=1, source_target_pairs={{1,8},{3,10},{5,12},{7,14},{8,1},{10,3},{12,5},{14,7},{17,24},{19,... | collective-permute-start | bytes 4718600 | tf_op jit(solution)/shard_map/ppermute | solution.py:214
  408.5 5.8 copy-start.102
  408.5 7.0 copy-start.79
  417.1 23.4 %collective-permute-start.8 = (bf16[130,1536]{1,0:T(8,128)(2,1)S(1)}, bf16[130,1536]{1,0:T(8,128)(2,1)}, u32[]{:S(2)}, u32[]{:S(2)}) collective-permute-start(bf16[130,1536]{1,0:T(8,128)(2,1)S(1)} %copy.276), channel_id=1, source_target_pairs={{0,8},{2,10},{4,12},{6,14},{8,0},{10,2},{12,4},{14,6},{16,24},{18,... | collective-permute-start | bytes 1198088 | tf_op jit(solution)/shard_map/ppermute | solution.py:191
  419.8 29.1 %copy-start.39 = (bf16[512,1536]{0,1:T(8,128)(2,1)}, bf16[512,1536]{0,1:T(8,128)(2,1)S(1)}, u32[]{:S(2)}) copy-start(bf16[512,1536]{0,1:T(8,128)(2,1)S(1)} %broadcast_select_fusion) | copy-start | bytes 4718596
  442.6 6.3 copy-start.167
  445.7 6.6 copy-start.14
  445.8 6.4 collective-permute-start.9
  459.0 11.7 collective-permute-start.10
  459.1 64.1 %collective-permute-start.14 = (bf16[130,1536]{1,0:T(8,128)(2,1)}, bf16[130,1536]{1,0:T(8,128)(2,1)}, u32[]{:S(2)}, u32[]{:S(2)}) collective-permute-start(bf16[130,1536]{1,0:T(8,128)(2,1)} %param.19), channel_id=1, source_target_pairs={{1,8},{3,10},{5,12},{7,14},{8,1},{10,3},{12,5},{14,7},{17,24},{19,... | collective-permute-start | bytes 1198088 | tf_op jit(solution)/shard_map/ppermute | solution.py:214
  464.9 7.9 copy-start.119
  479.9 10.4 collective-permute-start.11
  486.2 20.8 %copy-start.98 = (f32[4480]{0:T(1024)}, f32[4480]{0:T(1024)S(1)}, u32[]{:S(2)}) copy-start(f32[4480]{0:T(1024)S(1)} %slice_reduce_fusion) | copy-start | bytes 53764
  495.4 11.6 copy-start.46
  519.4 10.9 collective-permute-start.12
  541.6 9.9 collective-permute-start.15
  556.5 14.2 %copy-start.48 = (bf16[260,1536]{0,1:T(8,128)(2,1)}, bf16[260,1536]{0,1:T(8,128)(2,1)S(1)}, u32[]{:S(2)}) copy-start(bf16[260,1536]{0,1:T(8,128)(2,1)S(1)} %maximum_select_fusion.3) | copy-start | bytes 2396164
  570.7 8.2 copy-start.45
  579.0 11.7 collective-permute-start.16
  583.0 32.9 %collective-permute-start.13 = (bf16[130,1536]{1,0:T(8,128)(2,1)}, bf16[130,1536]{1,0:T(8,128)(2,1)}, u32[]{:S(2)}, u32[]{:S(2)}) collective-permute-start(bf16[130,1536]{1,0:T(8,128)(2,1)} %copy.289), channel_id=1, source_target_pairs={{1,8},{3,10},{5,12},{7,14},{8,1},{10,3},{12,5},{14,7},{17,24},{19,... | collective-permute-start | bytes 1198088 | tf_op jit(solution)/shard_map/ppermute | solution.py:214
  602.2 15.9 %collective-permute-start.17 = (bf16[130,1536]{1,0:T(8,128)(2,1)}, bf16[130,1536]{1,0:T(8,128)(2,1)}, u32[]{:S(2)}, u32[]{:S(2)}) collective-permute-start(bf16[130,1536]{1,0:T(8,128)(2,1)} %copy.299), channel_id=1, source_target_pairs={{0,8},{2,10},{4,12},{6,14},{8,0},{10,2},{12,4},{14,6},{16,24},{18,... | collective-permute-start | bytes 1198088 | tf_op jit(solution)/shard_map/ppermute | solution.py:191
  634.8 7.6 copy-start.118
  634.8 6.8 collective-permute-start.18
  648.1 10.8 collective-permute-start.19
  652.8 8.3 copy-start.80
  652.8 8.3 copy-start.115
  671.0 5.5 copy-start.95
  671.0 5.5 copy-start.116
  674.9 5.9 copy-start.121
  674.9 6.5 copy-start.123
  674.9 10.0 collective-permute-start.20
  676.5 10.6 copy-start.139
  735.3 5.5 copy-start.86
  735.3 5.5 copy-start.88
  735.3 5.5 copy-start.106
  735.3 5.5 copy-start.108
  744.1 3.2 collective-permute-start.21
  766.4 20.0 %collective-permute-start.22 = (bf16[130,1536]{1,0:T(8,128)(2,1)}, bf16[130,1536]{1,0:T(8,128)(2,1)}, u32[]{:S(2)}, u32[]{:S(2)}) collective-permute-start(bf16[130,1536]{1,0:T(8,128)(2,1)} %copy.319), channel_id=1, source_target_pairs={{0,8},{2,10},{4,12},{6,14},{8,0},{10,2},{12,4},{14,6},{16,24},{18,... | collective-permute-start | bytes 1198088 | tf_op jit(solution)/shard_map/ppermute | solution.py:191
  793.6 422.9 %collective-permute-start.23 = (f32[130,1536]{1,0:T(8,128)}, f32[130,1536]{1,0:T(8,128)S(1)}, u32[]{:S(2)}, u32[]{:S(2)}) collective-permute-start(f32[130,1536]{1,0:T(8,128)} %copy.321), channel_id=1, source_target_pairs={{1,8},{3,10},{5,12},{7,14},{8,1},{10,3},{12,5},{14,7},{17,24},{19,... | collective-permute-start | bytes 2396168 | tf_op jit(solution)/shard_map/ppermute | solution.py:214
  795.0 388.1 %copy-start.83 = (f32[1,12160]{1,0:T(1,128)S(1)}, f32[1,12160]{1,0:T(1,128)}, u32[]{:S(2)}) copy-start(f32[1,12160]{1,0:T(1,128)} %param.27) | copy-start | bytes 145924
  795.0 388.1 %copy-start.110 = (f32[1,12160]{1,0:T(1,128)S(1)}, f32[1,12160]{1,0:T(1,128)}, u32[]{:S(2)}) copy-start(f32[1,12160]{1,0:T(1,128)} %param.28) | copy-start | bytes 145924
  795.0 388.1 %copy-start.111 = (f32[1,12160]{1,0:T(1,128)S(1)}, f32[1,12160]{1,0:T(1,128)}, u32[]{:S(2)}) copy-start(f32[1,12160]{1,0:T(1,128)} %param.29) | copy-start | bytes 145924
  1191.6 24.1 %copy-start.76 = (f32[11,1536]{1,0:T(8,128)S(1)}, f32[11,1536]{1,0:T(8,128)}, u32[]{:S(2)}) copy-start(f32[11,1536]{1,0:T(8,128)} %param.30) | copy-start | bytes 202756
  1191.6 24.1 %copy-start.96 = (f32[11,1536]{1,0:T(8,128)S(1)}, f32[11,1536]{1,0:T(8,128)}, u32[]{:S(2)}) copy-start(f32[11,1536]{1,0:T(8,128)} %param.31) | copy-start | bytes 202756
  1191.6 24.1 %copy-start.97 = (f32[11,1536]{1,0:T(8,128)S(1)}, f32[11,1536]{1,0:T(8,128)}, u32[]{:S(2)}) copy-start(f32[11,1536]{1,0:T(8,128)} %param.32) | copy-start | bytes 202756
  (136 other events, 355.5 us)

commit v3 on v2

v3 whole, which is shorter than its diff:
```python
import functools

import jax
import jax.numpy as jnp
from jax import lax
from jax.experimental import pallas as pl
from jax.experimental.pallas import tpu as pltpu
from jax.sharding import PartitionSpec as P

D = 1536
HEADS = 12
HEAD = 128
FF = 8960
TSTEPS = 16
STEPC = 10


NORM_EPS = 1e-06
BETA_ONE = 0.9
BETA_TWO = 0.999
ADAM_EPS = 1e-08
TILE_RATE = 1.0
TILE_DECAY = 0.1
VECTOR_RATE = 0.5
GELU_COEF = 0.7978845608028654


def rope_tables(token_places, head_size):
    sixths = head_size // 6
    frame_pairs = (head_size - 4 * sixths) // 2
    frame_freq = 10000.0 ** (-jnp.arange(frame_pairs, dtype=jnp.float32) / frame_pairs)
    side_freq = 10000.0 ** (-jnp.arange(sixths, dtype=jnp.float32) / sixths)
    spots = token_places.astype(jnp.float32)
    angles = jnp.concatenate(
        [
            spots[0][..., None] * frame_freq,
            spots[1][..., None] * side_freq,
            spots[2][..., None] * side_freq,
        ],
        -1,
    )
    angles = jnp.repeat(angles, 2, axis=-1)
    return (jnp.cos(angles), jnp.sin(angles))


def owner_layout(owners, slot_count, devices):
    indices = jnp.arange(owners.shape[0], dtype=jnp.int32)
    same_owner = (owners[:, None] == owners[None, :]) & (indices[None, :] < indices[:, None])
    slot_of = jnp.sum(same_owner.astype(jnp.int32), axis=1)
    places = owners * slot_count + slot_of
    spots = jnp.arange(slot_count * devices, dtype=jnp.int32)
    holder = (
        jnp.sum(jnp.where(places[None, :] == spots[:, None], indices[None, :] + 1, 0), axis=1) - 1
    )
    return (places, holder)


def tile_scales(tile_count, heads_here, blocks_here):
    indices = jnp.arange(tile_count)
    scale_in = D ** (-0.5)
    scale_out = HEADS ** (-0.5)
    scale_down = FF ** (-0.5)
    scales = jnp.where(
        indices < 3 * heads_here,
        scale_in,
        jnp.where(
            indices < 4 * heads_here,
            scale_out,
            jnp.where(
                indices < 7 * heads_here,
                scale_in,
                jnp.where(
                    indices < 8 * heads_here,
                    scale_out,
                    jnp.where(indices < 8 * heads_here + blocks_here, scale_in, scale_down),
                ),
            ),
        ),
    )
    return scales.astype(jnp.float32)


def adam_step(weight, gradient, moment_one, moment_two, step_rate, decay_rate):
    first_new = BETA_ONE * moment_one + (1.0 - BETA_ONE) * gradient
    second_new = BETA_TWO * moment_two + (1.0 - BETA_TWO) * gradient * gradient
    first_hat = first_new / (1.0 - BETA_ONE**STEPC)
    second_hat = second_new / (1.0 - BETA_TWO**STEPC)
    weight_new = weight - step_rate * (
        first_hat / (jnp.sqrt(second_hat) + ADAM_EPS) + decay_rate * weight
    )
    return (weight_new, first_new, second_new)


MESH = pl.DeviceIdType.MESH
ANY = pl.BlockSpec(memory_space=pl.ANY)
MIB = 1 << 20


def chip_pairs():
    return lax.axis_size("dp") == 16 and lax.axis_size("tensor") == 2


def pair_rank():
    if chip_pairs():
        return (lax.axis_index("dp") // 4) % 2
    return lax.axis_index("tensor")


def pair_swap(value):
    if chip_pairs():
        return lax.ppermute(value, "dp", [(i, i ^ 4) for i in range(16)])
    return lax.ppermute(value, "tensor", [(0, 1), (1, 0)])


def pair_sums(*values):
    stacked = jnp.concatenate([v.reshape(-1) for v in values])
    total = stacked + pair_swap(stacked)
    out, at = [], 0
    for v in values:
        out.append(total[at : at + v.size].reshape(v.shape))
        at += v.size
    return tuple(out)


def home_swap(*values):
    if not chip_pairs():
        return values
    chip, core = lax.axis_index("dp"), lax.axis_index("tensor")
    away = (chip // 4) % 2 != core
    order = [
        (d * 2 + c, (d ^ 4) * 2 + 1 - c) for d in range(16) for c in range(2) if (d // 4) % 2 != c
    ]
    return tuple(
        jnp.where(away, lax.ppermute(v, ("dp", "tensor"), order), v) for v in values
    )


def place_of():
    chip, core = lax.axis_index("dp"), lax.axis_index("tensor")
    z, y, x = chip // 4, (chip // 2) % 2, chip % 2
    return chip, core, z, y, x


def column_of(z, y, x, k):
    high, low_bit = z // 2, z % 2
    if k & 2:
        high = 1 - high
    if k & 1:
        low_bit = 1 - low_bit
    return (2 * high + low_bit) * 4 + 2 * y + x


def greet(chip, core, z, y, x):
    barrier = pltpu.get_barrier_semaphore()
    friends = []
    for k in range(4):
        for flip in (0, 1):
            if k or flip:
                friends.append((column_of(z, y, x, k), core if flip == 0 else 1 - core))
    friends.append((column_of(z, y, 1 - x, 0), core))
    friends.append((column_of(z, 1 - y, x, 0), core))
    for friend in friends:
        pl.semaphore_signal(barrier, inc=1, device_id=friend, device_id_type=MESH)
    pl.semaphore_wait(barrier, len(friends))


def gather_kernel(own, out, near_s, local_s, col_r, x_s, x_r, y_s, y_r, ra_s, ra_r, rb_s, rb_r, sib_s, sib_r):
    chip, core, z, y, x = place_of()
    rank = z % 2
    half = own.shape[1] // 2
    part = half // 2
    at_x = column_of(z, y, 1 - x, 0)
    at_y = column_of(z, 1 - y, x, 0)
    greet(chip, core, z, y, x)

    def rows(ref, unit, first, count):
        return ref.at[unit, :, pl.ds(pl.multiple_of(first, 16), count), :]

    def remote(unit, first, count, send, recv, device):
        piece = rows(out, unit, first, count)
        return pltpu.make_async_remote_copy(
            src_ref=piece, dst_ref=piece, send_sem=send, recv_sem=recv,
            device_id=device, device_id_type=MESH,
        )

    started = []
    for j in range(2):
        zh = z // 2 if j == 0 else 1 - z // 2
        target = (2 * zh + core) * 4 + 2 * y + x
        for h in range(2):
            src = own.at[:, pl.ds(h * half, half), :]
            dst = out.at[chip, :, pl.ds(h * half, half), :]
            go = pltpu.make_async_remote_copy(
                src_ref=src, dst_ref=dst, send_sem=near_s.at[2 * j + h], recv_sem=col_r.at[z],
                device_id=(target, h), device_id_type=MESH,
            )
            if j == 0:
                here = pltpu.make_async_copy(src, dst, col_r.at[z])
                stays = jnp.logical_and(rank == core, core == h)

                @pl.when(stays)
                def _():
                    here.start()

                @pl.when(jnp.logical_not(stays))
                def _():
                    go.start()

                started.append((go, stays))
            else:
                go.start()
                started.append((go, None))

    def column_in(k):
        unit = column_of(z, y, x, k)
        source_z = unit // 4
        piece = rows(out, unit, core * half, half)
        pltpu.make_async_copy(piece, piece, col_r.at[source_z]).wait()
        to_x = remote(unit, core * half, half, x_s.at[k], x_r.at[k], (at_x, core))
        to_y = remote(unit, core * half, half, y_s.at[k], y_r.at[k], (at_y, core))
        to_sib = remote(unit, core * half, half, sib_s.at[k], sib_r.at[k], (chip, 1 - core))
        to_x.start()
        to_y.start()
        to_sib.start()
        return [to_x, to_y, to_sib]

    def side_in(k):
        ux = column_of(z, y, 1 - x, k)
        uy = column_of(z, 1 - y, x, k)
        remote(ux, core * half, half, x_s.at[k], x_r.at[k], (at_x, core)).wait_recv()
        on_y = remote(ux, core * half + part, part, rb_s.at[k], rb_r.at[k], (at_y, core))
        on_y.start()
        sib_x = remote(ux, core * half, half, sib_s.at[4 + k], sib_r.at[4 + k], (chip, 1 - core))
        sib_x.start()
        remote(uy, core * half, half, y_s.at[k], y_r.at[k], (at_y, core)).wait_recv()
        on_x = remote(uy, core * half, part, ra_s.at[k], ra_r.at[k], (at_x, core))
        on_x.start()
        sib_y = remote(uy, core * half, half, sib_s.at[8 + k], sib_r.at[8 + k], (chip, 1 - core))
        sib_y.start()
        return [on_y, sib_x, on_x, sib_y]

    def corner_in(k):
        unit = column_of(z, 1 - y, 1 - x, k)
        remote(unit, core * half, part, ra_s.at[k], ra_r.at[k], (at_x, core)).wait_recv()
        sib_a = remote(unit, core * half, part, sib_s.at[12 + k], sib_r.at[12 + k], (chip, 1 - core))
        sib_a.start()
        remote(unit, core * half + part, part, rb_s.at[k], rb_r.at[k], (at_y, core)).wait_recv()
        sib_b = remote(
            unit, core * half + part, part, sib_s.at[16 + k], sib_r.at[16 + k], (chip, 1 - core)
        )
        sib_b.start()
        return [sib_a, sib_b]

    sent = []
    for step in range(6):
        if step < 4:
            sent += column_in(step)
        if 1 <= step < 5:
            sent += side_in(step - 1)
        if step >= 2:
            sent += corner_in(step - 2)
    for copy in sent:
        copy.wait_send()
    for go, stays in started:
        if stays is None:
            go.wait_send()
        else:

            @pl.when(jnp.logical_not(stays))
            def _():
                go.wait_send()

    other = (1 - core) * half
    for k in range(4):
        for at, (yy, xx) in ((0, (y, x)), (4, (y, 1 - x)), (8, (1 - y, x))):
            remote(
                column_of(z, yy, xx, k), other, half, sib_s.at[at + k], sib_r.at[at + k],
                (chip, 1 - core),
            ).wait_recv()
        corner = column_of(z, 1 - y, 1 - x, k)
        remote(
            corner, other, part, sib_s.at[12 + k], sib_r.at[12 + k], (chip, 1 - core)
        ).wait_recv()
        remote(
            corner, other + part, part, sib_s.at[16 + k], sib_r.at[16 + k], (chip, 1 - core)
        ).wait_recv()


def gather_slots(scaled):
    if not chip_pairs():
        return lax.all_gather(scaled, "dp", axis=0, tiled=True)
    dma = pltpu.SemaphoreType.DMA
    counts = (4, 1, 4, 4, 4, 4, 4, 4, 4, 4, 4, 20, 20)
    everyone = pl.pallas_call(
        gather_kernel,
        out_shape=jax.ShapeDtypeStruct((16,) + scaled.shape, scaled.dtype),
        in_specs=[ANY],
        out_specs=ANY,
        scratch_shapes=[dma((n,)) for n in counts],
        compiler_params=pltpu.CompilerParams(
            collective_id=0, has_side_effects=True, vmem_limit_bytes=4 * MIB
        ),
    )(scaled)
    return everyone.reshape((-1,) + scaled.shape[1:])


def toggled(z, y, x, flip_y, flip_x, k):
    high = (z // 2 + k // 2) % 2
    low_bit = (z % 2 + k % 2) % 2
    return (2 * high + low_bit) * 4 + 2 * ((y + flip_y) % 2) + (x + flip_x) % 2


def reduce_kernel(
    kind, block, *refs,
):
    (
        *pieces, vec_in,
        final, vec_out, from_sib, from_x, from_y, corner_a, corner_b,
        left, right, ring, corners, side_x, side_y, middle, stage, vec_box,
        load_s, stage_s, sib_s, sib_r, x_s, x_r, y_s, y_r, ca_s, ca_r, cb_s, cb_r, f_s, f_r, v_s, v_r,
    ) = refs
    chip, core, z, y, x = place_of()
    rank = z % 2
    slots, width, lanes = final.shape[1:]
    half = width // 2
    part = half // 2
    at_x = toggled(z, y, x, 0, 1, 0)
    at_y = toggled(z, y, x, 1, 0, 0)
    sibling = (chip, 1 - core)
    mates = (
        sibling,
        (at_x, core),
        (at_y, core),
        (toggled(z, y, x, 0, 0, 1), core),
        (toggled(z, y, x, 0, 0, 2), core),
    )

    kinds = left.shape[0]
    depth = right.shape[1]
    loads = [
        pltpu.make_async_copy(pieces[i], left.at[i], load_s.at[i]) for i in range(kinds)
    ]
    first = 0
    blank = []
    for i, piece in enumerate(pieces[kinds:]):
        number, rows = piece.shape[:2]
        loads.append(
            pltpu.make_async_copy(
                piece, right.at[pl.ds(first, number), pl.ds(0, rows), :], load_s.at[kinds + i]
            )
        )
        if rows < depth:
            blank.append((first, number, rows))
        first += number
    for load in loads:
        load.start()
    for start, number, rows in blank:

        def clear(i, carry):
            right[start + i, pl.ds(rows, depth - rows), :] = jnp.zeros(
                (depth - rows, lanes), right.dtype
            )
            return carry

        lax.fori_loop(0, number, clear, 0)
    right[first] = jnp.zeros((depth, lanes), right.dtype)
    vec_out[...] = vec_in[...]
    greet(chip, core, z, y, x)
    for load in loads:
        load.wait()

    def remote(src, dst, send, recv, device):
        return pltpu.make_async_remote_copy(
            src_ref=src, dst_ref=dst, send_sem=send, recv_sem=recv,
            device_id=device, device_id_type=MESH,
        )

    def unit_of(q, k):
        return toggled(z, y, x, 1 - q % 2, 1 - q // 2, k)

    def sums(q, k, first, terms, total):
        base = unit_of(q, k) * slots
        count = total.shape[1]

        def one(i, carry):
            slot = base + i
            rows = pl.ds(pl.multiple_of(first, 128), count)
            acc = jnp.dot(
                left[kind[slot], rows, :], right[block[slot]], preferred_element_type=jnp.float32
            )
            for term in terms:
                acc = acc + term[i].astype(jnp.float32)
            total[i] = acc.astype(total.dtype)
            return carry

        lax.fori_loop(0, slots, one, 0)

    mine, other = core * half, (1 - core) * half

    def sub(ref, first):
        return ref.at[:, pl.ds(first, part), :]

    def sib_copy(q, k):
        i = 4 * q + k
        return remote(ring.at[q % 2], from_sib.at[i], sib_s.at[i], sib_r.at[i], sibling)

    def a_copy(k):
        return remote(
            sub(corners.at[k % 2], 0), corner_a.at[k], ca_s.at[k], ca_r.at[k], (at_x, core)
        )

    def b_copy(k):
        return remote(
            sub(corners.at[k % 2], part), corner_b.at[k], cb_s.at[k], cb_r.at[k], (at_y, core)
        )

    def x_copy(k):
        return remote(side_x.at[k % 2], from_x.at[k], x_s.at[k], x_r.at[k], (at_x, core))

    def y_copy(k):
        return remote(side_y.at[k % 2], from_y.at[k], y_s.at[k], y_r.at[k], (at_y, core))

    def f_copy(k):
        src = middle.at[k % 2]
        dst = final.at[z // 2, :, pl.ds(pl.multiple_of(mine, 128), half), :]
        recv = f_r.at[2 * (z // 2) + core]
        return remote(
            src, dst, f_s.at[k], recv, (toggled(z, y, x, 0, 0, k), rank)
        ), pltpu.make_async_copy(src, dst, recv)

    def stays(k):
        return jnp.logical_and(k == 0, rank == core)

    def staged(source, place, i):
        copy = pltpu.make_async_copy(source, place, stage_s.at[i])
        copy.start()
        return copy

    def for_sibling(k):
        def one(q, carry):
            @pl.when(jnp.logical_or(q >= 2, k < 3))
            def _():
                back = jnp.where(q >= 2, k, k + 1)
                sib_copy((q + 2) % 4, back).wait_send()

            sums(q, k, other, (), ring.at[q % 2])
            sib_copy(q, k).start()
            return carry

        lax.fori_loop(0, 4, one, 0)

    def corner(k):
        sib_copy(0, k).wait_recv()
        staged(from_sib.at[k], stage.at[0], 0).wait()

        @pl.when(k < 2)
        def _():
            a_copy(k + 2).wait_send()
            b_copy(k + 2).wait_send()

        sums(0, k, mine, (stage.at[0],), corners.at[k % 2])
        a_copy(k).start()
        b_copy(k).start()

    def sides(k):
        sib_copy(1, k).wait_recv()
        sib_copy(2, k).wait_recv()
        in_x = staged(from_sib.at[4 + k], stage.at[0], 0)
        in_y = staged(from_sib.at[8 + k], stage.at[1], 1)

        @pl.when(k < 2)
        def _():
            x_copy(k + 2).wait_send()
            y_copy(k + 2).wait_send()

        in_x.wait()
        sums(1, k, mine, (sub(stage.at[0], 0),), sub(side_x.at[k % 2], 0))
        b_copy(k).wait_recv()
        in_b = staged(corner_b.at[k], sub(stage.at[2], 0), 2)
        in_y.wait()
        sums(2, k, mine + part, (sub(stage.at[1], part),), sub(side_y.at[k % 2], part))
        in_b.wait()
        a_copy(k).wait_recv()
        in_a = staged(corner_a.at[k], sub(stage.at[2], part), 3)
        sums(
            1, k, mine + part, (sub(stage.at[0], part), sub(stage.at[2], 0)),
            sub(side_x.at[k % 2], part),
        )
        x_copy(k).start()
        in_a.wait()
        sums(2, k, mine, (sub(stage.at[1], 0), sub(stage.at[2], part)), sub(side_y.at[k % 2], 0))
        y_copy(k).start()

    def centre(k):
        sib_copy(3, k).wait_recv()
        in_sib = staged(from_sib.at[12 + k], stage.at[0], 0)
        x_copy(k).wait_recv()
        in_x = staged(from_x.at[k], stage.at[1], 1)
        y_copy(k).wait_recv()
        in_y = staged(from_y.at[k], stage.at[2], 2)

        @pl.when(k < 2)
        def _():
            f_copy(k + 2)[0].wait_send()

        in_sib.wait()
        in_x.wait()
        in_y.wait()
        sums(3, k, mine, (stage.at[0], stage.at[1], stage.at[2]), middle.at[k % 2])
        go, here = f_copy(k)

        @pl.when(stays(k))
        def _():
            here.start()

        @pl.when(jnp.logical_not(stays(k)))
        def _():
            go.start()

    def vec_copy(i):
        return remote(vec_out, vec_box.at[i], v_s.at[i], v_r.at[i], mates[i])

    def turn(step, carry):
        for i in range(5):

            @pl.when(step == i)
            def _():
                vec_copy(i).start()

        @pl.when(step < 4)
        def _():
            for_sibling(3 - step)
            corner(3 - step)

        @pl.when(jnp.logical_and(step >= 1, step < 5))
        def _():
            sides(4 - step)

        @pl.when(step >= 2)
        def _():
            centre(5 - step)

        for i in range(5):

            @pl.when(step == i)
            def _():
                vec_copy(i).wait()
                vec_out[...] = vec_out[...] + vec_box[i]

        return carry

    lax.fori_loop(0, 6, turn, 0)
    for q in (2, 3):
        sib_copy(q, 0).wait_send()
    for k in (1, 0):
        a_copy(k).wait_send()
        b_copy(k).wait_send()
        x_copy(k).wait_send()
        y_copy(k).wait_send()
    f_copy(1)[0].wait_send()

    @pl.when(rank != core)
    def _():
        f_copy(0)[0].wait_send()

    for plane in range(2):
        for h in range(2):
            piece = final.at[plane, :, pl.ds(h * half, half), :]
            pltpu.make_async_copy(piece, piece, f_r.at[2 * plane + h]).wait()


def reduce_slots(holder, kinds, rows, columns, vector, slot_count):
    if not chip_pairs():
        grads = slot_grads(holder, kinds, rows, columns)
        total = lax.psum_scatter(grads, "dp", scatter_dimension=0, tiled=True)
        return [total], lax.psum(vector, ("dp", "tensor"))
    depth = max(r.shape[0] for r in rows)
    left = [jnp.pad(r, ((0, depth - r.shape[0]), (0, 0))).T for r in rows]
    lanes = columns[0].shape[2]
    tiles = sum(c.shape[0] for c in columns)
    block = jnp.where(holder >= 0, holder, tiles)
    kind = kinds[jnp.maximum(holder, 0)]
    width = rows[0].shape[1]
    half = width // 2
    dma = pltpu.SemaphoreType.DMA
    scalars = pl.BlockSpec(memory_space=pltpu.SMEM)
    inside = pl.BlockSpec(memory_space=pltpu.VMEM)
    low = jnp.bfloat16

    def room(count, tall):
        return jax.ShapeDtypeStruct((count, slot_count, tall, lanes), low)

    def slab(count):
        return pltpu.VMEM((count, slot_count, half, lanes), low)

    outs = pl.pallas_call(
        reduce_kernel,
        out_shape=[
            room(2, width), jax.ShapeDtypeStruct(vector.shape, vector.dtype),
            room(16, half), room(4, half), room(4, half),
            room(4, half // 2), room(4, half // 2),
        ],
        in_specs=[scalars, scalars] + [ANY] * (len(left) + len(columns)) + [inside],
        out_specs=[ANY, inside] + [ANY] * 5,
        scratch_shapes=[
            pltpu.VMEM((len(left), width, depth), low),
            pltpu.VMEM((tiles + 1, depth, lanes), low),
            slab(2), slab(2), slab(2), slab(2), slab(2), slab(3),
            pltpu.VMEM((5,) + vector.shape, vector.dtype),
        ]
        + [dma((n,)) for n in (len(left) + len(columns), 4, 16, 16) + (4,) * 10 + (5, 5)],
        compiler_params=pltpu.CompilerParams(
            collective_id=1, has_side_effects=True, vmem_limit_bytes=58 * MIB
        ),
    )(kind, block, *left, *columns, vector)
    return [outs[0][0], outs[0][1]], outs[1]


def kind_of_blocks(tile_count, heads_here, blocks_here):
    number = jnp.arange(tile_count)
    kind = number // heads_here
    table = jnp.array([0, 0, 0, 1, 2, 3, 3, 4], jnp.int32)
    late = jnp.where(number < 8 * heads_here + blocks_here, 5, 6)
    return jnp.where(number < 8 * heads_here, table[jnp.minimum(kind, 7)], late).astype(jnp.int32)


def slot_grads(holder, kinds, rows, columns):
    depth = max(r.shape[0] for r in rows)

    def deep(value, axis):
        room = [(0, 0)] * value.ndim
        room[axis] = (0, depth - value.shape[axis])
        return jnp.pad(value, room)

    left = jnp.stack([deep(r, 0) for r in rows])
    right = jnp.concatenate([deep(c, 1) for c in columns], 0)
    slots = holder.shape[0]
    used = (holder >= 0).astype(jnp.int32)
    block = jnp.maximum(holder, 0)
    kind = kinds[block]
    width = rows[0].shape[1]
    lanes = right.shape[2]

    def multiply(kind_ref, block_ref, used_ref, left_ref, right_ref, out_ref):
        slot = pl.program_id(0)

        @pl.when(used_ref[slot] == 1)
        def _():
            out_ref[0] = lax.dot_general(
                left_ref[kind_ref[slot]],
                right_ref[0],
                (((0,), (0,)), ((), ())),
                preferred_element_type=jnp.float32,
            ).astype(out_ref.dtype)

        @pl.when(used_ref[slot] == 0)
        def _():
            out_ref[...] = jnp.zeros_like(out_ref)

    return pl.pallas_call(
        multiply,
        grid_spec=pltpu.PrefetchScalarGridSpec(
            num_scalar_prefetch=3,
            grid=(slots,),
            in_specs=[
                pl.BlockSpec(left.shape, lambda s, kd, b, u: (0, 0, 0)),
                pl.BlockSpec((1, depth, lanes), lambda s, kd, b, u: (b[s], 0, 0)),
            ],
            out_specs=pl.BlockSpec((1, width, lanes), lambda s, kd, b, u: (s, 0, 0)),
        ),
        out_shape=jax.ShapeDtypeStruct((slots, width, lanes), jnp.bfloat16),
        compiler_params=pltpu.CompilerParams(vmem_limit_bytes=48 * MIB),
    )(kind, block, used, left, right)


def adam_slots(parts, master, moment_one, moment_two, slot_scale, filled):
    slot_count, width, lanes = master.shape[1:]
    count = len(parts)
    tall = width // 2

    def step(scale_ref, fill_ref, *refs):
        grads = refs[:count]
        weight, one, two, new_weight, new_one, new_two = refs[count:]
        slot = pl.program_id(0)

        @pl.when(fill_ref[slot] == 1)
        def _():
            total = grads[0][0].astype(jnp.float32)
            for more in grads[1:]:
                total = total + more[0].astype(jnp.float32)
            results = adam_step(
                weight[0, 0], total * scale_ref[slot], one[0, 0], two[0, 0], TILE_RATE, TILE_DECAY
            )
            for ref, value in zip((new_weight, new_one, new_two), results):
                ref[0, 0] = value

        @pl.when(fill_ref[slot] == 0)
        def _():
            new_weight[...] = weight[...]
            new_one[...] = one[...]
            new_two[...] = two[...]

    flat = pl.BlockSpec((1, tall, lanes), lambda s, i: (s, i, 0))
    deep = pl.BlockSpec((1, 1, tall, lanes), lambda s, i: (0, s, i, 0))
    scalars = pl.BlockSpec(memory_space=pltpu.SMEM)
    return pl.pallas_call(
        step,
        grid=(slot_count, 2),
        in_specs=[scalars, scalars] + [flat] * count + [deep] * 3,
        out_specs=[deep] * 3,
        out_shape=[jax.ShapeDtypeStruct(master.shape, jnp.float32)] * 3,
    )(slot_scale, filled.astype(jnp.int32), *parts, master, moment_one, moment_two)


SCALING = HEAD ** (-0.5)
BF16 = jnp.bfloat16
F32 = jnp.float32


def nn(left, right):
    return jnp.dot(left, right, preferred_element_type=F32)


def nt(left, right):
    return lax.dot_general(left, right, (((1,), (1,)), ((), ())), preferred_element_type=F32)


def tn(left, right):
    return lax.dot_general(left, right, (((0,), (0,)), ((), ())), preferred_element_type=F32)


def normed(rows):
    centre = rows - jnp.mean(rows, -1, keepdims=True)
    inverse = lax.rsqrt(jnp.mean(centre * centre, -1, keepdims=True) + NORM_EPS)
    return centre * inverse, inverse


def normed_back(rows, grad):
    unit, inverse = normed(rows)
    mean = jnp.mean(grad, -1, keepdims=True)
    return (grad - mean - unit * jnp.mean(grad * unit, -1, keepdims=True)) * inverse, unit


def total_of(rows):
    return jnp.sum(rows, 0, keepdims=True)


def turned(rows, cos_tab, sin_tab):
    even = lax.broadcasted_iota(jnp.int32, rows.shape, 1) % 2 == 0
    partner = jnp.where(even, pltpu.roll(rows, HEAD - 1, 1), pltpu.roll(rows, 1, 1))
    return rows * cos_tab + partner * sin_tab


def wide(column):
    return jnp.broadcast_to(column, (column.shape[0], HEAD))


def pack_sums(for_rows, for_text=None):
    out = wide(for_rows)
    if for_text is None:
        return out
    lane = lax.broadcasted_iota(jnp.int32, out.shape, 1)
    count = for_text.shape[0] // 2
    rest = jnp.zeros((out.shape[0] - count, HEAD), F32)
    first = jnp.concatenate([wide(for_text[:count]), rest], 0)
    second = jnp.concatenate([wide(for_text[count:]), rest], 0)
    return jnp.where(lane < 32, out, jnp.where(lane < 64, first, second))


def unpack_text(sums, count):
    return jnp.concatenate([sums[: count // 2, 32:33], sums[: count // 2, 64:65]], 0)


def softmax(scores):
    expo = jnp.exp(scores - jnp.max(scores, -1, keepdims=True))
    return expo / jnp.sum(expo, -1, keepdims=True)


def self_scores(query_low, key_low, tokens):
    scores = nt(query_low, key_low) * SCALING
    lane = lax.broadcasted_iota(jnp.int32, scores.shape, 1)
    return jnp.where(lane < tokens, scores, -1e30)


def whole(array):
    zeros = (0,) * array.ndim
    return pl.BlockSpec(array.shape, lambda *_: zeros)


def block_at(first, stride=1):
    return pl.BlockSpec((1, D, HEAD), lambda i, where: (where[first + stride * i], 0, 0))


def call(body, places, grid, ins, outs, scratch=(), vmem=40):
    specs = [spec if spec is not None else whole(array) for array, spec in ins]
    shapes = [jax.ShapeDtypeStruct(shape, kind) for shape, kind, _ in outs]
    out_specs = [
        spec if spec is not None else whole(shape) for (_, _, spec), shape in zip(outs, shapes)
    ]
    return pl.pallas_call(
        body,
        grid_spec=pltpu.PrefetchScalarGridSpec(
            num_scalar_prefetch=1,
            grid=(grid,),
            in_specs=specs,
            out_specs=out_specs,
            scratch_shapes=list(scratch),
        ),
        out_shape=shapes,
        compiler_params=pltpu.CompilerParams(vmem_limit_bytes=vmem * MIB),
    )(places, *[array for array, _ in ins])


def head_lanes(rows):
    return pl.BlockSpec((rows, HEAD), lambda h, *_: (0, h))


def joined(refs):
    return jnp.concatenate([ref[0] for ref in refs], 1)


def project_self(places, everyone, rows, mod, vecs, heads):
    count = rows.shape[0]
    span = heads * HEAD

    def body(_, rows_ref, mod_ref, vec_ref, *refs):
        weights, (low, pre, value, sums, acc) = refs[:heads], refs[heads:]
        i = pl.program_id(0)

        @pl.when(i == 0)
        def _():
            unit, _ = normed(rows_ref[...])
            low[...] = (unit * (1.0 + mod_ref[1:2]) + mod_ref[0:1]).astype(BF16)

        made = nn(low[...], joined(weights))

        @pl.when(i == 0)
        def _():
            q = made + vec_ref[0:1]
            pre[0] = q
            acc[...] = wide(jnp.sum(q * q, -1, keepdims=True))

        @pl.when(i == 1)
        def _():
            k = made + vec_ref[1:2]
            pre[0] = k
            lane = lax.broadcasted_iota(jnp.int32, acc.shape, 1)
            sums[...] = jnp.where(lane < 64, acc[...], wide(jnp.sum(k * k, -1, keepdims=True)))

        @pl.when(i == 2)
        def _():
            value[...] = (made + vec_ref[2:3]).astype(BF16)

    return call(
        body, places, 3,
        [(rows, None), (mod, None), (vecs, None)]
        + [(everyone, block_at(h, heads)) for h in range(heads)],
        [
            ((count, D), BF16, None),
            ((2, count, span), F32, pl.BlockSpec((1, count, span), lambda i, _: (jnp.minimum(i, 1), 0, 0))),
            ((count, span), BF16, None),
            ((count, HEAD), F32, None),
        ],
        [pltpu.VMEM((count, HEAD), F32)],
    )


def attend_self(places, everyone, pre, value, sums, other, vecs, cos_tab, sin_tab, heads, tokens):
    count = value.shape[0]

    def body(_, pre_ref, value_ref, sum_ref, other_ref, vec_ref, cos_ref, sin_ref, weight, q_ref, k_ref, o_ref, y_ref, acc):
        h = pl.program_id(0)
        total = sum_ref[...] + other_ref[...]
        q_inv = lax.rsqrt(total[:, 0:1] / D + NORM_EPS)
        k_inv = lax.rsqrt(total[:, 64:65] / D + NORM_EPS)
        cos, sin = cos_ref[...], sin_ref[...]
        q = turned(pre_ref[0] * q_inv * vec_ref[3:4], cos, sin).astype(BF16)
        k = turned(pre_ref[1] * k_inv * vec_ref[4:5], cos, sin).astype(BF16)
        q_ref[...] = q
        k_ref[...] = k
        chance = softmax(self_scores(q, k, tokens))
        out = nn(chance.astype(BF16), value_ref[...]).astype(BF16)
        o_ref[0] = out
        part = nt(out, weight[0])

        @pl.when(h == 0)
        def _():
            acc[...] = part

        @pl.when(h > 0)
        def _():
            acc[...] = acc[...] + part

        @pl.when(h == heads - 1)
        def _():
            y_ref[...] = acc[...].astype(BF16)

    lanes = head_lanes(count)
    return call(
        body, places, heads,
        [
            (pre, pl.BlockSpec((2, count, HEAD), lambda h, _: (0, 0, h))),
            (value, lanes), (sums, None), (other, None),
            (vecs, head_lanes(vecs.shape[0])), (cos_tab, None), (sin_tab, None),
            (everyone, block_at(3 * heads)),
        ],
        [
            (value.shape, BF16, lanes),
            (value.shape, BF16, lanes),
            ((heads, count, HEAD), BF16, pl.BlockSpec((1, count, HEAD), lambda h, _: (h, 0, 0))),
            ((count, D), BF16, None),
        ],
        [pltpu.VMEM((count, D), F32)],
    )


def project_text(places, everyone, context, vecs, heads):
    count = context.shape[0]
    span = heads * HEAD

    def body(_, text_ref, vec_ref, *refs):
        weights, (key, value, sums) = refs[:heads], refs[heads:]
        i = pl.program_id(0)
        made = nn(text_ref[...], joined(weights))

        @pl.when(i == 0)
        def _():
            k = made + vec_ref[6:7]
            key[...] = k
            sums[...] = wide(jnp.sum(k * k, -1, keepdims=True))

        @pl.when(i == 1)
        def _():
            value[...] = (made + vec_ref[7:8]).astype(BF16)

    return call(
        body, places, 2,
        [(context, None), (vecs, None)]
        + [(everyone, block_at(5 * heads + h, heads)) for h in range(heads)],
        [((count, span), F32, None), ((count, span), BF16, None), ((count, HEAD), F32, None)],
    )


def project_cross(places, everyone, rows, part, other, mod, shared, vecs, text_sums, heads):
    count = rows.shape[0]
    span = heads * HEAD
    text = text_sums.shape[0]

    def body(_, rows_ref, part_ref, other_ref, mod_ref, shared_ref, vec_ref, text_ref, *refs):
        weights, (branch, after, low, pre, sums) = refs[:heads], refs[heads:]
        y = part_ref[...].astype(F32) + other_ref[...].astype(F32) + shared_ref[0:1]
        branch[...] = y
        x = rows_ref[...] + mod_ref[2:3] * y
        after[...] = x
        unit, _ = normed(x)
        a = (unit * shared_ref[3:4] + shared_ref[4:5]).astype(BF16)
        low[...] = a
        q = nn(a, joined(weights)) + vec_ref[5:6]
        pre[...] = q
        sums[...] = pack_sums(jnp.sum(q * q, -1, keepdims=True), text_ref[:, 0:1])

    return call(
        body, places, 1,
        [(v, None) for v in (rows, part, other, mod, shared, vecs, text_sums)]
        + [(everyone, block_at(4 * heads + h)) for h in range(heads)],
        [
            ((count, D), F32, None),
            ((count, D), F32, None),
            ((count, D), BF16, None),
            ((count, span), F32, None),
            ((count, HEAD), F32, None),
        ],
    )


def attend_cross(places, everyone, pre, key_pre, value, sums, other, vecs, heads):
    count, text = pre.shape[0], value.shape[0]

    def body(_, pre_ref, key_ref, value_ref, sum_ref, other_ref, vec_ref, weight, q_ref, k_ref, o_ref, y_ref, acc):
        h = pl.program_id(0)
        total = sum_ref[...] + other_ref[...]
        q_inv = lax.rsqrt(total[:, 0:1] / D + NORM_EPS)
        k_inv = lax.rsqrt(unpack_text(total, text) / D + NORM_EPS)
        q = (pre_ref[...] * q_inv * vec_ref[8:9]).astype(BF16)
        k = (key_ref[...] * k_inv * vec_ref[9:10]).astype(BF16)
        q_ref[...] = q
        k_ref[...] = k
        chance = softmax(nt(q, k) * SCALING)
        out = nn(chance.astype(BF16), value_ref[...]).astype(BF16)
        o_ref[0] = out
        part = nt(out, weight[0])

        @pl.when(h == 0)
        def _():
            acc[...] = part

        @pl.when(h > 0)
        def _():
            acc[...] = acc[...] + part

        @pl.when(h == heads - 1)
        def _():
            y_ref[...] = acc[...].astype(BF16)

    return call(
        body, places, heads,
        [
            (pre, head_lanes(count)), (key_pre, head_lanes(text)), (value, head_lanes(text)),
            (sums, None), (other, None), (vecs, head_lanes(vecs.shape[0])),
            (everyone, block_at(7 * heads)),
        ],
        [
            (pre.shape, BF16, head_lanes(count)),
            (value.shape, BF16, head_lanes(text)),
            ((heads, count, HEAD), BF16, pl.BlockSpec((1, count, HEAD), lambda h, _: (h, 0, 0))),
            ((count, D), BF16, None),
        ],
        [pltpu.VMEM((count, D), F32)],
    )


def feed_forward(places, everyone, after_one, part, other, mod, shared, cot, up_bias, heads, blocks):
    count = after_one.shape[0]
    group = max(g for g in (7, 5, 3, 1) if blocks % g == 0 and g <= 5)
    span = group * HEAD

    def body(_, after_ref, part_ref, other_ref, mod_ref, shared_ref, cot_ref, bias_ref, *refs):
        ups, downs = refs[:group], refs[group : 2 * group]
        after, low, grad, hidden, d_hidden, d_bias, y_ref, da_ref, y_acc, da_acc = refs[2 * group :]
        i = pl.program_id(0)

        @pl.when(i == 0)
        def _():
            x = after_ref[...] + part_ref[...].astype(F32) + other_ref[...].astype(F32)
            x = x + shared_ref[1:2]
            after[...] = x
            unit, _ = normed(x)
            low[...] = (unit * (1.0 + mod_ref[4:5]) + mod_ref[3:4]).astype(BF16)
            grad[...] = (mod_ref[5:6] * cot_ref[...]).astype(BF16)
            y_acc[...] = jnp.zeros_like(y_acc)
            da_acc[...] = jnp.zeros_like(da_acc)

        up, down = joined(ups), joined(downs)
        pre = nn(low[...], up) + bias_ref[...]
        square = pre * pre
        bent = jnp.tanh(GELU_COEF * (pre + 0.044715 * pre * square))
        act = (0.5 * pre * (1.0 + bent)).astype(BF16)
        slope = 0.5 * (1.0 + bent) + 0.5 * pre * (1.0 - bent * bent) * (
            GELU_COEF * (1.0 + 3.0 * 0.044715 * square)
        )
        dh = (nn(grad[...], down) * slope).astype(BF16)
        d_bias[...] = total_of(dh.astype(F32))
        for j in range(group):
            hidden[j] = act[:, j * HEAD : (j + 1) * HEAD]
            d_hidden[j] = dh[:, j * HEAD : (j + 1) * HEAD]
        y_acc[...] = y_acc[...] + nt(act, down)
        da_acc[...] = da_acc[...] + nt(dh, up)

        @pl.when(i == blocks // group - 1)
        def _():
            y_ref[...] = y_acc[...].astype(BF16)
            da_ref[...] = da_acc[...].astype(BF16)

    base = 8 * heads
    tall = pl.BlockSpec((group, count, HEAD), lambda i, _: (i, 0, 0))
    flat = pl.BlockSpec((1, span), lambda i, _: (0, i))
    return call(
        body, places, blocks // group,
        [(v, None) for v in (after_one, part, other, mod, shared, cot)]
        + [(up_bias, flat)]
        + [(everyone, block_at(base + j, group)) for j in range(group)]
        + [(everyone, block_at(base + blocks + j, group)) for j in range(group)],
        [
            ((count, D), F32, None),
            ((count, D), BF16, None),
            ((count, D), BF16, None),
            ((blocks, count, HEAD), BF16, tall),
            ((blocks, count, HEAD), BF16, tall),
            (up_bias.shape, F32, flat),
            ((count, D), BF16, None),
            ((count, D), BF16, None),
        ],
        [pltpu.VMEM((count, D), F32), pltpu.VMEM((count, D), F32)],
        vmem=48,
    )


def cross_back(places, everyone, cot, after_two, part, other, mod, query, key, value, pre, key_pre, vecs, heads):
    count, text = query.shape[0], key.shape[0]

    def body(_, cot_ref, after_ref, part_ref, other_ref, mod_ref, q_ref, k_ref, v_ref, pre_ref, key_ref, vec_ref, weight, dx_ref, low_ref, dq_ref, dk_ref, dv_ref, sums, q_acc, k_acc):
        h = pl.program_id(0)

        @pl.when(h == 0)
        def _():
            da = part_ref[...].astype(F32) + other_ref[...].astype(F32)
            back, _ = normed_back(after_ref[...], da * (1.0 + mod_ref[4:5]))
            dx = cot_ref[...] + back
            dx_ref[...] = dx
            low_ref[...] = dx.astype(BF16)
            q_acc[...] = jnp.zeros_like(q_acc)
            k_acc[...] = jnp.zeros_like(k_acc)

        do = nn(low_ref[...], weight[0]).astype(BF16)
        q, k = q_ref[...], k_ref[...]
        chance = softmax(nt(q, k) * SCALING)
        dp = nt(do, v_ref[...])
        ds = (chance * (dp - jnp.sum(chance * dp, -1, keepdims=True))).astype(BF16)
        dv_ref[0] = tn(chance.astype(BF16), do).astype(BF16)
        dq = nn(ds, k) * SCALING
        dk = tn(ds, q) * SCALING
        dq_ref[...] = dq
        dk_ref[...] = dk
        q_acc[...] = q_acc[...] + wide(jnp.sum(pre_ref[...] * vec_ref[8:9] * dq, -1, keepdims=True))
        k_acc[...] = k_acc[...] + wide(jnp.sum(key_ref[...] * vec_ref[9:10] * dk, -1, keepdims=True))

        @pl.when(h == heads - 1)
        def _():
            sums[...] = pack_sums(q_acc[:, 0:1], k_acc[:, 0:1])

    return call(
        body, places, heads,
        [(v, None) for v in (cot, after_two, part, other, mod)]
        + [
            (query, head_lanes(count)), (key, head_lanes(text)), (value, head_lanes(text)),
            (pre, head_lanes(count)), (key_pre, head_lanes(text)),
            (vecs, head_lanes(vecs.shape[0])), (everyone, block_at(7 * heads)),
        ],
        [
            ((count, D), F32, None),
            ((count, D), BF16, None),
            (query.shape, F32, head_lanes(count)),
            (key.shape, F32, head_lanes(text)),
            ((heads, text, HEAD), BF16, pl.BlockSpec((1, text, HEAD), lambda h, _: (h, 0, 0))),
            ((count, HEAD), F32, None),
        ],
        [pltpu.VMEM((count, HEAD), F32), pltpu.VMEM((text, HEAD), F32)],
    )


def norm_grad(pre, inverse, gain, incoming, total):
    grad = inverse * (gain * incoming) - pre * (inverse * inverse * inverse) * (total / D)
    low = grad.astype(BF16)
    return low, total_of(low.astype(F32)), total_of(incoming * pre * inverse)


def cross_back_rows(places, everyone, pre, key_pre, dq, dk, dv, squares, squares_other, sums, sums_other, vecs, heads):
    count, text = pre.shape[0], key_pre.shape[0]

    def body(_, pre_ref, key_ref, dq_ref, dk_ref, dv_ref, sq_ref, sqo_ref, sum_ref, sumo_ref, vec_ref, weight, gq_ref, gk_ref, vec_out, da_ref, acc):
        h = pl.program_id(0)
        squares_all = sq_ref[...] + sqo_ref[...]
        total = sum_ref[...] + sumo_ref[...]
        q_inv = lax.rsqrt(squares_all[:, 0:1] / D + NORM_EPS)
        k_inv = lax.rsqrt(unpack_text(squares_all, text) / D + NORM_EPS)
        low_q, bias_q, gain_q = norm_grad(pre_ref[...], q_inv, vec_ref[8:9], dq_ref[...], total[:, 0:1])
        low_k, bias_k, gain_k = norm_grad(
            key_ref[...], k_inv, vec_ref[9:10], dk_ref[...], unpack_text(total, text)
        )
        gq_ref[0] = low_q
        gk_ref[0] = low_k
        bias_v = total_of(dv_ref[0].astype(F32))
        vec_out[...] = jnp.concatenate(
            [bias_q, bias_k, bias_v, gain_q, gain_k, jnp.zeros((3, HEAD), F32)], 0
        )
        part = nt(low_q, weight[0])

        @pl.when(h == 0)
        def _():
            acc[...] = part

        @pl.when(h > 0)
        def _():
            acc[...] = acc[...] + part

        @pl.when(h == heads - 1)
        def _():
            da_ref[...] = acc[...].astype(BF16)

    tall = pl.BlockSpec((1, count, HEAD), lambda h, _: (h, 0, 0))
    tall_text = pl.BlockSpec((1, text, HEAD), lambda h, _: (h, 0, 0))
    return call(
        body, places, heads,
        [
            (pre, head_lanes(count)), (key_pre, head_lanes(text)), (dq, head_lanes(count)),
            (dk, head_lanes(text)), (dv, tall_text), (squares, None), (squares_other, None),
            (sums, None), (sums_other, None), (vecs, head_lanes(vecs.shape[0])),
            (everyone, block_at(4 * heads)),
        ],
        [
            ((heads, count, HEAD), BF16, tall),
            ((heads, text, HEAD), BF16, tall_text),
            ((8, heads * HEAD), F32, head_lanes(8)),
            ((count, D), BF16, None),
        ],
        [pltpu.VMEM((count, D), F32)],
    )


def self_back(places, everyone, dx_two, after_one, part, other, mod, shared, query, key, value, pre, vecs, cos_tab, sin_tab, heads, tokens):
    count = query.shape[0]

    def body(_, dx_in, after_ref, part_ref, other_ref, mod_ref, shared_ref, q_ref, k_ref, v_ref, pre_ref, vec_ref, cos_ref, sin_ref, weight, dx_ref, low_ref, d_ref, dv_ref, sums, q_acc, k_acc):
        h = pl.program_id(0)

        @pl.when(h == 0)
        def _():
            da = part_ref[...].astype(F32) + other_ref[...].astype(F32)
            back, _ = normed_back(after_ref[...], da * shared_ref[3:4])
            dx = dx_in[...] + back
            dx_ref[...] = dx
            low_ref[...] = (mod_ref[2:3] * dx).astype(BF16)
            q_acc[...] = jnp.zeros_like(q_acc)
            k_acc[...] = jnp.zeros_like(k_acc)

        do = nn(low_ref[...], weight[0]).astype(BF16)
        q, k = q_ref[...], k_ref[...]
        chance = softmax(self_scores(q, k, tokens))
        dp = nt(do, v_ref[...])
        ds = (chance * (dp - jnp.sum(chance * dp, -1, keepdims=True))).astype(BF16)
        dv_ref[0] = tn(chance.astype(BF16), do).astype(BF16)
        cos, sin = cos_ref[...], -sin_ref[...]
        dq = turned(nn(ds, k) * SCALING, cos, sin)
        dk = turned(tn(ds, q) * SCALING, cos, sin)
        d_ref[0] = dq
        d_ref[1] = dk
        q_acc[...] = q_acc[...] + wide(jnp.sum(pre_ref[0] * vec_ref[3:4] * dq, -1, keepdims=True))
        k_acc[...] = k_acc[...] + wide(jnp.sum(pre_ref[1] * vec_ref[4:5] * dk, -1, keepdims=True))

        @pl.when(h == heads - 1)
        def _():
            lane = lax.broadcasted_iota(jnp.int32, q_acc.shape, 1)
            sums[...] = jnp.where(lane < 64, q_acc[...], k_acc[...])

    lanes = head_lanes(count)
    pair = pl.BlockSpec((2, count, HEAD), lambda h, _: (0, 0, h))
    return call(
        body, places, heads,
        [(v, None) for v in (dx_two, after_one, part, other, mod, shared)]
        + [
            (query, lanes), (key, lanes), (value, lanes), (pre, pair),
            (vecs, head_lanes(vecs.shape[0])), (cos_tab, None), (sin_tab, None),
            (everyone, block_at(3 * heads)),
        ],
        [
            ((count, D), F32, None),
            ((count, D), BF16, None),
            (pre.shape, F32, pair),
            ((heads, count, HEAD), BF16, pl.BlockSpec((1, count, HEAD), lambda h, _: (h, 0, 0))),
            ((count, HEAD), F32, None),
        ],
        [pltpu.VMEM((count, HEAD), F32), pltpu.VMEM((count, HEAD), F32)],
    )


def self_back_rows(places, everyone, pre, grads, dv, squares, squares_other, sums, sums_other, vecs, heads):
    count = pre.shape[1]

    def body(_, pre_ref, d_ref, dv_ref, sq_ref, sqo_ref, sum_ref, sumo_ref, vec_ref, wq, wk, wv, gq_ref, gk_ref, vec_out, da_ref, acc):
        h = pl.program_id(0)
        squares_all = sq_ref[...] + sqo_ref[...]
        total = sum_ref[...] + sumo_ref[...]
        lows, biases, gains = [], [], []
        for n in range(2):
            inverse = lax.rsqrt(squares_all[:, 64 * n : 64 * n + 1] / D + NORM_EPS)
            low, bias, gain = norm_grad(
                pre_ref[n], inverse, vec_ref[3 + n : 4 + n], d_ref[n], total[:, 64 * n : 64 * n + 1]
            )
            lows.append(low)
            biases.append(bias)
            gains.append(gain)
        gq_ref[0] = lows[0]
        gk_ref[0] = lows[1]
        dv_low = dv_ref[0]
        bias_v = total_of(dv_low.astype(F32))
        vec_out[...] = jnp.concatenate(
            [biases[0], biases[1], bias_v, gains[0], gains[1], jnp.zeros((3, HEAD), F32)], 0
        )
        part = nt(
            jnp.concatenate([lows[0], lows[1], dv_low], 1),
            jnp.concatenate([wq[0], wk[0], wv[0]], 1),
        )

        @pl.when(h == 0)
        def _():
            acc[...] = part

        @pl.when(h > 0)
        def _():
            acc[...] = acc[...] + part

        @pl.when(h == heads - 1)
        def _():
            da_ref[...] = acc[...].astype(BF16)

    tall = pl.BlockSpec((1, count, HEAD), lambda h, _: (h, 0, 0))
    pair = pl.BlockSpec((2, count, HEAD), lambda h, _: (0, 0, h))
    return call(
        body, places, heads,
        [
            (pre, pair), (grads, pair), (dv, tall), (squares, None), (squares_other, None),
            (sums, None), (sums_other, None), (vecs, head_lanes(vecs.shape[0])),
            (everyone, block_at(0)), (everyone, block_at(heads)), (everyone, block_at(2 * heads)),
        ],
        [
            ((heads, count, HEAD), BF16, tall),
            ((heads, count, HEAD), BF16, tall),
            ((8, heads * HEAD), F32, head_lanes(8)),
            ((count, D), BF16, None),
        ],
        [pltpu.VMEM((count, D), F32)],
    )


def shared_sums(places, rows, after_one, after_two, low_grads, dx_one, branch, cot, das, y_three, shared):
    def body(_, x_ref, x1_ref, x2_ref, dy1, dy2, dy3, dx1_ref, y1_ref, cot_ref, da1, da3, da2, y3, shared_ref, out):
        def half(value):
            return 0.5 * total_of(value)

        out[0:1] = half(dy1[...].astype(F32))
        out[1:2] = half(dy2[...].astype(F32))
        out[2:3] = half(dy3[...].astype(F32))
        part = da3[...].astype(F32)
        out[3:4] = total_of(part * normed(x1_ref[...])[0])
        out[4:5] = total_of(part)
        part = da1[...].astype(F32)
        out[5:6] = total_of(part)
        out[6:7] = total_of(part * normed(x_ref[...])[0])
        out[7:8] = half(dx1_ref[...] * y1_ref[...])
        part = da2[...].astype(F32)
        out[8:9] = total_of(part)
        out[9:10] = total_of(part * normed(x2_ref[...])[0])
        out[10:11] = total_of(cot_ref[...] * (y3[...].astype(F32) + 0.5 * shared_ref[2:3]))

    return call(
        body, places, 1,
        [(v, None) for v in (rows, after_one, after_two, *low_grads, dx_one, branch, cot, *das, y_three, shared)],
        [(shared.shape, F32, None)],
        vmem=48,
    )[0]


def body(
    latents,
    context,
    cotangent,
    positions,
    step_ids,
    owners,
    time_table,
    master,
    first_moment,
    second_moment,
    head_params,
    head_first,
    head_second,
    shared_params,
    shared_first,
    shared_second,
):
    tensors = lax.axis_size("tensor")
    devices = lax.axis_size("dp")
    slot_count = master.shape[1]
    tile_count = owners.shape[0]
    heads_here = HEADS // tensors
    blocks_here = FF // (HEAD * tensors)
    width_here = D // tensors
    places, holder = owner_layout(owners, slot_count, devices)
    scales = tile_scales(tile_count, heads_here, blocks_here)
    my_slots = lax.dynamic_slice_in_dim(holder, lax.axis_index("dp") * slot_count, slot_count)
    rank = pair_rank()
    latents, context, cotangent, positions, step_ids, head_here = home_swap(
        latents, context, cotangent, positions, step_ids, head_params
    )
    filled = my_slots >= 0
    slot_scale = jnp.where(filled, scales[jnp.maximum(my_slots, 0)], 0.0)
    scaled = (master[0] * slot_scale[:, None, None]).astype(jnp.bfloat16)
    everyone = gather_slots(scaled)
    vectors = head_here[0]
    vecs = vectors[: 10 * width_here].reshape(10, width_here)
    up_bias = vectors[10 * width_here :].reshape(1, -1)
    chosen = (step_ids[0] == jnp.arange(TSTEPS)).astype(jnp.float32)
    mod = shared_params[5:11] + jnp.einsum(
        "s,skd->kd", chosen, time_table, precision=lax.Precision.HIGHEST
    )
    half = latents.shape[0]
    tokens = 2 * half
    count = -(-tokens // 16) * 16
    cos_tab, sin_tab = rope_tables(positions, HEAD)
    sin_tab = jnp.where(jnp.arange(HEAD) % 2 == 0, -sin_tab, sin_tab)
    cos_tab, sin_tab = (jnp.pad(t, ((0, count - tokens), (0, 0))) for t in (cos_tab, sin_tab))

    def all_rows(local_rows):
        other = pair_swap(local_rows)
        rows = jnp.where(
            rank == 0,
            jnp.concatenate([local_rows, other], 0),
            jnp.concatenate([other, local_rows], 0),
        )
        return jnp.pad(rows, ((0, count - tokens), (0, 0))).astype(jnp.float32)

    def own_rows(rows):
        return jnp.where(rank == 0, rows[:half], rows[half:tokens])

    def merged_rows(part):
        theirs = pair_swap(jnp.where(rank == 0, part[half:tokens], part[:half]))
        return own_rows(part).astype(jnp.float32) + theirs.astype(jnp.float32)

    rows = all_rows(latents)
    cot = all_rows(cotangent)
    low_one, pre_one, value_one, squares_one = project_self(
        places, everyone, rows, mod, vecs, heads_here
    )
    squares_one_other = pair_swap(squares_one)
    key_pre, value_two, text_squares = project_text(places, everyone, context, vecs, heads_here)
    query_one, key_one, heads_one, part_one = attend_self(
        places, everyone, pre_one, value_one, squares_one, squares_one_other, vecs, cos_tab,
        sin_tab, heads_here, tokens,
    )
    branch_one, after_one, low_two, pre_two, squares_two = project_cross(
        places, everyone, rows, part_one, pair_swap(part_one), mod, shared_params, vecs,
        text_squares, heads_here,
    )
    squares_two_other = pair_swap(squares_two)
    query_two, key_two, heads_two, part_two = attend_cross(
        places, everyone, pre_two, key_pre, value_two, squares_two, squares_two_other, vecs,
        heads_here,
    )
    after_two, low_three, grad_three, hidden, d_hidden, d_up_bias, y_three, da_two = feed_forward(
        places, everyone, after_one, part_two, pair_swap(part_two), mod, shared_params, cot,
        up_bias, heads_here, blocks_here,
    )
    dx_two, grad_two, dq_two, dk_two, dv_two, sums_two = cross_back(
        places, everyone, cot, after_two, da_two, pair_swap(da_two), mod, query_two, key_two,
        value_two, pre_two, key_pre, vecs, heads_here,
    )
    query_grad_two, key_grad_two, vecs_two, da_three = cross_back_rows(
        places, everyone, pre_two, key_pre, dq_two, dk_two, dv_two, squares_two,
        squares_two_other, sums_two, pair_swap(sums_two), vecs, heads_here,
    )
    dx_one, grad_one, d_one, dv_one, sums_one = self_back(
        places, everyone, dx_two, after_one, da_three, pair_swap(da_three), mod, shared_params,
        query_one, key_one, value_one, pre_one, vecs, cos_tab, sin_tab, heads_here, tokens,
    )
    query_grad_one, key_grad_one, vecs_one, da_one = self_back_rows(
        places, everyone, pre_one, d_one, dv_one, squares_one, squares_one_other, sums_one,
        pair_swap(sums_one), vecs, heads_here,
    )
    shared_grad = shared_sums(
        places, rows, after_one, after_two, (grad_one, grad_two, grad_three), dx_one,
        branch_one, cot, (da_one, da_three, da_two), y_three, shared_params,
    )
    result = own_rows(after_two) + mod[5] * (merged_rows(y_three) + shared_params[2])
    output = result.astype(jnp.bfloat16)
    back, _ = normed_back(own_rows(rows), merged_rows(da_one) * (1.0 + mod[1]))
    grad_input = own_rows(dx_one) + back
    head_grad = jnp.concatenate(
        [vecs_one[:5].reshape(-1), vecs_two[:5].reshape(-1), d_up_bias.reshape(-1)]
    )
    tensor_rank = lax.axis_index("tensor")
    head_padded = jnp.where(jnp.arange(tensors)[:, None] == rank, head_grad[None, :], 0.0)
    vector = jnp.concatenate([head_padded.reshape(-1), shared_grad.reshape(-1)])
    vector = jnp.pad(vector, (0, -vector.shape[0] % 1024)).reshape(-1, 128)
    parts, vector = reduce_slots(
        holder,
        kind_of_blocks(tile_count, heads_here, blocks_here),
        (low_one, grad_one, low_two, context, grad_two, low_three, grad_three),
        (
            query_grad_one,
            key_grad_one,
            dv_one,
            heads_one,
            query_grad_two,
            key_grad_two,
            dv_two,
            heads_two,
            d_hidden,
            hidden,
        ),
        vector,
        slot_count,
    )
    new_master, new_first, new_second = adam_slots(
        parts, master, first_moment, second_moment, slot_scale, filled
    )
    vector = vector.reshape(-1)
    head_total = vector[: head_padded.size].reshape(head_padded.shape)
    shared_total = vector[head_padded.size : head_padded.size + shared_grad.size]
    shared_total = shared_total.reshape(shared_grad.shape)
    mine_head = lax.dynamic_slice_in_dim(head_total, tensor_rank, 1, 0)
    new_head, new_head_first, new_head_second = adam_step(
        head_params, mine_head, head_first, head_second, VECTOR_RATE, 0.0
    )
    new_shared, new_shared_first, new_shared_second = adam_step(
        shared_params, shared_total, shared_first, shared_second, VECTOR_RATE, 0.0
    )
    output, grad_input = home_swap(output, grad_input)
    return (
        output,
        grad_input,
        new_master,
        new_first,
        new_second,
        new_head,
        new_head_first,
        new_head_second,
        new_shared,
        new_shared_first,
        new_shared_second,
    )


def solution(mesh):
    return jax.shard_map(
        body,
        mesh=mesh,
        in_specs=(
            P(("dp", "tensor"), None),
            P("dp", None),
            P(("dp", "tensor"), None),
            P(None, "dp"),
            P("dp"),
            P(),
            P(),
            P("tensor", "dp", None, None),
            P("tensor", "dp", None, None),
            P("tensor", "dp", None, None),
            P("tensor", None),
            P("tensor", None),
            P("tensor", None),
            P(),
            P(),
            P(),
        ),
        out_specs=(
            P(("dp", "tensor"), None),
            P(("dp", "tensor"), None),
            P("tensor", "dp", None, None),
            P("tensor", "dp", None, None),
            P("tensor", "dp", None, None),
            P("tensor", None),
            P("tensor", None),
            P("tensor", None),
            P(),
            P(),
            P(),
        ),
        check_vma=False,
    )
```

time: 1250 us -> 935 us (0.75); the launches traced: 1220 us -> 923 us
  local copies, waits for them, and re-layouts: 188 us -> 74.1 us
  matrix products: 105 us -> 0.31 us
  other arithmetic: 115 us -> 32.5 us
  waiting for transfers between devices: 49.5 us -> 74.7 us
  Pallas kernels: 732 us -> 713 us
    dot_general x30 -> x0, matrix products: 105 us -> none  [product(): return jnp.einsum(form, left, right, preferred_element_type=jnp.float32)]
    pallas_call x1, Pallas kernels: 387 us -> 308 us  [reduce_slots(): pl.pallas_call(reduce_kernel, out_shape=[room(2, width), jax.ShapeDtypeSt...]
    pallas_call x1 -> x11, Pallas kernels: 73.2 us -> 118 us  [call(): pl.pallas_call(body, grid_spec=pltpu.PrefetchScalarGridSpec(num_scalar_pr...]
    reduce_sum x24 -> x3, other arithmetic: 39.5 us -> 1.58 us  [the longest x1 0.8 us: normed(): inverse = lax.rsqrt(jnp.mean(centre * centre, -1, keepdims=True) + NORM_EPS)]
    reshape x18 -> x3, local copies, waits for them, and re-layouts: 36 us -> 1.36 us  [the longest x1 1.34 us: body(): vecs_two[:5].reshape(-1)]
    ppermute x16 -> x0, local copies, waits for them, and re-layouts: 27.6 us -> none  [the longest x12 21.3 us: pair_swap(): return lax.ppermute(value, 'dp', [(i, i ^ 4) for i in range(16)])]
    unnamed x386 -> x197, local copies, waits for them, and re-layouts: 59 us -> 32.6 us
    ppermute x16 -> x12, waiting for transfers between devices: 49.5 us -> 74.7 us  [pair_swap(): return lax.ppermute(value, 'dp', [(i, i ^ 4) for i in range(16)])]
  transfers between devices with their start and end apart: 24 -> 20, of which waited for: 8 -> 8; matrix products, arithmetic and copies ran while one was open for 14% -> 7% of each run, Pallas kernels for 60% -> 37%
where the time goes in v3:
time: 935 us; the launch traced here: 923 us
  Pallas kernels  713 us (76%)
  waiting for transfers between devices  74.7 us (8%)
  local copies, waits for them, and re-layouts  74.1 us (8%)
  other arithmetic  32.5 us (3%)
  starting transfers between devices  24.6 us (3%)
    pallas_call x1, Pallas kernels, reduce_slots(): pl.pallas_call(reduce_kernel, out_shape=[room(2, width), jax.ShapeDtypeSt...  308 us
    pallas_call x1, Pallas kernels, gather_slots(): pl.pallas_call(gather_kernel, out_shape=jax.ShapeDtypeStruct((16,) + scal...  263 us
    pallas_call x11, Pallas kernels, call(): pl.pallas_call(body, grid_spec=pltpu.PrefetchScalarGridSpec(num_scalar_pr...  118 us
    ppermute x12, waiting for transfers between devices, pair_swap(): return lax.ppermute(value, 'dp', [(i, i ^ 4) for i in range(16)])  74.7 us
    unnamed x197, local copies, waits for them, and re-layouts  32.6 us
    pallas_call x1, Pallas kernels, adam_slots(): pl.pallas_call(step, grid=(slot_count, 2), in_specs=[scalars, scalars] +...  24.2 us
  transfers between devices with their start and end apart: 20, of which 8 were waited for; matrix products, arithmetic and copies ran while one was open for 7% of the time, Pallas kernels for 37%

profile of v3, /device:TPU:9, one launch (start us, length us, event | category | flops | bytes accessed | tf_op | source)
XLA Modules:
  0.0 922.6 jit_solution(3568112119340042933)
XLA Ops:
  4.0 2.6 copy.52
  6.6 1.8 collective-permute-start.7
  12.0 3.7 fusion.own
  15.8 262.6 %shard_map.248 = bf16[16,9,1536,128]{3,2,1,0:T(8,128)(2,1)} custom-call(bf16[9,1536,128]{2,1,0:T(8,128)(2,1)S(1)} %fusion.own), custom_call_target="tpu_custom_call" | custom-call | tf_op jit(solution)/shard_map/pallas_call | solution.py:294
  279.1 2.1 gather_fusion.1
  281.2 1.6 collective-permute-start.10
  286.2 2.3 collective-permute-start.1
  288.7 10.7 %collective-permute-done.1 = bf16[130,1536]{1,0:T(8,128)(2,1)S(1)} collective-permute-done((bf16[130,1536]{1,0:T(8,128)(2,1)S(1)}, bf16[130,1536]{1,0:T(8,128)(2,1)S(1)}, u32[]{:S(2)}, u32[]{:S(2)}) %collective-permute-start.1) | collective-permute-done | bytes 399392 | tf_op jit(solution)/shard_map/ppermute | solution.py:111
  299.8 6.3 shard_map.249
  307.6 3.5 collective-permute-done.4.other_ref.sqo_ref
  311.1 11.1 %shard_map.250 = (bf16[272,768]{1,0:T(8,128)(2,1)S(1)}, bf16[272,768]{1,0:T(8,128)(2,1)S(1)}, bf16[6,272,128]{2,1,0:T(8,128)(2,1)S(1)}, bf16[272,1536]{1,0:T(8,128)(2,1)}) custom-call(s32[118]{0:T(128)S(1)} %multiply_add_fusion.3._, f32[2,272,768]{2,1,0:T(8,128)S(1)} %get-tuple-element.63.pre_ref, bf16[272,768]{1,0:T(8,128)(2,1)S(1)} %get-tuple-element.64.value_ref.v_ref, ...), custom_call_target="tpu_custom_call" | custom-call | tf_op jit(solution)/shard_map/pallas_call | solution.py:800
  322.7 1.8 broadcast_select_fusion.6
  325.6 2.8 broadcast_select_fusion
  328.4 1.7 copy.54.text_ref
  330.2 5.4 shard_map.251
  335.6 5.9 collective-permute-done.6.other_ref
  341.5 4.3 shard_map.252
  345.8 1.2 copy-done.35
  348.2 5.3 collective-permute-done.8.other_ref.sqo_ref
  353.5 10.3 %shard_map.253 = (bf16[272,768]{1,0:T(8,128)(2,1)S(1)}, bf16[512,768]{1,0:T(8,128)(2,1)S(1)}, bf16[6,272,128]{2,1,0:T(8,128)(2,1)S(1)}, bf16[272,1536]{1,0:T(8,128)(2,1)S(1)}) custom-call(s32[118]{0:T(128)S(1)} %multiply_add_fusion.3._, f32[272,768]{1,0:T(8,128)S(1)} %get-tuple-element.69.pre_ref, f32[512,768]{1,0:T(8,128)S(1)} %get-tuple-element.70.key_ref, ...), custom_call_target="tpu_custom_call" | custom-call | tf_op jit(solution)/shard_map/pallas_call | solution.py:800
  365.0 1.7 maximum_select_fusion.1
  366.7 1.4 pad_convert_fusion.cot_ref
  368.1 13.4 %collective-permute-done.9.other_ref = bf16[272,1536]{1,0:T(8,128)(2,1)S(1)} collective-permute-done((bf16[272,1536]{1,0:T(8,128)(2,1)S(1)}, bf16[272,1536]{1,0:T(8,128)(2,1)S(1)}, u32[]{:S(2)}, u32[]{:S(2)}) %collective-permute-start.9) | collective-permute-done | bytes 835616 | tf_op jit(solution)/shard_map/ppermute | solution.py:111
  381.4 28.3 %shard_map.254 = (f32[272,1536]{1,0:T(8,128)}, bf16[272,1536]{1,0:T(8,128)(2,1)S(1)}, bf16[272,1536]{1,0:T(8,128)(2,1)S(1)}, bf16[35,272,128]{2,1,0:T(8,128)(2,1...) custom-call(s32[118]{0:T(128)S(1)} %multiply_add_fusion.3._, ...), custom_call_target="tpu_custom_call" | custom-call | tf_op jit(solution)/shard_map/pallas_call | solution.py:800
  412.0 1.3 broadcast_select_fusion.3
  413.2 1.2 collective-permute-start.12
  414.4 1.4 copy.55
  415.8 2.6 pad_bitcast_fusion.5.refs_0_
  418.5 1.4 copy.57
  419.8 17.6 %collective-permute-done.12 = bf16[130,1536]{1,0:T(8,128)(2,1)S(1)} collective-permute-done((bf16[130,1536]{1,0:T(8,128)(2,1)S(1)}, bf16[130,1536]{1,0:T(8,128)(2,1)S(1)}, u32[]{:S(2)}, u32[]{:S(2)}) %collective-permute-start.12) | collective-permute-done | bytes 399392 | tf_op jit(solution)/shard_map/ppermute | solution.py:111
  438.3 3.1 add_convert_fusion
  441.3 1.4 collective-permute-start.13
  447.2 13.3 %shard_map.255 = (f32[272,1536]{1,0:T(8,128)S(1)}, bf16[272,1536]{1,0:T(8,128)(2,1)S(1)}, f32[272,768]{1,0:T(8,128)S(1)}, f32[512,768]{1,0:T(8,128)S(1)}, bf16[6...) custom-call(s32[118]{0:T(128)S(1)} %multiply_add_fusion.3._, f32[272,1536]{1,0:T(8,128)S(1)} %copy-done.3, ...), custom_call_target="tpu_custom_call" | custom-call | tf_op jit(solution)/shard_map/pallas_call | solution.py:800
  460.5 1.2 copy-done.36
  462.8 6.2 collective-permute-start.15
  469.0 1.3 pad_bitcast_fusion.3.refs_2_
  470.4 2.5 copy.59
  472.9 1.4 copy.60
  475.4 1.4 copy-done.41
  479.8 8.0 shard_map.256
  488.4 2.0 pad_bitcast_fusion
  491.1 1.8 broadcast_select_fusion.5
  492.9 1.4 copy.58
  494.4 2.7 pad_bitcast_fusion.2.refs_4_
  497.1 1.3 reshape.181
  498.4 10.2 %collective-permute-done.16.other_ref = bf16[272,1536]{1,0:T(8,128)(2,1)} collective-permute-done((bf16[272,1536]{1,0:T(8,128)(2,1)}, bf16[272,1536]{1,0:T(8,128)(2,1)}, u32[]{:S(2)}, u32[]{:S(2)}) %collective-permute-start.16) | collective-permute-done | bytes 835616 | tf_op jit(solution)/shard_map/ppermute | solution.py:111
  508.6 1.4 copy-done.37
  514.9 14.2 %shard_map.257 = (f32[272,1536]{1,0:T(8,128)S(1)}, bf16[272,1536]{1,0:T(8,128)(2,1)S(1)}, f32[2,272,768]{2,1,0:T(8,128)S(1)}, bf16[6,272,128]{2,1,0:T(8,128)(2,1)S(1)}, f32[272,128]{1,0:T(8,128)}) custom-call(s32[118]{0:T(128)S(1)} %multiply_add_fusion.3._, f32[272,1536]{1,0:T(8,128)S(1)} %copy-done.37, f32[272,1536]{1,0:T(8,128)S(1)} %copy-done.5, ...), custom_call_target="tpu_custom_call" | custom-call | tf_op jit(solution)/shard_map/pallas_call | solution.py:800
  529.1 1.2 copy-done.13
  532.0 1.2 copy-done.33
  533.7 2.3 copy.56
  536.0 2.8 pad_bitcast_fusion.4.refs_1_
  538.8 9.1 shard_map.258
  552.7 8.2 shard_map.259
  561.6 307.8 %shard_map.260 = (bf16[2,9,1536,128]{3,2,1,0:T(8,128)(2,1)}, f32[328,128]{1,0:T(8,128)}, bf16[16,9,768,128]{3,2,1,0:T(8,128)(2,1)}, bf16[4,9,768,128]{3,2,1,0:T(...) custom-call(s32[144]{0:T(256)} %gather_fusion.1, ...), custom_call_target="tpu_custom_call" | custom-call | tf_op jit(solution)/shard_map/pallas_call | solution.py:596
  869.4 1.7 slice.106
  871.1 1.6 reshape.185
  872.7 2.1 collective-permute-start.18
  874.8 1.9 multiply_subtract_fusion.1
  876.7 8.2 collective-permute-done.18
  885.5 1.4 multiply_add_fusion
  887.6 6.5 slice_bitcast_fusion
  895.1 24.2 %shard_map.261 = (f32[1,9,1536,128]{3,2,1,0:T(8,128)}, f32[1,9,1536,128]{3,2,1,0:T(8,128)}, f32[1,9,1536,128]{3,2,1,0:T(8,128)}) custom-call(f32[9]{0:T(128)} %copy-done.94, s32[9]{0:T(128)} %compare_convert_fusion.fill_ref, bf16[9,1536,128]{2,1,0:T(8,128)(2,1)} %get-tuple-element.132.refs_0_, bf16[9,1536,128]{2,1,0:T(8,128)(2,1)} %get-tuple-element.131.refs_1_, ...), custom_call_target="tpu_custom_call" | custom-call | tf_op jit(solution)/shard_map/pallas_call | solution.py:706
  920.0 2.1 broadcast_select_fusion.4
  (274 shorter events, 45.1 us)
Async XLA Ops:
  0.6 282.6 %copy-start = (f32[16,6,1536]{2,0,1:T(8,128)S(1)}, f32[16,6,1536]{2,0,1:T(8,128)}, u32[]{:S(2)}) copy-start(f32[16,6,1536]{2,0,1:T(8,128)} %param.23) | copy-start | bytes 1769476
  0.7 9.0 copy-start.97
  0.7 285.5 %collective-permute-start = (bf16[130,1536]{1,0:T(8,128)(2,1)}, bf16[130,1536]{1,0:T(8,128)(2,1)S(1)}, u32[]{:S(2)}, u32[]{:S(2)}) collective-permute-start(bf16[130,1536]{1,0:T(8,128)(2,1)} %param.17), channel_id=1, source_target_pairs={{1,8},{3,10},{5,12},{7,14},{8,1},{10,3},{12,5},{14,7},{17,24},{19,... | collective-permute-start | bytes 1198088 | tf_op jit(solution)/shard_map/ppermute | solution.py:134
  1.5 287.0 %collective-permute-start.3 = (f32[1,12160]{1,0:T(1,128)}, f32[1,12160]{1,0:T(1,128)S(1)}, u32[]{:S(2)}, u32[]{:S(2)}) collective-permute-start(f32[1,12160]{1,0:T(1,128)} %param.27), channel_id=1, source_target_pairs={{1,8},{3,10},{5,12},{7,14},{8,1},{10,3},{12,5},{14,7},{17,24},{19,... | collective-permute-start | bytes 145928 | tf_op jit(solution)/shard_map/ppermute | solution.py:134
  2.2 279.0 %collective-permute-start.2 = (s32[1]{0:T(128)}, s32[1]{0:T(128)}, u32[]{:S(2)}, u32[]{:S(2)}) collective-permute-start(s32[1]{0:T(128)} %param.21), channel_id=1, source_target_pairs={{1,8},{3,10},{5,12},{7,14},{8,1},{10,3},{12,5},{14,7},{17,24},{19,... | collective-permute-start | bytes 20 | tf_op jit(solution)/shard_map/ppermute | solution.py:134
  3.3 281.0 %collective-permute-start.5 = (s32[3,260]{1,0:T(4,128)}, s32[3,260]{1,0:T(4,128)S(1)}, u32[]{:S(2)}, u32[]{:S(2)}) collective-permute-start(s32[3,260]{1,0:T(4,128)} %param.20), channel_id=1, source_target_pairs={{1,8},{3,10},{5,12},{7,14},{8,1},{10,3},{12,5},{14,7},{17,24},{19,... | collective-permute-start | bytes 9368 | tf_op jit(solution)/shard_map/ppermute | solution.py:134
  6.6 319.1 %collective-permute-start.7 = (bf16[512,1536]{0,1:T(8,128)(2,1)}, bf16[512,1536]{0,1:T(8,128)(2,1)}, u32[]{:S(2)}, u32[]{:S(2)}) collective-permute-start(bf16[512,1536]{0,1:T(8,128)(2,1)} %copy.52), channel_id=1, source_target_pairs={{1,8},{3,10},{5,12},{7,14},{8,1},{10,3},{12,5},{14,7},{17,24},{19,... | collective-permute-start | bytes 4718600 | tf_op jit(solution)/shard_map/ppermute | solution.py:134
  15.8 262.7 %copy-start.29 = (f32[11,1536]{1,0:T(8,128)S(1)}, f32[11,1536]{1,0:T(8,128)}, u32[]{:S(2)}) copy-start(f32[11,1536]{1,0:T(8,128)} %shared_ref.7) | copy-start | bytes 202756
  278.4 5.9 copy-start.93
  281.2 41.5 %collective-permute-start.10 = (bf16[130,1536]{1,0:T(8,128)(2,1)}, bf16[130,1536]{1,0:T(8,128)(2,1)}, u32[]{:S(2)}, u32[]{:S(2)}) collective-permute-start(bf16[130,1536]{1,0:T(8,128)(2,1)} %param.19), channel_id=1, source_target_pairs={{1,8},{3,10},{5,12},{7,14},{8,1},{10,3},{12,5},{14,7},{17,24},{19,... | collective-permute-start | bytes 1198088 | tf_op jit(solution)/shard_map/ppermute | solution.py:134
  286.2 13.1 %collective-permute-start.1 = (bf16[130,1536]{1,0:T(8,128)(2,1)S(1)}, bf16[130,1536]{1,0:T(8,128)(2,1)S(1)}, u32[]{:S(2)}, u32[]{:S(2)}) collective-permute-start(bf16[130,1536]{1,0:T(8,128)(2,1)S(1)} %broadcast_select_fusion.7), channel_id=1, source_target_pairs={{0,8},{2,10},{4,12},{6,14},{8,0},{10,2},{12,4},{14,6},{16,24},{18,... | collective-permute-start | bytes 1198088 | tf_op jit(solution)/shard_map/ppermute | solution.py:111
  288.6 185.6 %copy-start.15 = (f32[10,768]{1,0:T(8,128)}, f32[10,768]{1,0:T(8,128)S(1)}, u32[]{:S(2)}) copy-start(f32[10,768]{1,0:T(8,128)S(1)} %reshape.178.vec_ref) | copy-start | bytes 92164
  299.8 47.5 %copy-start.2 = (f32[272,1536]{1,0:T(8,128)}, f32[272,1536]{1,0:T(8,128)S(1)}, u32[]{:S(2)}) copy-start(f32[272,1536]{1,0:T(8,128)S(1)} %pad_convert_fusion.1.rows_ref.x_ref) | copy-start | bytes 5013508
  299.8 6.7 copy-start.80
  306.1 16.1 %copy-start.6 = (f32[2,272,768]{2,1,0:T(8,128)}, f32[2,272,768]{2,1,0:T(8,128)S(1)}, u32[]{:S(2)}) copy-start(f32[2,272,768]{2,1,0:T(8,128)S(1)} %get-tuple-element.63.pre_ref) | copy-start | bytes 5013508
  306.1 16.1 %copy-start.38 = (bf16[272,768]{1,0:T(8,128)(2,1)}, bf16[272,768]{1,0:T(8,128)(2,1)S(1)}, u32[]{:S(2)}) copy-start(bf16[272,768]{1,0:T(8,128)(2,1)S(1)} %get-tuple-element.64.value_ref.v_ref) | copy-start | bytes 1253380
  306.1 16.1 %copy-start.48 = (bf16[272,1536]{1,0:T(8,128)(2,1)}, bf16[272,1536]{1,0:T(8,128)(2,1)S(1)}, u32[]{:S(2)}) copy-start(bf16[272,1536]{1,0:T(8,128)(2,1)S(1)} %get-tuple-element.92) | copy-start | bytes 2506756
  306.1 16.1 %copy-start.54 = (f32[272,128]{1,0:T(8,128)}, f32[272,128]{1,0:T(8,128)S(1)}, u32[]{:S(2)}) copy-start(f32[272,128]{1,0:T(8,128)S(1)} %get-tuple-element.65.sum_ref.sq_ref) | copy-start | bytes 417796
  306.1 4.9 collective-permute-start.4
  306.6 15.6 %copy-start.42 = (f32[272,128]{1,0:T(8,128)}, f32[272,128]{1,0:T(8,128)S(1)}, u32[]{:S(2)}) copy-start(f32[272,128]{1,0:T(8,128)S(1)} %pad.39.sin_ref) | copy-start | bytes 417796
  306.6 15.6 %copy-start.44 = (f32[272,128]{1,0:T(8,128)}, f32[272,128]{1,0:T(8,128)S(1)}, u32[]{:S(2)}) copy-start(f32[272,128]{1,0:T(8,128)S(1)} %pad.38.cos_ref) | copy-start | bytes 417796
  311.1 11.2 %copy-start.56 = (f32[272,128]{1,0:T(8,128)}, f32[272,128]{1,0:T(8,128)S(1)}, u32[]{:S(2)}) copy-start(f32[272,128]{1,0:T(8,128)S(1)} %collective-permute-done.4.other_ref.sqo_ref) | copy-start | bytes 417796
  322.3 19.2 %collective-permute-start.6 = (bf16[272,1536]{1,0:T(8,128)(2,1)}, bf16[272,1536]{1,0:T(8,128)(2,1)}, u32[]{:S(2)}, u32[]{:S(2)}) collective-permute-start(bf16[272,1536]{1,0:T(8,128)(2,1)} %get-tuple-element.66.part_ref), channel_id=1, source_target_pairs={{0,8},{2,10},{4,12},{6,14},{8,0},{10,2},{12,4},{14,6},{16,24},{18,... | collective-permute-start | bytes 2506760 | tf_op jit(solution)/shard_map/ppermute | solution.py:111
  324.5 40.5 %collective-permute-start.11 = (bf16[130,1536]{1,0:T(8,128)(2,1)}, bf16[130,1536]{1,0:T(8,128)(2,1)}, u32[]{:S(2)}, u32[]{:S(2)}) collective-permute-start(bf16[130,1536]{1,0:T(8,128)(2,1)} %broadcast_select_fusion.6), channel_id=1, source_target_pairs={{0,8},{2,10},{4,12},{6,14},{8,0},{10,2},{12,4},{14,6},{16,24},{18,... | collective-permute-start | bytes 1198088 | tf_op jit(solution)/shard_map/ppermute | solution.py:111
  330.2 11.4 %copy-start.30 = (f32[11,1536]{1,0:T(8,128)S(1)}, f32[11,1536]{1,0:T(8,128)}, u32[]{:S(2)}) copy-start(f32[11,1536]{1,0:T(8,128)} %shared_ref.7) | copy-start | bytes 202756
  335.6 17.8 %copy-start.8 = (f32[512,768]{1,0:T(8,128)}, f32[512,768]{1,0:T(8,128)S(1)}, u32[]{:S(2)}) copy-start(f32[512,768]{1,0:T(8,128)S(1)} %get-tuple-element.70.key_ref) | copy-start | bytes 4718596
  335.6 17.8 %copy-start.25 = (bf16[512,768]{1,0:T(8,128)(2,1)}, bf16[512,768]{1,0:T(8,128)(2,1)S(1)}, u32[]{:S(2)}) copy-start(bf16[512,768]{1,0:T(8,128)(2,1)S(1)} %get-tuple-element.71.value_ref.v_ref) | copy-start | bytes 2359300
  347.0 16.7 %copy-start.10 = (f32[272,768]{1,0:T(8,128)}, f32[272,768]{1,0:T(8,128)S(1)}, u32[]{:S(2)}) copy-start(f32[272,768]{1,0:T(8,128)S(1)} %get-tuple-element.69.pre_ref) | copy-start | bytes 2506756
  347.0 16.7 %copy-start.58 = (f32[272,128]{1,0:T(8,128)}, f32[272,128]{1,0:T(8,128)S(1)}, u32[]{:S(2)}) copy-start(f32[272,128]{1,0:T(8,128)S(1)} %get-tuple-element.72.sum_ref.sq_ref) | copy-start | bytes 417796
  347.0 6.5 collective-permute-start.8
  348.2 16.0 %copy-start.75 = (f32[130,1536]{1,0:T(8,128)}, f32[130,1536]{1,0:T(8,128)S(1)}, u32[]{:S(2)}) copy-start(f32[130,1536]{1,0:T(8,128)S(1)} %get-tuple-element.130) | copy-start | bytes 2396164
  353.5 10.3 %copy-start.60 = (f32[272,128]{1,0:T(8,128)}, f32[272,128]{1,0:T(8,128)S(1)}, u32[]{:S(2)}) copy-start(f32[272,128]{1,0:T(8,128)S(1)} %collective-permute-done.8.other_ref.sqo_ref) | copy-start | bytes 417796
  363.8 17.7 %collective-permute-start.9 = (bf16[272,1536]{1,0:T(8,128)(2,1)S(1)}, bf16[272,1536]{1,0:T(8,128)(2,1)S(1)}, u32[]{:S(2)}, u32[]{:S(2)}) collective-permute-start(bf16[272,1536]{1,0:T(8,128)(2,1)S(1)} %get-tuple-element.73.part_ref), channel_id=1, source_target_pairs={{0,8},{2,10},{4,12},{6,14},{8,0},{10,2},{12,4},{14,6},{16,24},{18,... | collective-permute-start | bytes 2506760 | tf_op jit(solution)/shard_map/ppermute | solution.py:111
  366.7 14.8 %copy-start.73 = (f32[1,4480]{1,0:T(1,128)S(1)}, f32[1,4480]{1,0:T(1,128)}, u32[]{:S(2)}) copy-start(f32[1,4480]{1,0:T(1,128)} %slice.125.bias_ref) | copy-start | bytes 53764
  381.4 33.0 %copy-start.95 = (f32[130]{0:T(256)S(1)}, f32[130]{0:T(256)}, u32[]{:S(2)}) copy-start(f32[130]{0:T(256)} %multiply_reduce_fusion.1) | copy-start | bytes 1564
  411.7 31.1 %collective-permute-start.14 = (bf16[272,1536]{1,0:T(8,128)(2,1)}, bf16[272,1536]{1,0:T(8,128)(2,1)}, u32[]{:S(2)}, u32[]{:S(2)}) collective-permute-start(bf16[272,1536]{1,0:T(8,128)(2,1)} %get-tuple-element.76.part_ref.da2), channel_id=1, source_target_pairs={{0,8},{2,10},{4,12},{6,14},{8,0},{10,2},{12,4},{14,6},{16,24},{18,... | collective-permute-start | bytes 2506760 | tf_op jit(solution)/shard_map/ppermute | solution.py:111
  413.2 24.3 %collective-permute-start.12 = (bf16[130,1536]{1,0:T(8,128)(2,1)S(1)}, bf16[130,1536]{1,0:T(8,128)(2,1)S(1)}, u32[]{:S(2)}, u32[]{:S(2)}) collective-permute-start(bf16[130,1536]{1,0:T(8,128)(2,1)S(1)} %broadcast_select_fusion.3), channel_id=1, source_target_pairs={{0,8},{2,10},{4,12},{6,14},{8,0},{10,2},{12,4},{14,6},{16,24},{18,... | collective-permute-start | bytes 1198088 | tf_op jit(solution)/shard_map/ppermute | solution.py:111
  418.5 19.8 %copy-start.89 = (f32[1536]{0:T(1024)S(1)}, f32[1536]{0:T(1024)}, u32[]{:S(2)}) copy-start(f32[1536]{0:T(1024)} %get-tuple-element.118) | copy-start | bytes 18436
  418.5 19.8 %copy-start.90 = (f32[1536]{0:T(1024)S(1)}, f32[1536]{0:T(1024)}, u32[]{:S(2)}) copy-start(f32[1536]{0:T(1024)} %slice_reduce_fusion.2) | copy-start | bytes 18436
  441.3 49.8 %collective-permute-start.13 = (bf16[130,1536]{1,0:T(8,128)(2,1)}, bf16[130,1536]{1,0:T(8,128)(2,1)}, u32[]{:S(2)}, u32[]{:S(2)}) collective-permute-start(bf16[130,1536]{1,0:T(8,128)(2,1)} %add_convert_fusion), channel_id=1, source_target_pairs={{1,8},{3,10},{5,12},{7,14},{8,1},{10,3},{12,5},{14,7},{17,24},{19,... | collective-permute-start | bytes 1198088 | tf_op jit(solution)/shard_map/ppermute | solution.py:134
  447.2 21.8 %copy-start.77 = (bf16[272,1536]{0,1:T(8,128)(2,1)S(1)}, bf16[272,1536]{0,1:T(8,128)(2,1)}, u32[]{:S(2)}) copy-start(bf16[272,1536]{0,1:T(8,128)(2,1)} %copy.57) | copy-start | bytes 2506756
  462.8 7.5 copy-start.20
  462.8 7.5 copy-start.27
  462.8 7.5 copy-start.46
  462.8 11.4 %collective-permute-start.15 = (f32[272,128]{1,0:T(8,128)}, f32[272,128]{1,0:T(8,128)}, u32[]{:S(2)}, u32[]{:S(2)}) collective-permute-start(f32[272,128]{1,0:T(8,128)} %get-tuple-element.83.sum_ref), channel_id=1, source_target_pairs={{0,8},{2,10},{4,12},{6,14},{8,0},{10,2},{12,4},{14,6},{16,24},{18,... | collective-permute-start | bytes 417800 | tf_op jit(solution)/shard_map/ppermute | solution.py:111
  479.8 8.7 copy-start.78
  479.8 8.7 copy-start.79
  487.8 20.9 %collective-permute-start.16 = (bf16[272,1536]{1,0:T(8,128)(2,1)}, bf16[272,1536]{1,0:T(8,128)(2,1)}, u32[]{:S(2)}, u32[]{:S(2)}) collective-permute-start(bf16[272,1536]{1,0:T(8,128)(2,1)} %get-tuple-element.84.part_ref.da3), channel_id=1, source_target_pairs={{0,8},{2,10},{4,12},{6,14},{8,0},{10,2},{12,4},{14,6},{16,24},{18,... | collective-permute-start | bytes 2506760 | tf_op jit(solution)/shard_map/ppermute | solution.py:111
  492.9 15.7 %copy-start.7 = (f32[2,272,768]{2,1,0:T(8,128)S(1)}, f32[2,272,768]{2,1,0:T(8,128)}, u32[]{:S(2)}) copy-start(f32[2,272,768]{2,1,0:T(8,128)} %copy-done.6) | copy-start | bytes 5013508
  494.3 14.3 %copy-start.5 = (f32[272,1536]{1,0:T(8,128)S(1)}, f32[272,1536]{1,0:T(8,128)}, u32[]{:S(2)}) copy-start(f32[272,1536]{1,0:T(8,128)} %copy-done.4) | copy-start | bytes 5013508
  494.3 14.3 %copy-start.16 = (f32[10,768]{1,0:T(8,128)S(1)}, f32[10,768]{1,0:T(8,128)}, u32[]{:S(2)}) copy-start(f32[10,768]{1,0:T(8,128)} %copy-done.15) | copy-start | bytes 92164
  533.2 5.6 collective-permute-start.17
  538.8 11.6 %copy-start.96 = (pred[2]{0:T(512)(128)(4,1)S(1)}, pred[2]{0:T(512)(128)(4,1)}, u32[]{:S(2)}) copy-start(pred[2]{0:T(512)(128)(4,1)} %iota_compare_fusion.5) | copy-start | bytes 10
  561.5 313.2 %copy-start.84 = (f32[1,12160]{1,0:T(1,128)S(1)}, f32[1,12160]{1,0:T(1,128)}, u32[]{:S(2)}) copy-start(f32[1,12160]{1,0:T(1,128)} %param.27) | copy-start | bytes 145924
  561.5 313.2 %copy-start.88 = (f32[1,12160]{1,0:T(1,128)S(1)}, f32[1,12160]{1,0:T(1,128)}, u32[]{:S(2)}) copy-start(f32[1,12160]{1,0:T(1,128)} %param.28) | copy-start | bytes 145924
  561.5 323.3 %copy-start.76 = (f32[130,1536]{1,0:T(8,128)S(1)}, f32[130,1536]{1,0:T(8,128)}, u32[]{:S(2)}) copy-start(f32[130,1536]{1,0:T(8,128)} %copy-done.75) | copy-start | bytes 2396164
  561.6 323.3 %copy-start.87 = (f32[1536]{0:T(1024)S(1)}, f32[1536]{0:T(1024)}, u32[]{:S(2)}) copy-start(f32[1536]{0:T(1024)} %get-tuple-element.117) | copy-start | bytes 18436
  561.6 323.3 %copy-start.92 = (f32[130]{0:T(256)S(1)}, f32[130]{0:T(256)}, u32[]{:S(2)}) copy-start(f32[130]{0:T(256)} %copy-done.91) | copy-start | bytes 1564
  869.4 16.1 %copy-start.14 = (f32[272,1536]{1,0:T(8,128)S(1)}, f32[272,1536]{1,0:T(8,128)}, u32[]{:S(2)}) copy-start(f32[272,1536]{1,0:T(8,128)} %copy-done.13) | copy-start | bytes 5013508
  872.7 12.2 %collective-permute-start.18 = (bf16[130,1536]{1,0:T(8,128)(2,1)}, bf16[130,1536]{1,0:T(8,128)(2,1)S(1)}, u32[]{:S(2)}, u32[]{:S(2)}) collective-permute-start(bf16[130,1536]{1,0:T(8,128)(2,1)} %broadcast_select_fusion.1), channel_id=1, source_target_pairs={{0,8},{2,10},{4,12},{6,14},{8,0},{10,2},{12,4},{14,6},{16,24},{18,... | collective-permute-start | bytes 1198088 | tf_op jit(solution)/shard_map/ppermute | solution.py:111
  886.9 33.1 %collective-permute-start.19 = (f32[130,1536]{1,0:T(8,128)}, f32[130,1536]{1,0:T(8,128)S(1)}, u32[]{:S(2)}, u32[]{:S(2)}) collective-permute-start(f32[130,1536]{1,0:T(8,128)} %multiply_add_fusion), channel_id=1, source_target_pairs={{1,8},{3,10},{5,12},{7,14},{8,1},{10,3},{12,5},{14,7},{17,24},{19,... | collective-permute-start | bytes 2396168 | tf_op jit(solution)/shard_map/ppermute | solution.py:134
  895.0 24.2 %copy-start.85 = (f32[11,1536]{1,0:T(8,128)S(1)}, f32[11,1536]{1,0:T(8,128)}, u32[]{:S(2)}) copy-start(f32[11,1536]{1,0:T(8,128)} %param.31) | copy-start | bytes 202756
  895.0 24.2 %copy-start.86 = (f32[11,1536]{1,0:T(8,128)S(1)}, f32[11,1536]{1,0:T(8,128)}, u32[]{:S(2)}) copy-start(f32[11,1536]{1,0:T(8,128)} %param.32) | copy-start | bytes 202756
  895.1 27.1 %copy-start.1 = (f32[16,6,1536]{2,0,1:T(8,128)S(1)}, f32[16,6,1536]{2,0,1:T(8,128)}, u32[]{:S(2)}) copy-start(f32[16,6,1536]{2,0,1:T(8,128)} %param.23) | copy-start | bytes 1769476
  (54 other events, 106.3 us)

commit v4 on v3

--- a/solution.py
+++ b/solution.py
@@ -122,19 +122,6 @@
     return tuple(out)
 
 
-def home_swap(*values):
-    if not chip_pairs():
-        return values
-    chip, core = lax.axis_index("dp"), lax.axis_index("tensor")
-    away = (chip // 4) % 2 != core
-    order = [
-        (d * 2 + c, (d ^ 4) * 2 + 1 - c) for d in range(16) for c in range(2) if (d // 4) % 2 != c
-    ]
-    return tuple(
-        jnp.where(away, lax.ppermute(v, ("dp", "tensor"), order), v) for v in values
-    )
-
-
 def place_of():
     chip, core = lax.axis_index("dp"), lax.axis_index("tensor")
     z, y, x = chip // 4, (chip // 2) % 2, chip % 2
@@ -164,7 +151,11 @@
     pl.semaphore_wait(barrier, len(friends))
 
 
-def gather_kernel(own, out, near_s, local_s, col_r, x_s, x_r, y_s, y_r, ra_s, ra_r, rb_s, rb_r, sib_s, sib_r):
+def gather_kernel(
+    own, lat, cot, text, small, out, lats, cots, texts, smalls, clip_s, clip_r,
+    near_s, col_r,
+    x_s, x_r, y_s, y_r, ra_s, ra_r, rb_s, rb_r, sib_s, sib_r,
+):
     chip, core, z, y, x = place_of()
     rank = z % 2
     half = own.shape[1] // 2
@@ -211,6 +202,63 @@
                 go.start()
                 started.append((go, None))
 
+    pair_chip = column_of(z, y, x, 1)
+    rows_of_text = text.shape[0] // 2
+
+    def clip_pieces(h):
+        share = pl.ds(h * rows_of_text, rows_of_text)
+        return ((lat, lats.at[h]), (cot, cots.at[h]), (text.at[share], texts.at[share]))
+
+    home = rank == core
+    trade = pltpu.make_async_remote_copy(
+        src_ref=small, dst_ref=smalls, send_sem=clip_s.at[6], recv_sem=clip_r.at[6],
+        device_id=(pair_chip, 1 - core), device_id_type=MESH,
+    )
+    keep = pltpu.make_async_copy(small, smalls, clip_r.at[6])
+
+    @pl.when(home)
+    def _():
+        keep.start()
+
+    @pl.when(jnp.logical_not(home))
+    def _():
+        trade.start()
+
+    def hand_out(h, n, wait):
+        src, dst = clip_pieces(h)[n]
+        far = pltpu.make_async_remote_copy(
+            src_ref=src, dst_ref=dst, send_sem=clip_s.at[n], recv_sem=clip_r.at[3 * h + n],
+            device_id=(pair_chip, rank), device_id_type=MESH,
+        )
+        near = pltpu.make_async_remote_copy(
+            src_ref=src, dst_ref=dst, send_sem=clip_s.at[3 + n], recv_sem=clip_r.at[3 * h + n],
+            device_id=(chip, 1 - core), device_id_type=MESH,
+        )
+        here = pltpu.make_async_copy(src, dst, clip_r.at[3 * h + n])
+
+        @pl.when(core == h)
+        def _():
+            if wait:
+                far.wait_send()
+            else:
+                far.start()
+
+            @pl.when(home)
+            def _():
+                if not wait:
+                    here.start()
+
+            @pl.when(jnp.logical_not(home))
+            def _():
+                if wait:
+                    near.wait_send()
+                else:
+                    near.start()
+
+    for n in range(3):
+        for h in range(2):
+            hand_out(h, n, False)
+
     def column_in(k):
         unit = column_of(z, y, x, k)
         source_z = unit // 4
@@ -270,6 +318,18 @@
             def _():
                 go.wait_send()
 
+    for n in range(3):
+        for h in range(2):
+            hand_out(h, n, True)
+            dst = clip_pieces(h)[n][1]
+            pltpu.make_async_copy(dst, dst, clip_r.at[3 * h + n]).wait()
+
+    @pl.when(jnp.logical_not(home))
+    def _():
+        trade.wait_send()
+
+    pltpu.make_async_copy(smalls, smalls, clip_r.at[6]).wait()
+
     other = (1 - core) * half
     for k in range(4):
         for at, (yy, xx) in ((0, (y, x)), (4, (y, 1 - x)), (8, (1 - y, x))):
@@ -286,22 +346,30 @@
         ).wait_recv()
 
 
-def gather_slots(scaled):
+def gather_slots(scaled, lat, cot, text, small):
     if not chip_pairs():
-        return lax.all_gather(scaled, "dp", axis=0, tiled=True)
+        everyone = lax.all_gather(scaled, "dp", axis=0, tiled=True)
+        lats, cots = (lax.all_gather(v, "tensor") for v in (lat, cot))
+        return everyone, lats, cots, text, small
     dma = pltpu.SemaphoreType.DMA
-    counts = (4, 1, 4, 4, 4, 4, 4, 4, 4, 4, 4, 20, 20)
-    everyone = pl.pallas_call(
+    counts = (7, 7, 4, 4, 4, 4, 4, 4, 4, 4, 4, 4, 20, 20)
+    everyone, *rest = pl.pallas_call(
         gather_kernel,
-        out_shape=jax.ShapeDtypeStruct((16,) + scaled.shape, scaled.dtype),
-        in_specs=[ANY],
-        out_specs=ANY,
+        out_shape=[
+            jax.ShapeDtypeStruct((16,) + scaled.shape, scaled.dtype),
+            jax.ShapeDtypeStruct((2,) + lat.shape, lat.dtype),
+            jax.ShapeDtypeStruct((2,) + cot.shape, cot.dtype),
+            jax.ShapeDtypeStruct(text.shape, text.dtype),
+            jax.ShapeDtypeStruct(small.shape, small.dtype),
+        ],
+        in_specs=[ANY] * 5,
+        out_specs=[ANY] * 5,
         scratch_shapes=[dma((n,)) for n in counts],
         compiler_params=pltpu.CompilerParams(
             collective_id=0, has_side_effects=True, vmem_limit_bytes=4 * MIB
         ),
-    )(scaled)
-    return everyone.reshape((-1,) + scaled.shape[1:])
+    )(scaled, lat, cot, text, small)
+    return everyone.reshape((-1,) + scaled.shape[1:]), *rest
 
 
 def toggled(z, y, x, flip_y, flip_x, k):
@@ -314,10 +382,11 @@
     kind, block, *refs,
 ):
     (
-        *pieces, vec_in,
-        final, vec_out, from_sib, from_x, from_y, corner_a, corner_b,
+        *pieces, rows_in, after_in, dx_in, y_in, da_in, gains, vec_in,
+        final, vec_out, result, result_grad, y_other, da_other, from_sib, from_x, from_y, corner_a, corner_b,
         left, right, ring, corners, side_x, side_y, middle, stage, vec_box,
         load_s, stage_s, sib_s, sib_r, x_s, x_r, y_s, y_r, ca_s, ca_r, cb_s, cb_r, f_s, f_r, v_s, v_r,
+        end_s, end_r,
     ) = refs
     chip, core, z, y, x = place_of()
     rank = z % 2
@@ -517,6 +586,39 @@
         def _():
             go.start()
 
+    home = rank == core
+    pair_device = (toggled(z, y, x, 0, 0, 1), core)
+    ends = [
+        remote(y_in, y_other, end_s.at[0], end_r.at[0], pair_device),
+        remote(da_in, da_other, end_s.at[1], end_r.at[1], pair_device),
+        remote(result, result, end_s.at[2], end_r.at[2], sibling),
+        remote(result_grad, result_grad, end_s.at[3], end_r.at[3], sibling),
+    ]
+
+    def finish_rows():
+        ends[0].wait_recv()
+        ends[1].wait_recv()
+        tall = 16
+        spec = pl.BlockSpec((tall, width), lambda i: (i, 0))
+
+        def one(x_ref, x2_ref, dx_ref, y_ref, yo_ref, da_ref, dao_ref, out_ref, grad_ref):
+            y_all = y_ref[...].astype(F32) + yo_ref[...].astype(F32) + gains[2:3]
+            out_ref[...] = (x2_ref[...] + gains[0:1] * y_all).astype(out_ref.dtype)
+            da = da_ref[...].astype(F32) + dao_ref[...].astype(F32)
+            back, _ = normed_back(x_ref[...], da * (1.0 + gains[1:2]))
+            grad_ref[...] = dx_ref[...] + back
+
+        pltpu.emit_pipeline(
+            one, grid=(rows_in.shape[0] // tall,), in_specs=[spec] * 7, out_specs=[spec] * 2
+        )(rows_in, after_in, dx_in, y_in, y_other, da_in, da_other, result, result_grad)
+        ends[2].start()
+        ends[3].start()
+
+    @pl.when(jnp.logical_not(home))
+    def _():
+        ends[0].start()
+        ends[1].start()
+
     def vec_copy(i):
         return remote(vec_out, vec_box.at[i], v_s.at[i], v_r.at[i], mates[i])
 
@@ -535,6 +637,10 @@
         @pl.when(jnp.logical_and(step >= 1, step < 5))
         def _():
             sides(4 - step)
+
+        @pl.when(jnp.logical_and(step == 4, home))
+        def _():
+            finish_rows()
 
         @pl.when(step >= 2)
         def _():
@@ -559,9 +665,18 @@
         y_copy(k).wait_send()
     f_copy(1)[0].wait_send()
 
-    @pl.when(rank != core)
+    @pl.when(home)
+    def _():
+        ends[2].wait_send()
+        ends[3].wait_send()
+
+    @pl.when(jnp.logical_not(home))
     def _():
         f_copy(0)[0].wait_send()
+        ends[0].wait_send()
+        ends[1].wait_send()
+        ends[2].wait_recv()
+        ends[3].wait_recv()
 
     for plane in range(2):
         for h in range(2):
@@ -569,11 +684,17 @@
             pltpu.make_async_copy(piece, piece, f_r.at[2 * plane + h]).wait()
 
 
-def reduce_slots(holder, kinds, rows, columns, vector, slot_count):
+def reduce_slots(holder, kinds, rows, columns, vector, ends, gains, slot_count):
     if not chip_pairs():
         grads = slot_grads(holder, kinds, rows, columns)
         total = lax.psum_scatter(grads, "dp", scatter_dimension=0, tiled=True)
-        return [total], lax.psum(vector, ("dp", "tensor"))
+        x, after, dx, y_part, da_part = ends
+        y_all, da_all = (
+            v.astype(F32) + pair_swap(v).astype(F32) for v in (y_part, da_part)
+        )
+        result = (after + gains[0] * (y_all + gains[2])).astype(BF16)
+        back, _ = normed_back(x, da_all * (1.0 + gains[1]))
+        return total[None], lax.psum(vector, ("dp", "tensor")), result, dx + back
     depth = max(r.shape[0] for r in rows)
     left = [jnp.pad(r, ((0, depth - r.shape[0]), (0, 0))).T for r in rows]
     lanes = columns[0].shape[2]
@@ -597,23 +718,25 @@
         reduce_kernel,
         out_shape=[
             room(2, width), jax.ShapeDtypeStruct(vector.shape, vector.dtype),
+            jax.ShapeDtypeStruct(ends[0].shape, low), jax.ShapeDtypeStruct(ends[0].shape, F32),
+            jax.ShapeDtypeStruct(ends[0].shape, low), jax.ShapeDtypeStruct(ends[0].shape, low),
             room(16, half), room(4, half), room(4, half),
             room(4, half // 2), room(4, half // 2),
         ],
-        in_specs=[scalars, scalars] + [ANY] * (len(left) + len(columns)) + [inside],
-        out_specs=[ANY, inside] + [ANY] * 5,
+        in_specs=[scalars, scalars] + [ANY] * (len(left) + len(columns) + 5) + [inside] * 2,
+        out_specs=[ANY, inside] + [ANY] * 9,
         scratch_shapes=[
             pltpu.VMEM((len(left), width, depth), low),
             pltpu.VMEM((tiles + 1, depth, lanes), low),
             slab(2), slab(2), slab(2), slab(2), slab(2), slab(3),
             pltpu.VMEM((5,) + vector.shape, vector.dtype),
         ]
-        + [dma((n,)) for n in (len(left) + len(columns), 4, 16, 16) + (4,) * 10 + (5, 5)],
+        + [dma((n,)) for n in (len(left) + len(columns), 4, 16, 16) + (4,) * 10 + (5, 5, 4, 4)],
         compiler_params=pltpu.CompilerParams(
             collective_id=1, has_side_effects=True, vmem_limit_bytes=58 * MIB
         ),
-    )(kind, block, *left, *columns, vector)
-    return [outs[0][0], outs[0][1]], outs[1]
+    )(kind, block, *left, *columns, *ends, gains, vector)
+    return outs[:4]
 
 
 def kind_of_blocks(tile_count, heads_here, blocks_here):
@@ -673,21 +796,17 @@
     )(kind, block, used, left, right)
 
 
-def adam_slots(parts, master, moment_one, moment_two, slot_scale, filled):
-    slot_count, width, lanes = master.shape[1:]
-    count = len(parts)
-    tall = width // 2
-
-    def step(scale_ref, fill_ref, *refs):
-        grads = refs[:count]
-        weight, one, two, new_weight, new_one, new_two = refs[count:]
+def adam_slots(planes, master, moment_one, moment_two, slot_scale, filled):
+    count, slot_count, width, lanes = planes.shape
+
+    def step(scale_ref, fill_ref, grads, weight, one, two, new_weight, new_one, new_two):
         slot = pl.program_id(0)
 
         @pl.when(fill_ref[slot] == 1)
         def _():
-            total = grads[0][0].astype(jnp.float32)
-            for more in grads[1:]:
-                total = total + more[0].astype(jnp.float32)
+            total = grads[0, 0].astype(jnp.float32)
+            for n in range(1, count):
+                total = total + grads[n, 0].astype(jnp.float32)
             results = adam_step(
                 weight[0, 0], total * scale_ref[slot], one[0, 0], two[0, 0], TILE_RATE, TILE_DECAY
             )
@@ -700,16 +819,17 @@
             new_one[...] = one[...]
             new_two[...] = two[...]
 
-    flat = pl.BlockSpec((1, tall, lanes), lambda s, i: (s, i, 0))
-    deep = pl.BlockSpec((1, 1, tall, lanes), lambda s, i: (0, s, i, 0))
+    deep = pl.BlockSpec((1, 1, width, lanes), lambda s: (0, s, 0, 0))
     scalars = pl.BlockSpec(memory_space=pltpu.SMEM)
     return pl.pallas_call(
         step,
-        grid=(slot_count, 2),
-        in_specs=[scalars, scalars] + [flat] * count + [deep] * 3,
+        grid=(slot_count,),
+        in_specs=[scalars, scalars, pl.BlockSpec((count, 1, width, lanes), lambda s: (0, s, 0, 0))]
+        + [deep] * 3,
         out_specs=[deep] * 3,
         out_shape=[jax.ShapeDtypeStruct(master.shape, jnp.float32)] * 3,
-    )(slot_scale, filled.astype(jnp.int32), *parts, master, moment_one, moment_two)
+        compiler_params=pltpu.CompilerParams(vmem_limit_bytes=32 * MIB),
+    )(slot_scale, filled.astype(jnp.int32), planes, master, moment_one, moment_two)
 
 
 SCALING = HEAD ** (-0.5)
@@ -1369,45 +1489,44 @@
     scales = tile_scales(tile_count, heads_here, blocks_here)
     my_slots = lax.dynamic_slice_in_dim(holder, lax.axis_index("dp") * slot_count, slot_count)
     rank = pair_rank()
-    latents, context, cotangent, positions, step_ids, head_here = home_swap(
-        latents, context, cotangent, positions, step_ids, head_params
-    )
     filled = my_slots >= 0
     slot_scale = jnp.where(filled, scales[jnp.maximum(my_slots, 0)], 0.0)
     scaled = (master[0] * slot_scale[:, None, None]).astype(jnp.bfloat16)
-    everyone = gather_slots(scaled)
-    vectors = head_here[0]
-    vecs = vectors[: 10 * width_here].reshape(10, width_here)
-    up_bias = vectors[10 * width_here :].reshape(1, -1)
-    chosen = (step_ids[0] == jnp.arange(TSTEPS)).astype(jnp.float32)
-    mod = shared_params[5:11] + jnp.einsum(
-        "s,skd->kd", chosen, time_table, precision=lax.Precision.HIGHEST
-    )
     half = latents.shape[0]
     tokens = 2 * half
     count = -(-tokens // 16) * 16
+    taller = ((0, -half % 16), (0, 0))
+    small = jnp.concatenate(
+        [
+            head_params[0],
+            positions.reshape(-1).astype(jnp.float32),
+            step_ids.astype(jnp.float32),
+        ]
+    )
+    packed = jnp.pad(small, (0, -small.shape[0] % 1024)).reshape(-1, HEAD)
+    everyone, lats, cots, context, packed = gather_slots(
+        scaled, jnp.pad(latents, taller), jnp.pad(cotangent, taller), context, packed
+    )
+    small = packed.reshape(-1)
+    vectors = small[: head_params.shape[1]]
+    small = small[head_params.shape[1] :]
+    positions = small[: positions.size].reshape(positions.shape)
+    step = small[positions.size]
+    vecs = vectors[: 10 * width_here].reshape(10, width_here)
+    up_bias = vectors[10 * width_here :].reshape(1, -1)
+    chosen = (step == jnp.arange(TSTEPS)).astype(jnp.float32)
+    mod = shared_params[5:11] + jnp.einsum(
+        "s,skd->kd", chosen, time_table, precision=lax.Precision.HIGHEST
+    )
     cos_tab, sin_tab = rope_tables(positions, HEAD)
     sin_tab = jnp.where(jnp.arange(HEAD) % 2 == 0, -sin_tab, sin_tab)
     cos_tab, sin_tab = (jnp.pad(t, ((0, count - tokens), (0, 0))) for t in (cos_tab, sin_tab))
 
-    def all_rows(local_rows):
-        other = pair_swap(local_rows)
-        rows = jnp.where(
-            rank == 0,
-            jnp.concatenate([local_rows, other], 0),
-            jnp.concatenate([other, local_rows], 0),
-        )
+    def all_rows(halves):
+        rows = jnp.concatenate([halves[0, :half], halves[1, :half]], 0)
         return jnp.pad(rows, ((0, count - tokens), (0, 0))).astype(jnp.float32)
 
-    def own_rows(rows):
-        return jnp.where(rank == 0, rows[:half], rows[half:tokens])
-
-    def merged_rows(part):
-        theirs = pair_swap(jnp.where(rank == 0, part[half:tokens], part[:half]))
-        return own_rows(part).astype(jnp.float32) + theirs.astype(jnp.float32)
-
-    rows = all_rows(latents)
-    cot = all_rows(cotangent)
+    rows, cot = all_rows(lats), all_rows(cots)
     low_one, pre_one, value_one, squares_one = project_self(
         places, everyone, rows, mod, vecs, heads_here
     )
@@ -1450,10 +1569,6 @@
         places, rows, after_one, after_two, (grad_one, grad_two, grad_three), dx_one,
         branch_one, cot, (da_one, da_three, da_two), y_three, shared_params,
     )
-    result = own_rows(after_two) + mod[5] * (merged_rows(y_three) + shared_params[2])
-    output = result.astype(jnp.bfloat16)
-    back, _ = normed_back(own_rows(rows), merged_rows(da_one) * (1.0 + mod[1]))
-    grad_input = own_rows(dx_one) + back
     head_grad = jnp.concatenate(
         [vecs_one[:5].reshape(-1), vecs_two[:5].reshape(-1), d_up_bias.reshape(-1)]
     )
@@ -1461,7 +1576,7 @@
     head_padded = jnp.where(jnp.arange(tensors)[:, None] == rank, head_grad[None, :], 0.0)
     vector = jnp.concatenate([head_padded.reshape(-1), shared_grad.reshape(-1)])
     vector = jnp.pad(vector, (0, -vector.shape[0] % 1024)).reshape(-1, 128)
-    parts, vector = reduce_slots(
+    parts, vector, output, grad_input = reduce_slots(
         holder,
         kind_of_blocks(tile_count, heads_here, blocks_here),
         (low_one, grad_one, low_two, context, grad_two, low_three, grad_three),
@@ -1478,7 +1593,13 @@
             hidden,
         ),
         vector,
+        (rows, after_two, dx_one, y_three, da_one),
+        jnp.concatenate([mod[5:6], mod[1:2], shared_params[2:3], jnp.zeros((5, D), F32)], 0),
         slot_count,
+    )
+    output, grad_input = (
+        jnp.where(lax.axis_index("tensor") == 0, v[:half], v[half:tokens])
+        for v in (output, grad_input)
     )
     new_master, new_first, new_second = adam_slots(
         parts, master, first_moment, second_moment, slot_scale, filled
@@ -1494,7 +1615,6 @@
     new_shared, new_shared_first, new_shared_second = adam_step(
         shared_params, shared_total, shared_first, shared_second, VECTOR_RATE, 0.0
     )
-    output, grad_input = home_swap(output, grad_input)
     return (
         output,
         grad_input,

time: 935 us -> 856 us (0.916)
  Pallas kernels: 713 us -> 680 us
  waiting for transfers between devices: 74.7 us -> 42 us
  local copies, waits for them, and re-layouts: 74.1 us -> 91.7 us
  other arithmetic: 32.5 us -> 19.3 us
  starting transfers between devices: 24.6 us -> 14.6 us
    pallas_call x2, Pallas kernels: 287 us -> 253 us  [the longest x1 240 us: gather_slots(): pl.pallas_call(gather_kernel, out_shape=[jax.ShapeDtypeStruct((16,) + sca...]
    ppermute x12 -> x8, waiting for transfers between devices: 74.7 us -> 42 us  [pair_swap(): return lax.ppermute(value, 'dp', [(i, i ^ 4) for i in range(16)])]
    unnamed x197 -> x216, local copies, waits for them, and re-layouts: 32.6 us -> 51.9 us
    select_n x11 -> x2, other arithmetic: 13.3 us -> 3.32 us  [body(): jnp.where(lax.axis_index('tensor') == 0, v[:half], v[half:tokens])]
  transfers between devices with their start and end apart: 20 -> 8, of which waited for: 8 -> 6; matrix products, arithmetic and copies ran while one was open for 7% -> 5% of each run, Pallas kernels for 37% -> 1%
where the time goes in v4:
time: 856 us; the launch traced here: 851 us
  Pallas kernels  680 us (79%)
  local copies, waits for them, and re-layouts  91.7 us (11%)
  waiting for transfers between devices  42 us (5%)
  other arithmetic  19.3 us (2%)
  starting transfers between devices  14.6 us (2%)
    pallas_call x1, Pallas kernels, reduce_slots(): pl.pallas_call(reduce_kernel, out_shape=[room(2, width), jax.ShapeDtypeSt...  309 us
    pallas_call x1, Pallas kernels, gather_slots(): pl.pallas_call(gather_kernel, out_shape=[jax.ShapeDtypeStruct((16,) + sca...  240 us
    pallas_call x11, Pallas kernels, call(): pl.pallas_call(body, grid_spec=pltpu.PrefetchScalarGridSpec(num_scalar_pr...  118 us
    unnamed x216, local copies, waits for them, and re-layouts  51.9 us
    ppermute x8, waiting for transfers between devices, pair_swap(): return lax.ppermute(value, 'dp', [(i, i ^ 4) for i in range(16)])  42 us
  transfers between devices with their start and end apart: 8, of which 6 were waited for; matrix products, arithmetic and copies ran while one was open for 5% of the time, Pallas kernels for 1%

profile of v4, /device:TPU:9, one launch (start us, length us, event | category | flops | bytes accessed | tf_op | source)
XLA Modules:
  0.0 850.8 jit_solution(1929225829470984640)
XLA Ops:
  3.8 1.0 pad.48.lat
  5.9 3.8 fusion.own
  9.8 240.1 %shard_map.248 = (bf16[16,9,1536,128]{3,2,1,0:T(8,128)(2,1)}, bf16[2,144,1536]{2,1,0:T(8,128)(2,1)S(1)}, bf16[2,144,1536]{2,1,0:T(8,128)(2,1)S(1)}, bf16[512,1536]{1,0:T(8,128)(2,1)S(1)}, f32[104,128]{1,0:T(8,128)S(1)}) custom-call(bf16[9,1536,128]{2,1,0:T(8,128)(2,1)S(1)} %fusion.own, bf16[144,1536]{1,0:T(8,128)(2,1)S(1)} %pad.48.lat, ...), custom_call_target="tpu_custom_call" | custom-call | tf_op jit(solution)/shard_map/pallas_call | solution.py:356
  250.0 1.2 copy-done.19
  253.0 1.0 fusion.15
  254.0 6.2 shard_map.249
  260.3 1.2 copy-done.7
  261.4 11.6 %collective-permute-start = (f32[272,128]{1,0:T(8,128)S(1)}, f32[272,128]{1,0:T(8,128)S(1)}, u32[]{:S(2)}, u32[]{:S(2)}) collective-permute-start(f32[272,128]{1,0:T(8,128)S(1)} %get-tuple-element.77.sum_ref.sq_ref), channel_id=1, source_target_pairs={{0,8},{2,10},{4,12},{6,14},{8,0},{10,2},{12,4},{14,6},{16,24},{18,... | collective-permute-start | bytes 417800 | tf_op jit(solution)/shard_map/ppermute | solution.py:111
  273.3 1.0 fusion.11
  275.2 1.7 copy.47
  278.6 1.0 copy.46
  280.7 1.5 copy-done.8
  282.2 11.1 %shard_map.250 = (bf16[272,768]{1,0:T(8,128)(2,1)S(1)}, bf16[272,768]{1,0:T(8,128)(2,1)S(1)}, bf16[6,272,128]{2,1,0:T(8,128)(2,1)S(1)}, bf16[272,1536]{1,0:T(8,128)(2,1)}) custom-call(s32[118]{0:T(128)S(1)} %get-tuple-element.152._, f32[2,272,768]{2,1,0:T(8,128)S(1)} %copy-done.8, bf16[272,768]{1,0:T(8,128)(2,1)S(1)} %get-tuple-element.76.value_ref.v_ref, ...), custom_call_target="tpu_custom_call" | custom-call | tf_op jit(solution)/shard_map/pallas_call | solution.py:920
  294.9 5.5 shard_map.251
  300.4 1.2 copy-done.10
  301.6 2.6 copy.45
  304.2 2.7 pad_bitcast_fusion.5.refs_0_
  306.8 7.9 collective-permute-done.1.other_ref
  314.8 4.3 shard_map.252
  319.0 1.2 copy-done.5
  320.2 1.2 copy-done.47
  325.4 10.2 %shard_map.253 = (bf16[272,768]{1,0:T(8,128)(2,1)S(1)}, bf16[512,768]{1,0:T(8,128)(2,1)S(1)}, bf16[6,272,128]{2,1,0:T(8,128)(2,1)S(1)}, bf16[272,1536]{1,0:T(8,128)(2,1)S(1)}) custom-call(s32[118]{0:T(128)S(1)} %get-tuple-element.152._, f32[272,768]{1,0:T(8,128)S(1)} %get-tuple-element.82.pre_ref, f32[512,768]{1,0:T(8,128)S(1)} %copy-done.11, ...), custom_call_target="tpu_custom_call" | custom-call | tf_op jit(solution)/shard_map/pallas_call | solution.py:920
  336.6 1.4 fusion.8.cot_ref
  338.0 15.2 %collective-permute-done.3.other_ref = bf16[272,1536]{1,0:T(8,128)(2,1)S(1)} collective-permute-done((bf16[272,1536]{1,0:T(8,128)(2,1)S(1)}, bf16[272,1536]{1,0:T(8,128)(2,1)S(1)}, u32[]{:S(2)}, u32[]{:S(2)}) %collective-permute-start.3) | collective-permute-done | bytes 835616 | tf_op jit(solution)/shard_map/ppermute | solution.py:111
  353.3 28.6 %shard_map.254 = (f32[272,1536]{1,0:T(8,128)}, bf16[272,1536]{1,0:T(8,128)(2,1)S(1)}, bf16[272,1536]{1,0:T(8,128)(2,1)S(1)}, bf16[35,272,128]{2,1,0:T(8,128)(2,1...) custom-call(s32[118]{0:T(128)S(1)} %get-tuple-element.152._, ...), custom_call_target="tpu_custom_call" | custom-call | tf_op jit(solution)/shard_map/pallas_call | solution.py:920
  385.0 15.2 %collective-permute-done.4.other_ref = bf16[272,1536]{1,0:T(8,128)(2,1)S(1)} collective-permute-done((bf16[272,1536]{1,0:T(8,128)(2,1)S(1)}, bf16[272,1536]{1,0:T(8,128)(2,1)S(1)}, u32[]{:S(2)}, u32[]{:S(2)}) %collective-permute-start.4) | collective-permute-done | bytes 835616 | tf_op jit(solution)/shard_map/ppermute | solution.py:111
  400.3 12.9 %shard_map.255 = (f32[272,1536]{1,0:T(8,128)S(1)}, bf16[272,1536]{1,0:T(8,128)(2,1)S(1)}, f32[272,768]{1,0:T(8,128)S(1)}, f32[512,768]{1,0:T(8,128)S(1)}, bf16[6...) custom-call(s32[118]{0:T(128)S(1)} %get-tuple-element.152._, f32[272,1536]{1,0:T(8,128)S(1)} %copy-done.4, ...), custom_call_target="tpu_custom_call" | custom-call | tf_op jit(solution)/shard_map/pallas_call | solution.py:920
  415.0 1.2 copy-done.48
  416.2 1.2 copy-done.53
  419.3 2.6 copy.51
  421.9 2.4 gather_fusion
  424.3 2.4 copy.50
  426.7 1.4 copy-done.54
  428.1 1.1 copy-done.60
  431.0 7.9 shard_map.256
  441.2 1.4 pad_bitcast_fusion.3.refs_2_
  443.2 1.4 copy.54
  445.3 2.6 pad_bitcast_fusion.refs_6_
  447.9 1.4 pad_bitcast_fusion.1.refs_5_
  449.3 1.4 copy.52
  450.7 2.7 pad_bitcast_fusion.2.refs_4_
  453.5 1.3 reshape.179
  454.8 1.8 collective-permute-done.6.other_ref
  456.6 1.4 copy-done.49
  458.0 1.0 copy-done.51
  460.8 1.0 copy-done.82
  462.9 14.4 %shard_map.257 = (f32[272,1536]{1,0:T(8,128)S(1)}, bf16[272,1536]{1,0:T(8,128)(2,1)S(1)}, f32[2,272,768]{2,1,0:T(8,128)S(1)}, bf16[6,272,128]{2,1,0:T(8,128)(2,1)S(1)}, f32[272,128]{1,0:T(8,128)}) custom-call(s32[118]{0:T(128)S(1)} %get-tuple-element.152._, f32[272,1536]{1,0:T(8,128)S(1)} %copy-done.49, f32[272,1536]{1,0:T(8,128)S(1)} %copy-done.6, ...), custom_call_target="tpu_custom_call" | custom-call | tf_op jit(solution)/shard_map/pallas_call | solution.py:920
  477.3 1.2 copy-done.18
  480.2 1.2 copy-done.45
  481.5 1.6 copy.49
  483.2 1.4 pad_bitcast_fusion.4.refs_1_
  487.1 8.9 %shard_map.258 = (bf16[6,272,128]{2,1,0:T(8,128)(2,1)S(1)}, bf16[6,272,128]{2,1,0:T(8,128)(2,1)S(1)}, f32[8,768]{1,0:T(8,128)S(1)}, bf16[272,1536]{1,0:T(8,128)(2,1)S(1)}) custom-call(s32[118]{0:T(128)S(1)} %get-tuple-element.152._, f32[2,272,768]{2,1,0:T(8,128)S(1)} %copy-done.9, f32[2,272,768]{2,1,0:T(8,128)S(1)} %copy-done.46, ...), custom_call_target="tpu_custom_call" | custom-call | tf_op jit(solution)/shard_map/pallas_call | solution.py:920
  499.4 1.1 copy-done.28
  500.5 1.1 copy-done.31
  501.7 1.1 copy-done.34
  502.8 1.1 copy-done.36
  504.0 7.7 shard_map.259
  512.4 309.2 %shard_map.260 = (bf16[2,9,1536,128]{3,2,1,0:T(8,128)(2,1)}, f32[328,128]{1,0:T(8,128)}, bf16[272,1536]{1,0:T(8,128)(2,1)}, f32[272,1536]{1,0:T(8,128)}, bf16[27...) custom-call(s32[144]{0:T(256)} %gather_fusion, ...), custom_call_target="tpu_custom_call" | custom-call | tf_op jit(solution)/shard_map/pallas_call | solution.py:717
  823.5 2.5 slice_select_fusion
  827.6 3.0 copy-done.3
  830.6 3.0 copy-done.16
  833.6 3.0 copy-done.17
  836.7 13.1 %shard_map.261 = (f32[1,9,1536,128]{3,2,1,0:T(8,128)}, f32[1,9,1536,128]{3,2,1,0:T(8,128)}, f32[1,9,1536,128]{3,2,1,0:T(8,128)}) custom-call(f32[9]{0:T(128)S(1)} %copy-done.90, s32[9]{0:T(128)S(1)} %compare_convert_fusion.fill_ref, bf16[2,9,1536,128]{3,2,1,0:T(8,128)(2,1)S(1)} %copy-done.17, f32[1,9,1536,128]{3,2,1,0:T(8,128)S(1)} %copy-done.3, ...), custom_call_target="tpu_custom_call" | custom-call | tf_op jit(solution)/shard_map/pallas_call | solution.py:824
  849.8 1.0 multiply_subtract_fusion.1
  (264 shorter events, 42.8 us)
Async XLA Ops:
  0.6 252.3 %copy-start = (f32[16,6,1536]{2,0,1:T(8,128)S(1)}, f32[16,6,1536]{2,0,1:T(8,128)}, u32[]{:S(2)}) copy-start(f32[16,6,1536]{2,0,1:T(8,128)} %param.23) | copy-start | bytes 1769476
  0.7 4.2 copy-start.94
  0.7 4.3 copy-start.102
  0.7 5.0 copy-start.95
  3.8 6.0 copy-start.89
  5.9 3.9 copy-start.52
  252.1 73.3 %copy-start.21 = (f32[10,768]{1,0:T(8,128)}, f32[10,768]{1,0:T(8,128)S(1)}, u32[]{:S(2)}) copy-start(f32[10,768]{1,0:T(8,128)S(1)} %reshape.175.vec_ref) | copy-start | bytes 92164
  253.0 61.8 %copy-start.2 = (f32[272,1536]{1,0:T(8,128)}, f32[272,1536]{1,0:T(8,128)S(1)}, u32[]{:S(2)}) copy-start(f32[272,1536]{1,0:T(8,128)S(1)} %fusion.6.rows_ref.x_ref.refs_17_) | copy-start | bytes 5013508
  261.4 31.9 %copy-start.50 = (bf16[272,768]{1,0:T(8,128)(2,1)}, bf16[272,768]{1,0:T(8,128)(2,1)S(1)}, u32[]{:S(2)}) copy-start(bf16[272,768]{1,0:T(8,128)(2,1)S(1)} %get-tuple-element.76.value_ref.v_ref) | copy-start | bytes 1253380
  261.4 31.9 %copy-start.64 = (bf16[272,1536]{1,0:T(8,128)(2,1)}, bf16[272,1536]{1,0:T(8,128)(2,1)S(1)}, u32[]{:S(2)}) copy-start(bf16[272,1536]{1,0:T(8,128)(2,1)S(1)} %get-tuple-element.73) | copy-start | bytes 2506756
  261.4 31.9 %copy-start.68 = (f32[272,128]{1,0:T(8,128)}, f32[272,128]{1,0:T(8,128)S(1)}, u32[]{:S(2)}) copy-start(f32[272,128]{1,0:T(8,128)S(1)} %get-tuple-element.77.sum_ref.sq_ref) | copy-start | bytes 417796
  261.4 19.2 %collective-permute-start = (f32[272,128]{1,0:T(8,128)S(1)}, f32[272,128]{1,0:T(8,128)S(1)}, u32[]{:S(2)}, u32[]{:S(2)}) collective-permute-start(f32[272,128]{1,0:T(8,128)S(1)} %get-tuple-element.77.sum_ref.sq_ref), channel_id=1, source_target_pairs={{0,8},{2,10},{4,12},{6,14},{8,0},{10,2},{12,4},{14,6},{16,24},{18,... | collective-permute-start | bytes 417800 | tf_op jit(solution)/shard_map/ppermute | solution.py:111
  280.6 12.8 %copy-start.55 = (f32[272,128]{1,0:T(8,128)}, f32[272,128]{1,0:T(8,128)S(1)}, u32[]{:S(2)}) copy-start(f32[272,128]{1,0:T(8,128)S(1)} %pad.55.sin_ref) | copy-start | bytes 417796
  280.6 12.7 %copy-start.57 = (f32[272,128]{1,0:T(8,128)}, f32[272,128]{1,0:T(8,128)S(1)}, u32[]{:S(2)}) copy-start(f32[272,128]{1,0:T(8,128)S(1)} %pad.54.cos_ref) | copy-start | bytes 417796
  280.6 12.7 %copy-start.70 = (f32[272,128]{1,0:T(8,128)}, f32[272,128]{1,0:T(8,128)S(1)}, u32[]{:S(2)}) copy-start(f32[272,128]{1,0:T(8,128)S(1)} %collective-permute-done.other_ref.sqo_ref) | copy-start | bytes 417796
  282.2 12.7 %copy-start.20 = (bf16[512,1536]{1,0:T(8,128)(2,1)S(1)}, bf16[512,1536]{1,0:T(8,128)(2,1)}, u32[]{:S(2)}) copy-start(bf16[512,1536]{1,0:T(8,128)(2,1)} %copy-done.19) | copy-start | bytes 4718596
  294.9 5.5 copy-start.76
  294.9 19.9 %collective-permute-start.1 = (bf16[272,1536]{1,0:T(8,128)(2,1)}, bf16[272,1536]{1,0:T(8,128)(2,1)}, u32[]{:S(2)}, u32[]{:S(2)}) collective-permute-start(bf16[272,1536]{1,0:T(8,128)(2,1)} %get-tuple-element.78.part_ref), channel_id=1, source_target_pairs={{0,8},{2,10},{4,12},{6,14},{8,0},{10,2},{12,4},{14,6},{16,24},{18,... | collective-permute-start | bytes 2506760 | tf_op jit(solution)/shard_map/ppermute | solution.py:111
  301.6 23.8 %copy-start.37 = (bf16[512,768]{1,0:T(8,128)(2,1)}, bf16[512,768]{1,0:T(8,128)(2,1)S(1)}, u32[]{:S(2)}) copy-start(bf16[512,768]{1,0:T(8,128)(2,1)S(1)} %get-tuple-element.84.value_ref.v_ref) | copy-start | bytes 2359300
  304.2 10.6 %copy-start.42 = (f32[11,1536]{1,0:T(8,128)S(1)}, f32[11,1536]{1,0:T(8,128)}, u32[]{:S(2)}) copy-start(f32[11,1536]{1,0:T(8,128)} %shared_ref.7) | copy-start | bytes 202756
  314.8 9.0 %copy-start.103 = (s32[144]{0:T(256)S(1)}, s32[144]{0:T(256)}, u32[]{:S(2)}) copy-start(s32[144]{0:T(256)} %get-tuple-element.147) | copy-start | bytes 1732
  314.8 10.6 %copy-start.11 = (f32[512,768]{1,0:T(8,128)S(1)}, f32[512,768]{1,0:T(8,128)}, u32[]{:S(2)}) copy-start(f32[512,768]{1,0:T(8,128)} %copy-done.10) | copy-start | bytes 4718596
  321.4 14.2 %copy-start.13 = (f32[272,768]{1,0:T(8,128)}, f32[272,768]{1,0:T(8,128)S(1)}, u32[]{:S(2)}) copy-start(f32[272,768]{1,0:T(8,128)S(1)} %get-tuple-element.82.pre_ref) | copy-start | bytes 2506756
  321.4 14.2 %copy-start.61 = (bf16[272,1536]{1,0:T(8,128)(2,1)}, bf16[272,1536]{1,0:T(8,128)(2,1)S(1)}, u32[]{:S(2)}) copy-start(bf16[272,1536]{1,0:T(8,128)(2,1)S(1)} %get-tuple-element.100) | copy-start | bytes 2506756
  321.4 14.2 %copy-start.72 = (f32[272,128]{1,0:T(8,128)}, f32[272,128]{1,0:T(8,128)S(1)}, u32[]{:S(2)}) copy-start(f32[272,128]{1,0:T(8,128)S(1)} %get-tuple-element.85.sum_ref.sq_ref) | copy-start | bytes 417796
  321.4 3.9 collective-permute-start.2
  325.3 10.3 %copy-start.74 = (f32[272,128]{1,0:T(8,128)}, f32[272,128]{1,0:T(8,128)S(1)}, u32[]{:S(2)}) copy-start(f32[272,128]{1,0:T(8,128)S(1)} %collective-permute-done.2.other_ref.sqo_ref) | copy-start | bytes 417796
  325.4 11.2 %copy-start.66 = (bf16[2,144,1536]{2,1,0:T(8,128)(2,1)S(1)}, bf16[2,144,1536]{2,1,0:T(8,128)(2,1)}, u32[]{:S(2)}) copy-start(bf16[2,144,1536]{2,1,0:T(8,128)(2,1)} %copy-done.65) | copy-start | bytes 2654212
  335.7 17.5 %collective-permute-start.3 = (bf16[272,1536]{1,0:T(8,128)(2,1)S(1)}, bf16[272,1536]{1,0:T(8,128)(2,1)S(1)}, u32[]{:S(2)}, u32[]{:S(2)}) collective-permute-start(bf16[272,1536]{1,0:T(8,128)(2,1)S(1)} %get-tuple-element.86.part_ref), channel_id=1, source_target_pairs={{0,8},{2,10},{4,12},{6,14},{8,0},{10,2},{12,4},{14,6},{16,24},{18,... | collective-permute-start | bytes 2506760 | tf_op jit(solution)/shard_map/ppermute | solution.py:111
  353.2 31.1 %copy-start.101 = (f32[1,1536]{1,0:T(1,128)S(1)}, f32[1,1536]{1,0:T(1,128)}, u32[]{:S(2)}) copy-start(f32[1,1536]{1,0:T(1,128)} %slice.102) | copy-start | bytes 18436
  353.2 31.1 %copy-start.106 = (f32[8]{0:T(128)S(1)}, f32[8]{0:T(128)}, u32[]{:S(2)}) copy-start(f32[8]{0:T(128)} %pad.70.clone) | copy-start | bytes 100
  353.2 47.0 %copy-start.4 = (f32[272,1536]{1,0:T(8,128)S(1)}, f32[272,1536]{1,0:T(8,128)}, u32[]{:S(2)}) copy-start(f32[272,1536]{1,0:T(8,128)} %fusion.8.cot_ref) | copy-start | bytes 5013508
  353.2 47.0 %copy-start.12 = (f32[512,768]{1,0:T(8,128)S(1)}, f32[512,768]{1,0:T(8,128)}, u32[]{:S(2)}) copy-start(f32[512,768]{1,0:T(8,128)} %copy-done.10) | copy-start | bytes 4718596
  353.2 47.0 %copy-start.14 = (f32[272,768]{1,0:T(8,128)S(1)}, f32[272,768]{1,0:T(8,128)}, u32[]{:S(2)}) copy-start(f32[272,768]{1,0:T(8,128)} %copy-done.13) | copy-start | bytes 2506756
  353.2 47.0 %copy-start.22 = (f32[10,768]{1,0:T(8,128)S(1)}, f32[10,768]{1,0:T(8,128)}, u32[]{:S(2)}) copy-start(f32[10,768]{1,0:T(8,128)} %copy-done.21) | copy-start | bytes 92164
  353.2 47.0 %copy-start.38 = (bf16[512,768]{1,0:T(8,128)(2,1)S(1)}, bf16[512,768]{1,0:T(8,128)(2,1)}, u32[]{:S(2)}) copy-start(bf16[512,768]{1,0:T(8,128)(2,1)} %copy-done.37) | copy-start | bytes 2359300
  383.7 29.5 %copy-start.23 = (bf16[272,1536]{1,0:T(8,128)(2,1)}, bf16[272,1536]{1,0:T(8,128)(2,1)S(1)}, u32[]{:S(2)}) copy-start(bf16[272,1536]{1,0:T(8,128)(2,1)S(1)} %get-tuple-element.88.part_ref.da2) | copy-start | bytes 2506756
  383.7 29.5 %copy-start.62 = (bf16[272,1536]{1,0:T(8,128)(2,1)}, bf16[272,1536]{1,0:T(8,128)(2,1)S(1)}, u32[]{:S(2)}) copy-start(bf16[272,1536]{1,0:T(8,128)(2,1)S(1)} %get-tuple-element.102) | copy-start | bytes 2506756
  383.7 16.6 %collective-permute-start.4 = (bf16[272,1536]{1,0:T(8,128)(2,1)S(1)}, bf16[272,1536]{1,0:T(8,128)(2,1)S(1)}, u32[]{:S(2)}, u32[]{:S(2)}) collective-permute-start(bf16[272,1536]{1,0:T(8,128)(2,1)S(1)} %get-tuple-element.88.part_ref.da2), channel_id=1, source_target_pairs={{0,8},{2,10},{4,12},{6,14},{8,0},{10,2},{12,4},{14,6},{16,24},{18,... | collective-permute-start | bytes 2506760 | tf_op jit(solution)/shard_map/ppermute | solution.py:111
  400.3 19.0 %copy-start.105 = (s32[144]{0:T(256)S(1)}, s32[144]{0:T(256)}, u32[]{:S(2)}) copy-start(s32[144]{0:T(256)} %copy-done.104) | copy-start | bytes 1732
  418.2 3.7 copy-start.91
  418.2 8.4 collective-permute-start.5
  421.9 4.7 copy-start.15
  421.9 4.7 copy-start.40
  431.0 10.2 %copy-start.92 = (bf16[272,1536]{0,1:T(8,128)(2,1)S(1)}, bf16[272,1536]{0,1:T(8,128)(2,1)}, u32[]{:S(2)}) copy-start(bf16[272,1536]{0,1:T(8,128)(2,1)} %copy.50) | copy-start | bytes 2506756
  440.6 16.0 %collective-permute-start.6 = (bf16[272,1536]{1,0:T(8,128)(2,1)}, bf16[272,1536]{1,0:T(8,128)(2,1)}, u32[]{:S(2)}, u32[]{:S(2)}) collective-permute-start(bf16[272,1536]{1,0:T(8,128)(2,1)} %get-tuple-element.96.part_ref.da3), channel_id=1, source_target_pairs={{0,8},{2,10},{4,12},{6,14},{8,0},{10,2},{12,4},{14,6},{16,24},{18,... | collective-permute-start | bytes 2506760 | tf_op jit(solution)/shard_map/ppermute | solution.py:111
  449.3 7.3 copy-start.9
  450.7 5.8 copy-start.6
  481.4 4.1 collective-permute-start.7
  483.2 3.0 copy-start.44
  483.2 3.0 copy-start.46
  483.2 3.0 copy-start.69
  487.1 12.3 %copy-start.24 = (bf16[272,1536]{1,0:T(8,128)(2,1)S(1)}, bf16[272,1536]{1,0:T(8,128)(2,1)}, u32[]{:S(2)}) copy-start(bf16[272,1536]{1,0:T(8,128)(2,1)} %copy-done.23) | copy-start | bytes 2506756
  487.1 12.3 %copy-start.26 = (bf16[272,1536]{1,0:T(8,128)(2,1)S(1)}, bf16[272,1536]{1,0:T(8,128)(2,1)}, u32[]{:S(2)}) copy-start(bf16[272,1536]{1,0:T(8,128)(2,1)} %copy-done.25) | copy-start | bytes 2506756
  821.6 4.4 copy-start.93
  823.4 3.4 copy-start.97
  823.5 3.4 copy-start.98
  827.6 3.0 copy-start.3
  830.6 3.0 copy-start.16
  833.6 3.0 copy-start.17
  836.7 13.2 %copy-start.96 = (f32[1,12160]{1,0:T(1,128)S(1)}, f32[1,12160]{1,0:T(1,128)}, u32[]{:S(2)}) copy-start(f32[1,12160]{1,0:T(1,128)} %param.27) | copy-start | bytes 145924
  836.7 13.2 %copy-start.99 = (f32[1,12160]{1,0:T(1,128)S(1)}, f32[1,12160]{1,0:T(1,128)}, u32[]{:S(2)}) copy-start(f32[1,12160]{1,0:T(1,128)} %param.28) | copy-start | bytes 145924
  836.7 13.2 %copy-start.100 = (f32[1,12160]{1,0:T(1,128)S(1)}, f32[1,12160]{1,0:T(1,128)}, u32[]{:S(2)}) copy-start(f32[1,12160]{1,0:T(1,128)} %param.29) | copy-start | bytes 145924
  836.7 14.2 %copy-start.1 = (f32[16,6,1536]{2,0,1:T(8,128)S(1)}, f32[16,6,1536]{2,0,1:T(8,128)}, u32[]{:S(2)}) copy-start(f32[16,6,1536]{2,0,1:T(8,128)} %param.23) | copy-start | bytes 1769476
  (51 other events, 60.9 us)

commit v5 on v4

--- a/solution.py
+++ b/solution.py
@@ -483,11 +483,19 @@
             sub(corners.at[k % 2], part), corner_b.at[k], cb_s.at[k], cb_r.at[k], (at_y, core)
         )
 
-    def x_copy(k):
-        return remote(side_x.at[k % 2], from_x.at[k], x_s.at[k], x_r.at[k], (at_x, core))
-
-    def y_copy(k):
-        return remote(side_y.at[k % 2], from_y.at[k], y_s.at[k], y_r.at[k], (at_y, core))
+    def x_copy(k, n):
+        rows = pl.ds(n * part, part)
+        return remote(
+            side_x.at[k % 2, :, rows, :], from_x.at[k, :, rows, :], x_s.at[4 * n + k],
+            x_r.at[4 * n + k], (at_x, core),
+        )
+
+    def y_copy(k, n):
+        rows = pl.ds((1 - n) * part, part)
+        return remote(
+            side_y.at[k % 2, :, rows, :], from_y.at[k, :, rows, :], y_s.at[4 * n + k],
+            y_r.at[4 * n + k], (at_y, core),
+        )
 
     def f_copy(k):
         src = middle.at[k % 2]
@@ -531,41 +539,48 @@
         a_copy(k).start()
         b_copy(k).start()
 
-    def sides(k):
+    def direct_sides(k):
         sib_copy(1, k).wait_recv()
+        in_x = staged(from_sib.at[4 + k], stage.at[0], 0)
         sib_copy(2, k).wait_recv()
-        in_x = staged(from_sib.at[4 + k], stage.at[0], 0)
         in_y = staged(from_sib.at[8 + k], stage.at[1], 1)
 
         @pl.when(k < 2)
         def _():
-            x_copy(k + 2).wait_send()
-            y_copy(k + 2).wait_send()
+            for n in range(2):
+                x_copy(k + 2, n).wait_send()
+                y_copy(k + 2, n).wait_send()
 
         in_x.wait()
         sums(1, k, mine, (sub(stage.at[0], 0),), sub(side_x.at[k % 2], 0))
+        x_copy(k, 0).start()
+        in_y.wait()
+        sums(2, k, mine + part, (sub(stage.at[1], part),), sub(side_y.at[k % 2], part))
+        y_copy(k, 0).start()
+
+    def relayed_sides(k):
         b_copy(k).wait_recv()
         in_b = staged(corner_b.at[k], sub(stage.at[2], 0), 2)
-        in_y.wait()
-        sums(2, k, mine + part, (sub(stage.at[1], part),), sub(side_y.at[k % 2], part))
-        in_b.wait()
         a_copy(k).wait_recv()
         in_a = staged(corner_a.at[k], sub(stage.at[2], part), 3)
+        in_b.wait()
         sums(
             1, k, mine + part, (sub(stage.at[0], part), sub(stage.at[2], 0)),
             sub(side_x.at[k % 2], part),
         )
-        x_copy(k).start()
+        x_copy(k, 1).start()
         in_a.wait()
         sums(2, k, mine, (sub(stage.at[1], 0), sub(stage.at[2], part)), sub(side_y.at[k % 2], 0))
-        y_copy(k).start()
+        y_copy(k, 1).start()
 
     def centre(k):
         sib_copy(3, k).wait_recv()
         in_sib = staged(from_sib.at[12 + k], stage.at[0], 0)
-        x_copy(k).wait_recv()
+        x_copy(k, 0).wait_recv()
+        x_copy(k, 1).wait_recv()
         in_x = staged(from_x.at[k], stage.at[1], 1)
-        y_copy(k).wait_recv()
+        y_copy(k, 0).wait_recv()
+        y_copy(k, 1).wait_recv()
         in_y = staged(from_y.at[k], stage.at[2], 2)
 
         @pl.when(k < 2)
@@ -631,20 +646,24 @@
 
         @pl.when(step < 4)
         def _():
-            for_sibling(3 - step)
             corner(3 - step)
-
-        @pl.when(jnp.logical_and(step >= 1, step < 5))
-        def _():
-            sides(4 - step)
-
-        @pl.when(jnp.logical_and(step == 4, home))
+            direct_sides(3 - step)
+
+        @pl.when(step < 3)
+        def _():
+            for_sibling(2 - step)
+
+        @pl.when(step < 4)
+        def _():
+            relayed_sides(3 - step)
+
+        @pl.when(step >= 1)
+        def _():
+            centre(4 - step)
+
+        @pl.when(jnp.logical_and(step == 3, home))
         def _():
             finish_rows()
-
-        @pl.when(step >= 2)
-        def _():
-            centre(5 - step)
 
         for i in range(5):
 
@@ -655,14 +674,16 @@
 
         return carry
 
-    lax.fori_loop(0, 6, turn, 0)
+    for_sibling(3)
+    lax.fori_loop(0, 5, turn, 0)
     for q in (2, 3):
         sib_copy(q, 0).wait_send()
     for k in (1, 0):
         a_copy(k).wait_send()
         b_copy(k).wait_send()
-        x_copy(k).wait_send()
-        y_copy(k).wait_send()
+        for n in range(2):
+            x_copy(k, n).wait_send()
+            y_copy(k, n).wait_send()
     f_copy(1)[0].wait_send()
 
     @pl.when(home)
@@ -686,7 +707,7 @@
 
 def reduce_slots(holder, kinds, rows, columns, vector, ends, gains, slot_count):
     if not chip_pairs():
-        grads = slot_grads(holder, kinds, rows, columns)
+        grads = slot_grads(holder, kinds, [r.T for r in rows], columns)
         total = lax.psum_scatter(grads, "dp", scatter_dimension=0, tiled=True)
         x, after, dx, y_part, da_part = ends
         y_all, da_all = (
@@ -695,13 +716,12 @@
         result = (after + gains[0] * (y_all + gains[2])).astype(BF16)
         back, _ = normed_back(x, da_all * (1.0 + gains[1]))
         return total[None], lax.psum(vector, ("dp", "tensor")), result, dx + back
-    depth = max(r.shape[0] for r in rows)
-    left = [jnp.pad(r, ((0, depth - r.shape[0]), (0, 0))).T for r in rows]
+    left = rows
+    width, depth = left[0].shape
     lanes = columns[0].shape[2]
     tiles = sum(c.shape[0] for c in columns)
     block = jnp.where(holder >= 0, holder, tiles)
     kind = kinds[jnp.maximum(holder, 0)]
-    width = rows[0].shape[1]
     half = width // 2
     dma = pltpu.SemaphoreType.DMA
     scalars = pl.BlockSpec(memory_space=pltpu.SMEM)
@@ -731,7 +751,8 @@
             slab(2), slab(2), slab(2), slab(2), slab(2), slab(3),
             pltpu.VMEM((5,) + vector.shape, vector.dtype),
         ]
-        + [dma((n,)) for n in (len(left) + len(columns), 4, 16, 16) + (4,) * 10 + (5, 5, 4, 4)],
+        + [dma((n,)) for n in (len(left) + len(columns), 4, 16, 16)
+        + (8,) * 4 + (4,) * 6 + (5, 5, 4, 4)],
         compiler_params=pltpu.CompilerParams(
             collective_id=1, has_side_effects=True, vmem_limit_bytes=58 * MIB
         ),
@@ -829,7 +850,14 @@
         out_specs=[deep] * 3,
         out_shape=[jax.ShapeDtypeStruct(master.shape, jnp.float32)] * 3,
         compiler_params=pltpu.CompilerParams(vmem_limit_bytes=32 * MIB),
-    )(slot_scale, filled.astype(jnp.int32), planes, master, moment_one, moment_two)
+    )(
+        slot_scale,
+        filled.astype(jnp.int32),
+        *[
+            pltpu.with_memory_space_constraint(v, pltpu.HBM)
+            for v in (planes, master, moment_one, moment_two)
+        ],
+    )
 
 
 SCALING = HEAD ** (-0.5)
@@ -903,7 +931,7 @@
 
 
 def whole(array):
-    zeros = (0,) * array.ndim
+    zeros = (0,) * len(array.shape)
     return pl.BlockSpec(array.shape, lambda *_: zeros)
 
 
@@ -911,9 +939,9 @@
     return pl.BlockSpec((1, D, HEAD), lambda i, where: (where[first + stride * i], 0, 0))
 
 
-def call(body, places, grid, ins, outs, scratch=(), vmem=40):
+def call(body, places, grid, ins, outs, scratch=(), vmem=24):
     specs = [spec if spec is not None else whole(array) for array, spec in ins]
-    shapes = [jax.ShapeDtypeStruct(shape, kind) for shape, kind, _ in outs]
+    shapes = [pltpu.HBM(shape, kind) for shape, kind, _ in outs]
     out_specs = [
         spec if spec is not None else whole(shape) for (_, _, spec), shape in zip(outs, shapes)
     ]
@@ -928,7 +956,7 @@
         ),
         out_shape=shapes,
         compiler_params=pltpu.CompilerParams(vmem_limit_bytes=vmem * MIB),
-    )(places, *[array for array, _ in ins])
+    )(places, *[pltpu.with_memory_space_constraint(array, pltpu.HBM) for array, _ in ins])
 
 
 def head_lanes(rows):
@@ -1139,14 +1167,70 @@
     )
 
 
-def feed_forward(places, everyone, after_one, part, other, mod, shared, cot, up_bias, heads, blocks):
+def hidden_group(blocks):
+    return max(g for g in (5, 4, 3, 2, 1) if blocks % g == 0)
+
+
+def block_lanes(where, everyone, held, sems, first, group, steps):
+    i = pl.program_id(0)
+
+    def fetch(step, act):
+        slot = step % 2
+        for j in range(group):
+            copy = pltpu.make_async_copy(
+                everyone.at[where[first + step * group + j]],
+                held.at[slot, :, pl.ds(j * HEAD, HEAD)],
+                sems.at[slot, j],
+            )
+            copy.start() if act else copy.wait()
+
+    @pl.when(i == 0)
+    def _():
+        fetch(0, True)
+
+    @pl.when(i + 1 < steps)
+    def _():
+        fetch(i + 1, True)
+
+    fetch(i, False)
+    return held[i % 2]
+
+
+def lanes_scratch(group):
+    return [pltpu.VMEM((2, D, group * HEAD), BF16), pltpu.SemaphoreType.DMA((2, group))]
+
+
+def hidden_back(places, everyone, mod, cot, heads, blocks):
+    count = cot.shape[0]
+    group = hidden_group(blocks)
+    steps = blocks // group
+
+    def body(where, weights, mod_ref, cot_ref, grad, out, held, sems):
+        @pl.when(pl.program_id(0) == 0)
+        def _():
+            grad[...] = (mod_ref[5:6] * cot_ref[...]).astype(BF16)
+
+        down = block_lanes(where, weights, held, sems, 8 * heads + blocks, group, steps)
+        out[...] = nn(grad[...], down).astype(BF16)
+
+    return call(
+        body, places, steps,
+        [(everyone, ANY), (mod, None), (cot, None)],
+        [
+            ((count, D), BF16, None),
+            ((count, blocks * HEAD), BF16, pl.BlockSpec((count, group * HEAD), lambda i, _: (0, i))),
+        ],
+        lanes_scratch(group),
+    )
+
+
+def hidden_both(places, everyone, after_one, part, other, mod, shared, d_act, up_bias, heads, blocks):
     count = after_one.shape[0]
-    group = max(g for g in (7, 5, 3, 1) if blocks % g == 0 and g <= 5)
+    group = hidden_group(blocks)
+    steps = blocks // group
     span = group * HEAD
 
-    def body(_, after_ref, part_ref, other_ref, mod_ref, shared_ref, cot_ref, bias_ref, *refs):
-        ups, downs = refs[:group], refs[group : 2 * group]
-        after, low, grad, hidden, d_hidden, d_bias, y_ref, da_ref, y_acc, da_acc = refs[2 * group :]
+    def body(where, weights, after_ref, part_ref, other_ref, mod_ref, shared_ref, d_ref, bias_ref, after, low, hidden, d_hidden, d_bias, da_ref, acc, held, sems):
         i = pl.program_id(0)
 
         @pl.when(i == 0)
@@ -1156,11 +1240,9 @@
             after[...] = x
             unit, _ = normed(x)
             low[...] = (unit * (1.0 + mod_ref[4:5]) + mod_ref[3:4]).astype(BF16)
-            grad[...] = (mod_ref[5:6] * cot_ref[...]).astype(BF16)
-            y_acc[...] = jnp.zeros_like(y_acc)
-            da_acc[...] = jnp.zeros_like(da_acc)
-
-        up, down = joined(ups), joined(downs)
+            acc[...] = jnp.zeros_like(acc)
+
+        up = block_lanes(where, weights, held, sems, 8 * heads, group, steps)
         pre = nn(low[...], up) + bias_ref[...]
         square = pre * pre
         bent = jnp.tanh(GELU_COEF * (pre + 0.044715 * pre * square))
@@ -1168,41 +1250,65 @@
         slope = 0.5 * (1.0 + bent) + 0.5 * pre * (1.0 - bent * bent) * (
             GELU_COEF * (1.0 + 3.0 * 0.044715 * square)
         )
-        dh = (nn(grad[...], down) * slope).astype(BF16)
+        dh = (d_ref[...].astype(F32) * slope).astype(BF16)
         d_bias[...] = total_of(dh.astype(F32))
         for j in range(group):
             hidden[j] = act[:, j * HEAD : (j + 1) * HEAD]
             d_hidden[j] = dh[:, j * HEAD : (j + 1) * HEAD]
-        y_acc[...] = y_acc[...] + nt(act, down)
-        da_acc[...] = da_acc[...] + nt(dh, up)
-
-        @pl.when(i == blocks // group - 1)
-        def _():
-            y_ref[...] = y_acc[...].astype(BF16)
-            da_ref[...] = da_acc[...].astype(BF16)
-
-    base = 8 * heads
+        acc[...] = acc[...] + nt(dh, up)
+
+        @pl.when(i == steps - 1)
+        def _():
+            da_ref[...] = acc[...].astype(BF16)
+
     tall = pl.BlockSpec((group, count, HEAD), lambda i, _: (i, 0, 0))
     flat = pl.BlockSpec((1, span), lambda i, _: (0, i))
     return call(
-        body, places, blocks // group,
-        [(v, None) for v in (after_one, part, other, mod, shared, cot)]
-        + [(up_bias, flat)]
-        + [(everyone, block_at(base + j, group)) for j in range(group)]
-        + [(everyone, block_at(base + blocks + j, group)) for j in range(group)],
+        body, places, steps,
+        [(everyone, ANY)]
+        + [(v, None) for v in (after_one, part, other, mod, shared)]
+        + [(d_act, pl.BlockSpec((count, span), lambda i, _: (0, i))), (up_bias, flat)],
         [
             ((count, D), F32, None),
-            ((count, D), BF16, None),
             ((count, D), BF16, None),
             ((blocks, count, HEAD), BF16, tall),
             ((blocks, count, HEAD), BF16, tall),
             (up_bias.shape, F32, flat),
             ((count, D), BF16, None),
-            ((count, D), BF16, None),
-        ],
-        [pltpu.VMEM((count, D), F32), pltpu.VMEM((count, D), F32)],
-        vmem=48,
-    )
+        ],
+        [pltpu.VMEM((count, D), F32)] + lanes_scratch(group),
+        vmem=32,
+    )
+
+
+def hidden_out(places, everyone, hidden, heads):
+    blocks, count = hidden.shape[:2]
+    group = hidden_group(blocks)
+    steps = blocks // group
+
+    def body(where, weights, hidden_ref, y_ref, acc, held, sems):
+        i = pl.program_id(0)
+        down = block_lanes(where, weights, held, sems, 8 * heads + blocks, group, steps)
+        part = nt(jnp.concatenate([hidden_ref[j] for j in range(group)], 1), down)
+
+        @pl.when(i == 0)
+        def _():
+            acc[...] = part
+
+        @pl.when(i > 0)
+        def _():
+            acc[...] = acc[...] + part
+
+        @pl.when(i == steps - 1)
+        def _():
+            y_ref[...] = acc[...].astype(BF16)
+
+    return call(
+        body, places, steps,
+        [(everyone, ANY), (hidden, pl.BlockSpec((group, count, HEAD), lambda i, _: (i, 0, 0)))],
+        [((count, D), BF16, None)],
+        [pltpu.VMEM((count, D), F32)] + lanes_scratch(group),
+    )[0]
 
 
 def cross_back(places, everyone, cot, after_two, part, other, mod, query, key, value, pre, key_pre, vecs, heads):
@@ -1317,10 +1423,10 @@
     )
 
 
-def self_back(places, everyone, dx_two, after_one, part, other, mod, shared, query, key, value, pre, vecs, cos_tab, sin_tab, heads, tokens):
+def self_back(places, everyone, dx_two, after_one, part, other, mod, shared, branch, query, key, value, pre, vecs, cos_tab, sin_tab, heads, tokens):
     count = query.shape[0]
 
-    def body(_, dx_in, after_ref, part_ref, other_ref, mod_ref, shared_ref, q_ref, k_ref, v_ref, pre_ref, vec_ref, cos_ref, sin_ref, weight, dx_ref, low_ref, d_ref, dv_ref, sums, q_acc, k_acc):
+    def body(_, dx_in, after_ref, part_ref, other_ref, mod_ref, shared_ref, branch_ref, q_ref, k_ref, v_ref, pre_ref, vec_ref, cos_ref, sin_ref, weight, dx_ref, low_ref, d_ref, dv_ref, sums, vec_out, q_acc, k_acc):
         h = pl.program_id(0)
 
         @pl.when(h == 0)
@@ -1329,7 +1435,10 @@
             back, _ = normed_back(after_ref[...], da * shared_ref[3:4])
             dx = dx_in[...] + back
             dx_ref[...] = dx
-            low_ref[...] = (mod_ref[2:3] * dx).astype(BF16)
+            low = (mod_ref[2:3] * dx).astype(BF16)
+            low_ref[...] = low
+            vec_out[0:1] = 0.5 * total_of(low.astype(F32))
+            vec_out[1:2] = 0.5 * total_of(dx * branch_ref[...])
             q_acc[...] = jnp.zeros_like(q_acc)
             k_acc[...] = jnp.zeros_like(k_acc)
 
@@ -1356,7 +1465,7 @@
     pair = pl.BlockSpec((2, count, HEAD), lambda h, _: (0, 0, h))
     return call(
         body, places, heads,
-        [(v, None) for v in (dx_two, after_one, part, other, mod, shared)]
+        [(v, None) for v in (dx_two, after_one, part, other, mod, shared, branch)]
         + [
             (query, lanes), (key, lanes), (value, lanes), (pre, pair),
             (vecs, head_lanes(vecs.shape[0])), (cos_tab, None), (sin_tab, None),
@@ -1368,15 +1477,16 @@
             (pre.shape, F32, pair),
             ((heads, count, HEAD), BF16, pl.BlockSpec((1, count, HEAD), lambda h, _: (h, 0, 0))),
             ((count, HEAD), F32, None),
+            ((2, D), F32, None),
         ],
         [pltpu.VMEM((count, HEAD), F32), pltpu.VMEM((count, HEAD), F32)],
     )
 
 
-def self_back_rows(places, everyone, pre, grads, dv, squares, squares_other, sums, sums_other, vecs, heads):
+def self_back_rows(places, everyone, rows, pre, grads, dv, squares, squares_other, sums, sums_other, vecs, heads):
     count = pre.shape[1]
 
-    def body(_, pre_ref, d_ref, dv_ref, sq_ref, sqo_ref, sum_ref, sumo_ref, vec_ref, wq, wk, wv, gq_ref, gk_ref, vec_out, da_ref, acc):
+    def body(_, rows_ref, pre_ref, d_ref, dv_ref, sq_ref, sqo_ref, sum_ref, sumo_ref, vec_ref, wq, wk, wv, gq_ref, gk_ref, vec_out, da_ref, row_out, acc):
         h = pl.program_id(0)
         squares_all = sq_ref[...] + sqo_ref[...]
         total = sum_ref[...] + sumo_ref[...]
@@ -1411,14 +1521,17 @@
 
         @pl.when(h == heads - 1)
         def _():
-            da_ref[...] = acc[...].astype(BF16)
+            da = acc[...]
+            da_ref[...] = da.astype(BF16)
+            row_out[0:1] = total_of(da)
+            row_out[1:2] = total_of(da * normed(rows_ref[...])[0])
 
     tall = pl.BlockSpec((1, count, HEAD), lambda h, _: (h, 0, 0))
     pair = pl.BlockSpec((2, count, HEAD), lambda h, _: (0, 0, h))
     return call(
         body, places, heads,
         [
-            (pre, pair), (grads, pair), (dv, tall), (squares, None), (squares_other, None),
+            (rows, None), (pre, pair), (grads, pair), (dv, tall), (squares, None), (squares_other, None),
             (sums, None), (sums_other, None), (vecs, head_lanes(vecs.shape[0])),
             (everyone, block_at(0)), (everyone, block_at(heads)), (everyone, block_at(2 * heads)),
         ],
@@ -1427,26 +1540,20 @@
             ((heads, count, HEAD), BF16, tall),
             ((8, heads * HEAD), F32, head_lanes(8)),
             ((count, D), BF16, None),
+            ((2, D), F32, None),
         ],
         [pltpu.VMEM((count, D), F32)],
     )
 
 
-def shared_sums(places, rows, after_one, after_two, low_grads, dx_one, branch, cot, das, y_three, shared):
-    def body(_, x_ref, x1_ref, x2_ref, dy1, dy2, dy3, dx1_ref, y1_ref, cot_ref, da1, da3, da2, y3, shared_ref, out):
-        def half(value):
-            return 0.5 * total_of(value)
-
-        out[0:1] = half(dy1[...].astype(F32))
-        out[1:2] = half(dy2[...].astype(F32))
-        out[2:3] = half(dy3[...].astype(F32))
+def shared_sums(places, after_one, after_two, grad_two, grad_three, cot, da_two, da_three, y_three, shared):
+    def body(_, x1_ref, x2_ref, dy2, dy3, cot_ref, da2, da3, y3, shared_ref, out):
+        out[...] = jnp.zeros_like(out)
+        out[1:2] = 0.5 * total_of(dy2[...].astype(F32))
+        out[2:3] = 0.5 * total_of(dy3[...].astype(F32))
         part = da3[...].astype(F32)
         out[3:4] = total_of(part * normed(x1_ref[...])[0])
         out[4:5] = total_of(part)
-        part = da1[...].astype(F32)
-        out[5:6] = total_of(part)
-        out[6:7] = total_of(part * normed(x_ref[...])[0])
-        out[7:8] = half(dx1_ref[...] * y1_ref[...])
         part = da2[...].astype(F32)
         out[8:9] = total_of(part)
         out[9:10] = total_of(part * normed(x2_ref[...])[0])
@@ -1454,9 +1561,8 @@
 
     return call(
         body, places, 1,
-        [(v, None) for v in (rows, after_one, after_two, *low_grads, dx_one, branch, cot, *das, y_three, shared)],
+        [(v, None) for v in (after_one, after_two, grad_two, grad_three, cot, da_two, da_three, y_three, shared)],
         [(shared.shape, F32, None)],
-        vmem=48,
     )[0]
 
 
@@ -1526,18 +1632,30 @@
         rows = jnp.concatenate([halves[0, :half], halves[1, :half]], 0)
         return jnp.pad(rows, ((0, count - tokens), (0, 0))).astype(jnp.float32)
 
+    def upright(rows):
+        return jnp.pad(rows, ((0, context.shape[0] - rows.shape[0]), (0, 0))).T
+
+    def beside(*values):
+        return lax.optimization_barrier(values)
+
     rows, cot = all_rows(lats), all_rows(cots)
     low_one, pre_one, value_one, squares_one = project_self(
         places, everyone, rows, mod, vecs, heads_here
     )
     squares_one_other = pair_swap(squares_one)
-    key_pre, value_two, text_squares = project_text(places, everyone, context, vecs, heads_here)
     query_one, key_one, heads_one, part_one = attend_self(
         places, everyone, pre_one, value_one, squares_one, squares_one_other, vecs, cos_tab,
         sin_tab, heads_here, tokens,
     )
+    part_one, context = beside(part_one, context)
+    part_one_other = pair_swap(part_one)
+    key_pre, value_two, text_squares = project_text(places, everyone, context, vecs, heads_here)
+    left_context, left_one = upright(context), upright(low_one)
+    part_one_other, key_pre, left_context, left_one = beside(
+        part_one_other, key_pre, left_context, left_one
+    )
     branch_one, after_one, low_two, pre_two, squares_two = project_cross(
-        places, everyone, rows, part_one, pair_swap(part_one), mod, shared_params, vecs,
+        places, everyone, rows, part_one, part_one_other, mod, shared_params, vecs,
         text_squares, heads_here,
     )
     squares_two_other = pair_swap(squares_two)
@@ -1545,29 +1663,47 @@
         places, everyone, pre_two, key_pre, value_two, squares_two, squares_two_other, vecs,
         heads_here,
     )
-    after_two, low_three, grad_three, hidden, d_hidden, d_up_bias, y_three, da_two = feed_forward(
-        places, everyone, after_one, part_two, pair_swap(part_two), mod, shared_params, cot,
-        up_bias, heads_here, blocks_here,
-    )
+    part_two, cot, low_two = beside(part_two, cot, low_two)
+    part_two_other = pair_swap(part_two)
+    grad_three, d_act = hidden_back(places, everyone, mod, cot, heads_here, blocks_here)
+    left_two, left_grad_three = upright(low_two), upright(grad_three)
+    part_two_other, d_act, left_two, left_grad_three = beside(
+        part_two_other, d_act, left_two, left_grad_three
+    )
+    after_two, low_three, hidden, d_hidden, d_up_bias, da_two = hidden_both(
+        places, everyone, after_one, part_two, part_two_other, mod, shared_params, d_act, up_bias,
+        heads_here, blocks_here,
+    )
+    da_two_other = pair_swap(da_two)
+    y_three = hidden_out(places, everyone, hidden, heads_here)
+    left_three = upright(low_three)
+    da_two_other, y_three, left_three = beside(da_two_other, y_three, left_three)
     dx_two, grad_two, dq_two, dk_two, dv_two, sums_two = cross_back(
-        places, everyone, cot, after_two, da_two, pair_swap(da_two), mod, query_two, key_two,
+        places, everyone, cot, after_two, da_two, da_two_other, mod, query_two, key_two,
         value_two, pre_two, key_pre, vecs, heads_here,
     )
     query_grad_two, key_grad_two, vecs_two, da_three = cross_back_rows(
         places, everyone, pre_two, key_pre, dq_two, dk_two, dv_two, squares_two,
         squares_two_other, sums_two, pair_swap(sums_two), vecs, heads_here,
     )
-    dx_one, grad_one, d_one, dv_one, sums_one = self_back(
-        places, everyone, dx_two, after_one, da_three, pair_swap(da_three), mod, shared_params,
-        query_one, key_one, value_one, pre_one, vecs, cos_tab, sin_tab, heads_here, tokens,
-    )
-    query_grad_one, key_grad_one, vecs_one, da_one = self_back_rows(
-        places, everyone, pre_one, d_one, dv_one, squares_one, squares_one_other, sums_one,
+    da_three_other = pair_swap(da_three)
+    shared_grad = shared_sums(
+        places, after_one, after_two, grad_two, grad_three, cot, da_two, da_three, y_three,
+        shared_params,
+    )
+    left_grad_two = upright(grad_two)
+    da_three_other, shared_grad, left_grad_two = beside(da_three_other, shared_grad, left_grad_two)
+    dx_one, grad_one, d_one, dv_one, sums_one, rows_a = self_back(
+        places, everyone, dx_two, after_one, da_three, da_three_other, mod, shared_params,
+        branch_one, query_one, key_one, value_one, pre_one, vecs, cos_tab, sin_tab, heads_here,
+        tokens,
+    )
+    query_grad_one, key_grad_one, vecs_one, da_one, rows_b = self_back_rows(
+        places, everyone, rows, pre_one, d_one, dv_one, squares_one, squares_one_other, sums_one,
         pair_swap(sums_one), vecs, heads_here,
     )
-    shared_grad = shared_sums(
-        places, rows, after_one, after_two, (grad_one, grad_two, grad_three), dx_one,
-        branch_one, cot, (da_one, da_three, da_two), y_three, shared_params,
+    shared_grad = jnp.concatenate(
+        [rows_a[0:1], shared_grad[1:5], rows_b, rows_a[1:2], shared_grad[8:]], 0
     )
     head_grad = jnp.concatenate(
         [vecs_one[:5].reshape(-1), vecs_two[:5].reshape(-1), d_up_bias.reshape(-1)]
@@ -1579,7 +1715,7 @@
     parts, vector, output, grad_input = reduce_slots(
         holder,
         kind_of_blocks(tile_count, heads_here, blocks_here),
-        (low_one, grad_one, low_two, context, grad_two, low_three, grad_three),
+        (left_one, upright(grad_one), left_two, left_context, left_grad_two, left_three, left_grad_three),
         (
             query_grad_one,
             key_grad_one,

time: 856 us -> 823 us (0.961)
  local copies, waits for them, and re-layouts: 91.7 us -> 38.2 us
  Pallas kernels: 680 us -> 726 us
  waiting for transfers between devices: 42 us -> 13.6 us
    unnamed x216 -> x76, local copies, waits for them, and re-layouts: 51.9 us -> 8.07 us
    pallas_call x11 -> x13, Pallas kernels: 118 us -> 153 us  [call(): pl.pallas_call(body, grid_spec=pltpu.PrefetchScalarGridSpec(num_scalar_pr...]
    ppermute x8, waiting for transfers between devices: 42 us -> 13.6 us  [pair_swap(): return lax.ppermute(value, 'dp', [(i, i ^ 4) for i in range(16)])]
  transfers between devices with their start and end apart: 8 -> 8, of which waited for: 6 -> 6; matrix products, arithmetic and copies ran while one was open for 5% -> 3% of each run, Pallas kernels for 1% -> 5%
where the time goes in v5:
time: 823 us; the launch traced here: 817 us
  Pallas kernels  726 us (88%)
  local copies, waits for them, and re-layouts  38.2 us (5%)
  starting transfers between devices  18.8 us (2%)
  other arithmetic  18.3 us (2%)
  waiting for transfers between devices  13.6 us (2%)
    pallas_call x1, Pallas kernels, reduce_slots(): pl.pallas_call(reduce_kernel, out_shape=[room(2, width), jax.ShapeDtypeSt...  312 us
    pallas_call x1, Pallas kernels, gather_slots(): pl.pallas_call(gather_kernel, out_shape=[jax.ShapeDtypeStruct((16,) + sca...  240 us
    pallas_call x13, Pallas kernels, call(): pl.pallas_call(body, grid_spec=pltpu.PrefetchScalarGridSpec(num_scalar_pr...  153 us
    pallas_call x1, Pallas kernels, adam_slots(): pl.pallas_call(step, grid=(slot_count,), in_specs=[scalars, scalars, pl.B...  20.4 us
    ppermute x8, starting transfers between devices, pair_swap(): return lax.ppermute(value, 'dp', [(i, i ^ 4) for i in range(16)])  18.8 us
  transfers between devices with their start and end apart: 8, of which 6 were waited for; matrix products, arithmetic and copies ran while one was open for 3% of the time, Pallas kernels for 5%

profile of v5, /device:TPU:9, one launch (start us, length us, event | category | flops | bytes accessed | tf_op | source)
XLA Modules:
  0.0 817.3 jit_solution(4131676538603252376)
XLA Ops:
  0.7 0.9 convert_reduce_fusion
  3.8 1.0 pad.48.lat
  5.9 3.8 fusion.own
  9.8 240.1 %shard_map.248 = (bf16[16,9,1536,128]{3,2,1,0:T(8,128)(2,1)}, bf16[2,144,1536]{2,1,0:T(8,128)(2,1)S(1)}, bf16[2,144,1536]{2,1,0:T(8,128)(2,1)S(1)}, bf16[512,1536]{1,0:T(8,128)(2,1)S(1)}, f32[104,128]{1,0:T(8,128)S(1)}) custom-call(bf16[9,1536,128]{2,1,0:T(8,128)(2,1)S(1)} %fusion.own, bf16[144,1536]{1,0:T(8,128)(2,1)S(1)} %pad.48.lat, ...), custom_call_target="tpu_custom_call" | custom-call | tf_op jit(solution)/shard_map/pallas_call | solution.py:356
  250.0 1.1 copy-done.2
  253.0 1.4 fusion.6.rows_ref.refs_17_
  254.4 1.0 fusion.15
  256.0 8.5 %shard_map.249 = (bf16[272,1536]{1,0:T(8,128)(2,1)}, f32[2,272,768]{2,1,0:T(8,128)}, bf16[272,768]{1,0:T(8,128)(2,1)}, f32[272,128]{1,0:T(8,128)}) custom-call(s32[118]{0:T(128)S(1)} %get-tuple-element.196._.where, f32[272,1536]{1,0:T(8,128)} %fusion.6.rows_ref.refs_17_, f32[6,1536]{1,0:T(8,128)} %bitcast_add_fusion.mod_ref, f32[10,768]{1,0:T(8,128)} %reshape.175.vec_ref, ...), custom_call_target="tpu_custom_call" | custom-call | tf_op jit(solution)/shard_map/pallas_call | solution.py:948
  264.6 11.6 %collective-permute-start = (f32[272,128]{1,0:T(8,128)}, f32[272,128]{1,0:T(8,128)S(1)}, u32[]{:S(2)}, u32[]{:S(2)}) collective-permute-start(f32[272,128]{1,0:T(8,128)} %get-tuple-element.96.sum_ref.sq_ref), channel_id=1, source_target_pairs={{0,8},{2,10},{4,12},{6,14},{8,0},{10,2},{12,4},{14,6},{16,24},{18,... | collective-permute-start | bytes 417800 | tf_op jit(solution)/shard_map/ppermute | solution.py:111
  278.8 1.4 collective-permute-done.other_ref.sqo_ref
  280.9 11.4 %shard_map.250 = (bf16[272,768]{1,0:T(8,128)(2,1)}, bf16[272,768]{1,0:T(8,128)(2,1)}, bf16[6,272,128]{2,1,0:T(8,128)(2,1)}, bf16[272,1536]{1,0:T(8,128)(2,1)}) custom-call(s32[118]{0:T(128)S(1)} %get-tuple-element.196._.where, f32[2,272,768]{2,1,0:T(8,128)} %get-tuple-element.94.pre_ref, bf16[272,768]{1,0:T(8,128)(2,1)} %get-tuple-element.95.value_ref.v_ref, ...), custom_call_target="tpu_custom_call" | custom-call | tf_op jit(solution)/shard_map/pallas_call | solution.py:948
  292.3 1.2 collective-permute-start.1
  293.5 1.6 copy.49
  295.1 1.3 pad_bitcast_fusion.5.refs_0_
  296.4 1.0 slice_bitcast_fusion.1
  297.4 7.9 shard_map.251
  305.3 1.6 copy.48
  306.9 4.9 collective-permute-done.1.other_ref
  311.8 0.9 copy-done.14
  312.7 6.1 shard_map.252
  318.8 0.8 collective-permute-start.2
  319.6 1.4 fusion.8.cot_ref
  321.0 1.9 collective-permute-done.2.other_ref.sqo_ref
  323.6 11.3 %shard_map.253 = (bf16[272,768]{1,0:T(8,128)(2,1)}, bf16[512,768]{1,0:T(8,128)(2,1)}, bf16[6,272,128]{2,1,0:T(8,128)(2,1)}, bf16[272,1536]{1,0:T(8,128)(2,1)}) custom-call(s32[118]{0:T(128)S(1)} %get-tuple-element.196._.where, f32[272,768]{1,0:T(8,128)} %get-tuple-element.106.pre_ref, f32[512,768]{1,0:T(8,128)} %get-tuple-element.107.key_ref, ...), custom_call_target="tpu_custom_call" | custom-call | tf_op jit(solution)/shard_map/pallas_call | solution.py:948
  334.9 0.9 collective-permute-start.3
  335.8 0.7 slice_bitcast_fusion.4
  337.2 12.5 %shard_map.254 = (bf16[272,1536]{1,0:T(8,128)(2,1)}, bf16[272,4480]{1,0:T(8,128)(2,1)}) custom-call(s32[118]{0:T(128)S(1)} %get-tuple-element.196._.where, bf16[144,1536,128]{2,1,0:T(8,128)(2,1)} %bitcast.75, f32[6,1536]{1,0:T(8,128)} %bitcast_add_fusion.mod_ref, f32[272,1536]{1,0:T(8,128)} %fusion.8.cot_ref), custom_call_target="tpu_custom_call" | custom-call | tf_op jit(solution)/shard_map/pallas_call | solution.py:948
  349.7 0.7 copy.50
  351.6 1.4 pad_bitcast_fusion.4.refs_2_
  353.0 1.4 pad_bitcast_fusion.3.refs_6_
  354.3 21.9 %shard_map.255 = (f32[272,1536]{1,0:T(8,128)}, bf16[272,1536]{1,0:T(8,128)(2,1)}, bf16[35,272,128]{2,1,0:T(8,128)(2,1)}, bf16[35,272,128]{2,1,0:T(8,128)(2,1)}, ...) custom-call(s32[118]{0:T(128)S(1)} %get-tuple-element.196._.where, bf16[144,1536,128]{2,1,0:T(8,128)(2,1)} %bitcast.76, ...), custom_call_target="tpu_custom_call" | custom-call | tf_op jit(solution)/shard_map/pallas_call | solution.py:948
  376.2 0.7 collective-permute-start.4
  376.9 0.9 fusion.26
  377.9 12.9 %shard_map.256.y3.refs_20_ = bf16[272,1536]{1,0:T(8,128)(2,1)} custom-call(s32[118]{0:T(128)S(1)} %get-tuple-element.196._.where, bf16[144,1536,128]{2,1,0:T(8,128)(2,1)} %bitcast.77, bf16[35,272,128]{2,1,0:T(8,128)(2,1)} %get-tuple-element.123.hidden_ref.refs_16_), custom_call_target="tpu_custom_call" | custom-call | tf_op jit(solution)/shard_map/pallas_call | solution.py:948
  390.8 0.7 copy.52
  391.5 1.4 pad_bitcast_fusion.2.refs_5_
  393.1 0.9 copy-done.15
  394.0 14.9 %shard_map.257 = (f32[272,1536]{1,0:T(8,128)}, bf16[272,1536]{1,0:T(8,128)(2,1)}, f32[272,768]{1,0:T(8,128)}, f32[512,768]{1,0:T(8,128)}, bf16[6,512,128]{2,1,0:T(8,128)(2,1)}, /*index=5*/f32[272,128]{1,0:T(8,128)}) custom-call(s32[118]{0:T(128)S(1)} %get-tuple-element.196._.where, f32[272,1536]{1,0:T(8,128)} %fusion.8.cot_ref, ...), custom_call_target="tpu_custom_call" | custom-call | tf_op jit(solution)/shard_map/pallas_call | solution.py:948
  408.9 1.1 collective-permute-start.5
  409.9 0.8 slice.114
  410.7 2.1 gather_fusion
  413.7 9.2 %shard_map.258 = (bf16[6,272,128]{2,1,0:T(8,128)(2,1)}, bf16[6,512,128]{2,1,0:T(8,128)(2,1)}, f32[8,768]{1,0:T(8,128)}, bf16[272,1536]{1,0:T(8,128)(2,1)}) custom-call(s32[118]{0:T(128)S(1)} %get-tuple-element.196._.where, f32[272,768]{1,0:T(8,128)} %get-tuple-element.106.pre_ref, f32[512,768]{1,0:T(8,128)} %get-tuple-element.107.key_ref, ...), custom_call_target="tpu_custom_call" | custom-call | tf_op jit(solution)/shard_map/pallas_call | solution.py:948
  422.9 1.1 collective-permute-start.6
  424.7 0.7 copy.53
  425.4 1.3 pad_bitcast_fusion.1.refs_4_
  426.8 7.1 shard_map.259
  433.9 3.9 collective-permute-done.6.other_ref
  437.8 0.8 slice.118
  438.6 17.4 %shard_map.260 = (f32[272,1536]{1,0:T(8,128)}, bf16[272,1536]{1,0:T(8,128)(2,1)}, f32[2,272,768]{2,1,0:T(8,128)}, bf16[6,272,128]{2,1,0:T(8,128)(2,1)}, f32[272,128]{1,0:T(8,128)}, /*index=5*/f32[2,1536]{1,0:T(2,128)}) custom-call(s32[118]{0:T(128)S(1)} %get-tuple-element.196._.where, f32[272,1536]{1,0:T(8,128)} %get-tuple-element.128.dx_in, ...), custom_call_target="tpu_custom_call" | custom-call | tf_op jit(solution)/shard_map/pallas_call | solution.py:948
  456.1 1.7 copy.54
  457.8 1.4 collective-permute-start.7
  459.2 1.3 pad_bitcast_fusion.refs_1_
  460.5 1.2 collective-permute-done.7.sumo_ref
  462.4 11.8 %shard_map.261 = (bf16[6,272,128]{2,1,0:T(8,128)(2,1)}, bf16[6,272,128]{2,1,0:T(8,128)(2,1)}, f32[8,768]{1,0:T(8,128)}, bf16[272,1536]{1,0:T(8,128)(2,1)}, f32[2,1536]{1,0:T(2,128)}) custom-call(s32[118]{0:T(128)S(1)} %get-tuple-element.196._.where, f32[272,1536]{1,0:T(8,128)} %fusion.6.rows_ref.refs_17_, f32[2,272,768]{2,1,0:T(8,128)} %get-tuple-element.94.pre_ref, ...), custom_call_target="tpu_custom_call" | custom-call | tf_op jit(solution)/shard_map/pallas_call | solution.py:948
  474.2 0.8 concatenate.30
  475.0 0.7 reshape.178
  476.7 312.0 %shard_map.262 = (bf16[2,9,1536,128]{3,2,1,0:T(8,128)(2,1)}, f32[328,128]{1,0:T(8,128)}, bf16[272,1536]{1,0:T(8,128)(2,1)}, f32[272,1536]{1,0:T(8,128)}, bf16[27...) custom-call(s32[144]{0:T(256)} %gather_fusion, ...), custom_call_target="tpu_custom_call" | custom-call | tf_op jit(solution)/shard_map/pallas_call | solution.py:737
  788.7 0.9 slice.125
  789.6 0.9 slice.126
  790.5 2.0 slice_select_fusion.1
  792.5 2.5 slice_select_fusion
  795.1 0.7 multiply_subtract_fusion
  795.9 20.4 %shard_map.263 = (f32[1,9,1536,128]{3,2,1,0:T(8,128)}, f32[1,9,1536,128]{3,2,1,0:T(8,128)}, f32[1,9,1536,128]{3,2,1,0:T(8,128)}) custom-call(f32[9]{0:T(128)S(1)} %copy-done.7, s32[9]{0:T(128)S(1)} %compare_convert_fusion.fill_ref, bf16[2,9,1536,128]{3,2,1,0:T(8,128)(2,1)} %get-tuple-element.166.grads, f32[1,9,1536,128]{3,2,1,0:T(8,128)} %weight.1, ...), custom_call_target="tpu_custom_call" | custom-call | tf_op jit(solution)/shard_map/pallas_call | solution.py:845
  816.3 1.0 multiply_subtract_fusion.1
  (131 shorter events, 14.3 us)
Async XLA Ops:
  0.6 253.8 %copy-start = (f32[16,6,1536]{2,0,1:T(8,128)S(1)}, f32[16,6,1536]{2,0,1:T(8,128)}, u32[]{:S(2)}) copy-start(f32[16,6,1536]{2,0,1:T(8,128)} %param.23) | copy-start | bytes 1769476
  0.7 4.2 copy-start.20
  0.7 4.3 copy-start.33
  0.7 5.0 copy-start.21
  3.0 1.9 copy-start.35
  3.8 2.1 copy-start.6
  5.9 3.9 copy-start.4
  249.9 1.1 copy-start.2
  251.1 0.6 copy-start.5
  251.8 3.6 copy-start.10
  264.6 15.6 %collective-permute-start = (f32[272,128]{1,0:T(8,128)}, f32[272,128]{1,0:T(8,128)S(1)}, u32[]{:S(2)}, u32[]{:S(2)}) collective-permute-start(f32[272,128]{1,0:T(8,128)} %get-tuple-element.96.sum_ref.sq_ref), channel_id=1, source_target_pairs={{0,8},{2,10},{4,12},{6,14},{8,0},{10,2},{12,4},{14,6},{16,24},{18,... | collective-permute-start | bytes 417800 | tf_op jit(solution)/shard_map/ppermute | solution.py:111
  280.2 0.7 copy-start.18
  292.3 19.6 %collective-permute-start.1 = (bf16[272,1536]{1,0:T(8,128)(2,1)}, bf16[272,1536]{1,0:T(8,128)(2,1)S(1)}, u32[]{:S(2)}, u32[]{:S(2)}) collective-permute-start(bf16[272,1536]{1,0:T(8,128)(2,1)} %get-tuple-element.99.part_ref), channel_id=1, source_target_pairs={{0,8},{2,10},{4,12},{6,14},{8,0},{10,2},{12,4},{14,6},{16,24},{18,... | collective-permute-start | bytes 2506760 | tf_op jit(solution)/shard_map/ppermute | solution.py:111
  297.4 7.9 copy-start.3
  311.8 0.9 copy-start.14
  312.7 6.9 copy-start.12
  312.7 6.9 copy-start.13
  318.8 4.1 collective-permute-start.2
  322.9 0.7 copy-start.19
  334.9 19.4 %collective-permute-start.3 = (bf16[272,1536]{1,0:T(8,128)(2,1)}, bf16[272,1536]{1,0:T(8,128)(2,1)}, u32[]{:S(2)}, u32[]{:S(2)}) collective-permute-start(bf16[272,1536]{1,0:T(8,128)(2,1)} %get-tuple-element.115.part_ref), channel_id=1, source_target_pairs={{0,8},{2,10},{4,12},{6,14},{8,0},{10,2},{12,4},{14,6},{16,24},{18,... | collective-permute-start | bytes 2506760 | tf_op jit(solution)/shard_map/ppermute | solution.py:111
  337.2 12.6 %copy-start.16 = (bf16[272,1536]{1,0:T(8,128)(2,1)S(1)}, bf16[272,1536]{1,0:T(8,128)(2,1)}, u32[]{:S(2)}) copy-start(bf16[272,1536]{1,0:T(8,128)(2,1)} %get-tuple-element.117) | copy-start | bytes 2506756
  349.7 1.2 copy-start.8
  354.3 22.6 %copy-start.34 = (s32[144]{0:T(256)S(1)}, s32[144]{0:T(256)}, u32[]{:S(2)}) copy-start(s32[144]{0:T(256)} %get-tuple-element.191) | copy-start | bytes 1732
  376.2 16.9 %collective-permute-start.4 = (bf16[272,1536]{1,0:T(8,128)(2,1)}, bf16[272,1536]{1,0:T(8,128)(2,1)S(1)}, u32[]{:S(2)}, u32[]{:S(2)}) collective-permute-start(bf16[272,1536]{1,0:T(8,128)(2,1)} %get-tuple-element.122.part_ref.da2), channel_id=1, source_target_pairs={{0,8},{2,10},{4,12},{6,14},{8,0},{10,2},{12,4},{14,6},{16,24},{18,... | collective-permute-start | bytes 2506760 | tf_op jit(solution)/shard_map/ppermute | solution.py:111
  377.8 12.9 %copy-start.17 = (bf16[272,1536]{1,0:T(8,128)(2,1)S(1)}, bf16[272,1536]{1,0:T(8,128)(2,1)}, u32[]{:S(2)}) copy-start(bf16[272,1536]{1,0:T(8,128)(2,1)} %get-tuple-element.124) | copy-start | bytes 2506756
  393.1 0.9 copy-start.15
  394.0 18.9 %copy-start.36 = (s32[144]{0:T(256)S(1)}, s32[144]{0:T(256)}, u32[]{:S(2)}) copy-start(s32[144]{0:T(256)} %copy-done.35) | copy-start | bytes 1732
  408.9 4.2 collective-permute-start.5
  413.0 0.7 copy-start.23
  413.7 11.0 %copy-start.31 = (f32[1,4480]{1,0:T(1,128)S(1)}, f32[1,4480]{1,0:T(1,128)}, u32[]{:S(2)}) copy-start(f32[1,4480]{1,0:T(1,128)} %get-tuple-element.160) | copy-start | bytes 53764
  413.7 11.0 %copy-start.9 = (bf16[272,1536]{1,0:T(8,128)(2,1)S(1)}, bf16[272,1536]{1,0:T(8,128)(2,1)}, u32[]{:S(2)}) copy-start(bf16[272,1536]{1,0:T(8,128)(2,1)} %get-tuple-element.134.dy2) | copy-start | bytes 2506756
  422.9 14.9 %collective-permute-start.6 = (bf16[272,1536]{1,0:T(8,128)(2,1)}, bf16[272,1536]{1,0:T(8,128)(2,1)}, u32[]{:S(2)}, u32[]{:S(2)}) collective-permute-start(bf16[272,1536]{1,0:T(8,128)(2,1)} %get-tuple-element.133.da3.part_ref), channel_id=1, source_target_pairs={{0,8},{2,10},{4,12},{6,14},{8,0},{10,2},{12,4},{14,6},{16,24},{18,... | collective-permute-start | bytes 2506760 | tf_op jit(solution)/shard_map/ppermute | solution.py:111
  426.8 7.1 copy-start.30
  456.0 1.7 copy-start.24
  456.1 3.1 copy-start.32
  457.8 4.0 collective-permute-start.7
  461.7 0.6 copy-start.25
  462.4 11.8 %slice-start = ((f32[11,1536]{1,0:T(8,128)}), f32[3,1536]{1,0:T(4,128)S(1)}, s32[]{:S(2)}) async-start(f32[11,1536]{1,0:T(8,128)} %shard_map.259), calls=%async_computation | async-start | bytes 49152 | tf_op jit(solution)/shard_map/slice | solution.py:1706
  792.5 2.6 copy-start.11
  792.5 2.6 copy-start.26
  792.5 2.6 copy-start.27
  792.5 3.3 copy-start.7
  795.8 20.4 %copy-start.22 = (f32[1,12160]{1,0:T(1,128)S(1)}, f32[1,12160]{1,0:T(1,128)}, u32[]{:S(2)}) copy-start(f32[1,12160]{1,0:T(1,128)} %param.27) | copy-start | bytes 145924
  795.8 20.4 %copy-start.28 = (f32[1,12160]{1,0:T(1,128)S(1)}, f32[1,12160]{1,0:T(1,128)}, u32[]{:S(2)}) copy-start(f32[1,12160]{1,0:T(1,128)} %param.28) | copy-start | bytes 145924
  795.8 20.4 %copy-start.29 = (f32[1,12160]{1,0:T(1,128)S(1)}, f32[1,12160]{1,0:T(1,128)}, u32[]{:S(2)}) copy-start(f32[1,12160]{1,0:T(1,128)} %param.29) | copy-start | bytes 145924
  795.8 21.4 %copy-start.1 = (f32[16,6,1536]{2,0,1:T(8,128)S(1)}, f32[16,6,1536]{2,0,1:T(8,128)}, u32[]{:S(2)}) copy-start(f32[16,6,1536]{2,0,1:T(8,128)} %param.23) | copy-start | bytes 1769476
